TPU v7x, 256 devices: a whole 4x4x8 slice. The times are simulated.
256 devices in a mesh: ctx: 32 (over y, z_lo, x), tp: 8 (over z_hi, core).
Axes of the slice: x: 4, y: 4, z: 8 (z_hi: 4, z_lo: 2; z = z_hi * 2 + z_lo), core: 2. Of those that a mesh axis runs over, the one named last changes fastest.
Arguments:
- stream_first: bfloat16 [4096, 3072], P('ctx', 'tp'), may hold values from -6 to 6
- stream_second: bfloat16 [4096, 3072], P('ctx', 'tp'), may hold values from -6 to 6
- grad_first: bfloat16 [4096, 3072], P('ctx', 'tp'), may hold values from -6 to 6
- grad_second: bfloat16 [4096, 3072], P('ctx', 'tp'), may hold values from -6 to 6
- expert_ids: int32 [4096, 4], P('ctx'), may hold values from 0 to 31, all different within a row; in each aligned block of 128 rows (0 to 127, 128 to 255, ...) at most 32 rows name the same one
- gate_probs: float32 [4096, 4], P('ctx'), may hold values from 0.05 to 1
- w_in: bfloat16 [32, 3072, 2048], P('ctx', None, 'tp'), may hold values from -0.109375 to 0.109375
- w_out: bfloat16 [32, 2048, 3072], P('ctx', 'tp'), may hold values from -0.125 to 0.125
Outputs:
- stream_input: bfloat16 [4096, 3072], P('ctx', 'tp')
- grad_stream: bfloat16 [4096, 3072], P('ctx', 'tp')
- grad_w_in: float32 [32, 3072, 2048], P('ctx', None, 'tp')
- grad_w_out: float32 [32, 2048, 3072], P('ctx', 'tp')
- grad_gates: float32 [4096, 4], P('ctx')
Inputs may be any that keep to these rules, and one draw needn't show every extreme that they name: `expert_ids`: each row names 4 different experts. In each aligned block of 128 rows (the rows of one index of ctx) no expert is named more than 32 times, a bound that some block reaches.
All inputs are finite; a program needn't handle non-finite values.
Results may differ from a plain program's by a relative error of at most 0.017.
Values may be sent and summed in bfloat16 or wider, within the bound.
No kernel may reach another device: no remote copies, remote signals or barrier semaphores. Data moves between devices by JAX's collectives and lax.ppermute only.
A program may use at most 192 MiB of HBM per device.

v0:
```python
import jax
import jax.numpy as jnp
from jax import lax
from jax.sharding import PartitionSpec as P


def gelu_value(x):
    return x * 0.5 * (1.0 + lax.erf(x * 0.7071067811865476))


def gelu_slope(x):
    return (
        0.5 * (1.0 + lax.erf(x * 0.7071067811865476))
        + x * jnp.exp(-0.5 * x * x) * 0.3989422804014327
    )


def feature_sums(values):
    return lax.psum(values, "tp")


def pack_rows(source, index, filled, owners, local_experts, capacity):
    picked = jnp.where(filled[:, None], source[index], jnp.zeros((), source.dtype))
    return picked.reshape(owners, local_experts, capacity, source.shape[1])


def send_out(buffer):
    arrived = lax.all_to_all(buffer, "ctx", split_axis=0, concat_axis=0, tiled=True)
    return lax.all_gather(arrived, "tp", axis=3, tiled=True)


def bring_back(stacked):
    summed = lax.psum_scatter(
        stacked.astype(jnp.bfloat16), "tp", scatter_dimension=3, tiled=True
    ).astype(jnp.float32)
    return lax.all_to_all(
        summed.astype(jnp.bfloat16), "ctx", split_axis=0, concat_axis=0, tiled=True
    ).astype(summed.dtype)


def on_device(
    stream_first, stream_second, grad_first, grad_second, expert_ids, gate_probs, w_in, w_out
):
    tokens, width_local = stream_first.shape
    topk = expert_ids.shape[1]
    width = width_local * lax.axis_size("tp")
    owners = lax.axis_size("ctx")
    local_experts = w_in.shape[0]
    experts = local_experts * owners
    capacity = 2 * tokens * topk // experts
    routes = tokens * topk
    first = stream_first.astype(jnp.float32)
    mean = feature_sums(jnp.sum(first, axis=1)) / width
    centred = first - mean[:, None]
    var = feature_sums(jnp.sum(centred * centred, axis=1)) / width
    rstd = lax.rsqrt(var + 1e-05)
    normed = centred * rstd[:, None]
    normed_low = normed.astype(jnp.bfloat16)
    flat_ids = expert_ids.reshape(routes)
    onehot = (flat_ids[:, None] == jnp.arange(experts, dtype=jnp.int32)[None, :]).astype(jnp.int32)
    rank = jnp.sum(jnp.cumsum(onehot, axis=0) * onehot, axis=1) - 1
    slot_of = flat_ids * capacity + rank
    route_at = (
        jnp.full((experts * capacity,), routes, jnp.int32)
        .at[slot_of]
        .set(jnp.arange(routes, dtype=jnp.int32))
    )
    filled = route_at < routes
    route_index = jnp.minimum(route_at, routes - 1)
    token_index = route_index // topk
    grad_wide = grad_second.astype(jnp.float32)
    scaled = (
        (gate_probs[:, :, None] * grad_wide[:, None, :]).astype(jnp.bfloat16).reshape(routes, -1)
    )

    def unpack(back):
        return back.reshape(experts * capacity, back.shape[3])[slot_of].reshape(
            tokens, topk, back.shape[3]
        )

    arrived = send_out(pack_rows(normed_low, token_index, filled, owners, local_experts, capacity))
    local = 0
    rows = arrived[:, local].reshape(-1, width)
    preact = jnp.dot(rows, w_in[local], preferred_element_type=jnp.float32)
    hidden = gelu_value(preact).astype(jnp.bfloat16)
    result = jnp.dot(hidden, w_out[local], preferred_element_type=jnp.float32)
    parts = [result.reshape(owners, capacity, width)]
    saved = [(rows, preact, hidden)]
    routes_out = unpack(bring_back(jnp.stack(parts, axis=1)))
    branch = jnp.sum(gate_probs[:, :, None] * routes_out, axis=1)
    gate_term = jnp.sum(grad_wide[:, None, :] * routes_out, axis=2)
    stream_input = (stream_second.astype(jnp.float32) - branch).astype(jnp.bfloat16)
    arrived_grad = send_out(pack_rows(scaled, route_index, filled, owners, local_experts, capacity))
    local = 0
    rows, preact, hidden = saved[local]
    grad_rows = arrived_grad[:, local].reshape(-1, width)
    grad_hidden = lax.dot_general(
        grad_rows, w_out[local], (((1,), (1,)), ((), ())), preferred_element_type=jnp.float32
    )
    grad_pre = (grad_hidden * gelu_slope(preact)).astype(jnp.bfloat16)
    grads_out = [
        lax.dot_general(
            hidden, grad_rows, (((0,), (0,)), ((), ())), preferred_element_type=jnp.float32
        )
    ]
    grads_in = [
        lax.dot_general(
            rows, grad_pre, (((0,), (0,)), ((), ())), preferred_element_type=jnp.float32
        )
    ]
    route_dx = lax.dot_general(
        grad_pre, w_in[local], (((1,), (1,)), ((), ())), preferred_element_type=jnp.float32
    )
    dparts = [route_dx.reshape(owners, capacity, width)]
    routes_dx = unpack(bring_back(jnp.stack(dparts, axis=1)))
    grad_normed = jnp.sum(routes_dx, axis=1)
    sum_grad, sum_mixed, gate_grad = feature_sums(
        (jnp.sum(grad_normed, axis=1), jnp.sum(grad_normed * normed, axis=1), gate_term)
    )
    correction = grad_normed - (sum_grad / width)[:, None] - normed * (sum_mixed / width)[:, None]
    grad_stream = (grad_first.astype(jnp.float32) + rstd[:, None] * correction).astype(jnp.bfloat16)
    return (
        stream_input,
        grad_stream,
        jnp.stack(grads_in, axis=0),
        jnp.stack(grads_out, axis=0),
        gate_grad,
    )


def solution(mesh):
    in_specs = (
        P("ctx", "tp"),
        P("ctx", "tp"),
        P("ctx", "tp"),
        P("ctx", "tp"),
        P("ctx", None),
        P("ctx", None),
        P("ctx", None, "tp"),
        P("ctx", "tp", None),
    )
    out_specs = (
        P("ctx", "tp"),
        P("ctx", "tp"),
        P("ctx", None, "tp"),
        P("ctx", "tp", None),
        P("ctx", None),
    )
    return jax.shard_map(
        on_device, mesh=mesh, in_specs=in_specs, out_specs=out_specs, check_vma=False
    )
```

profile of v0, /device:TPU:65, one launch (start us, length us, event | category | flops | bytes accessed | tf_op | source)
XLA Modules:
  0.0 546.7 jit_solution(1525877978738683078)
XLA Ops:
  7.2 0.8 broadcast_multiply_fusion
  8.0 0.8 copy.22
  8.8 0.1 eq.29
  8.9 0.1 eq.25
  9.0 0.1 copy.21
  9.1 0.1 mul.120
  9.3 1.2 reduce-window.6
  10.4 0.2 slice_reduce_fusion
  10.7 0.1 fusion.28
  10.9 2.4 scatter_custom_fusion
  13.3 1.0 convert_reduce_fusion
  14.3 14.6 %psum.35 = f32[128]{0:T(128)S(1)} all-reduce(f32[128]{0:T(128)S(1)} %convert_reduce_fusion), channel_id=1, replica_groups=mesh['ctx'=32,'tp'=8] {'tp'}, use_global_device_ids=true, to_apply=%region_5.6 | all-reduce | flops 128 | bytes 1024 | tf_op jit(solution)/shard_map/psum | solution.py:19
  29.0 1.1 fusion.26
  30.0 14.9 %psum.36 = f32[128]{0:T(128)S(1)} all-reduce(f32[128]{0:T(128)S(1)} %fusion.26), channel_id=1, replica_groups=mesh['ctx'=32,'tp'=8] {'tp'}, use_global_device_ids=true, to_apply=%region_7.8 | all-reduce | flops 128 | bytes 1024 | tf_op jit(solution)/shard_map/psum | solution.py:19
  44.9 0.8 copy.20
  45.7 0.1 mul.129
  45.8 0.5 copy-done.4
  46.4 1.0 fusion.20
  47.4 1.0 mul.131
  48.4 0.3 mul.132
  48.7 3.9 gather_fusion
  52.6 0.1 multiply_convert_fusion.1
  52.8 3.9 gather_fusion.2
  56.7 1.2 broadcast_select_fusion
  57.9 20.1 %all_to_all.20 = bf16[32,1,32,384]{3,2,1,0:T(8,128)(2,1)} all-to-all(bf16[32,1,32,384]{3,2,1,0:T(8,128)(2,1)S(1)} %get-tuple-element.16), channel_id=1, replica_groups=mesh['ctx'=32,'tp'=8] {'ctx'}, dimensions={0} | all-to-all | bytes 1572864 | tf_op jit(solution)/shard_map/all_to_all | solution.py:28
  78.1 18.5 %all_to_all.21 = bf16[32,1,32,384]{3,2,1,0:T(8,128)(2,1)} all-to-all(bf16[32,1,32,384]{3,2,1,0:T(8,128)(2,1)} %get-tuple-element.15), channel_id=1, replica_groups=mesh['ctx'=32,'tp'=8] {'ctx'}, dimensions={0} | all-to-all | bytes 1572864 | tf_op jit(solution)/shard_map/all_to_all | solution.py:28
  96.5 0.2 reduce-scatter.9.cloned.1.call-start
  96.8 53.5 %all-gather.3.cloned.1.call-done = bf16[32,1,32,3072]{3,2,1,0:T(8,128)(2,1)} async-done(((bf16[32,1,32,384]{3,2,1,0:T(8,128)(2,1)}), bf16[32,1,32,3072]{3,2,1,0:T(8,128)(2,1)}) %all-gather.3.cloned.1.call-update) | async-done | bytes 6291472 | tf_op jit(solution)/shard_map/all_gather | solution.py:29
  150.2 5.5 %multiply_convert_fusion = (bf16[1024,256]{1,0:T(8,128)(2,1)S(1)}, f32[1024,256]{1,0:T(8,128)}) fusion(bf16[1024,3072]{1,0:T(8,128)(2,1)} %bitcast.93, bf16[1,3072,256]{2,1,0:T(8,128)(2,1)S(1)} %copy-done), kind=kOutput, calls=%fused_computation.22 | convolution fusion | flops 1611923456 | bytes 9437184 | tf_op jit(solution)/shard_map/dot_general | solution.py:84
  155.8 59.6 %all-gather.5.cloned.1.call-done = bf16[32,1,32,3072]{3,2,1,0:T(8,128)(2,1)} async-done(((bf16[32,1,32,384]{3,2,1,0:T(8,128)(2,1)}), bf16[32,1,32,3072]{3,2,1,0:T(8,128)(2,1)}) %all-gather.5.cloned.1.call-update) | async-done | bytes 6291472 | tf_op jit(solution)/shard_map/all_gather | solution.py:29
  215.4 5.5 fusion.9
  220.8 4.5 convert_bitcast_fusion
  225.3 33.6 %copy.33 = bf16[32,1,32,3072]{2,0,1,3:T(8,128)(2,1)} copy(bf16[32,1,32,3072]{3,2,0,1:T(8,128)(2,1)} %convert_bitcast_fusion) | data formatting | bytes 12582912
  258.9 34.1 %reshape.198 = bf16[3072,1024]{1,0:T(8,128)(2,1)} reshape(bf16[3072,1,32,32]{3,2,1,0:T(8,128)(2,1)} %bitcast.80) | data formatting | bytes 12582912
  293.1 0.3 reduce-scatter.7.cloned.1.call-start
  293.3 1.1 copy-done.3
  294.4 4.4 convert_bitcast_fusion.1
  298.8 33.6 %copy.31 = bf16[32,1,32,3072]{2,0,1,3:T(8,128)(2,1)} copy(bf16[32,1,32,3072]{3,2,0,1:T(8,128)(2,1)} %convert_bitcast_fusion.1) | data formatting | bytes 12582912
  332.4 34.3 %reshape.196 = bf16[3072,1024]{1,0:T(8,128)(2,1)} reshape(bf16[3072,1,32,32]{3,2,1,0:T(8,128)(2,1)} %bitcast.81) | data formatting | bytes 12582912
  366.7 10.7 %reduce-scatter.9.cloned.1.call-done = bf16[384,1024]{1,0:T(8,128)(2,1)} async-done(((bf16[3072,1024]{1,0:T(8,128)(2,1)}), bf16[384,1024]{1,0:T(8,128)(2,1)}) %reduce-scatter.9.cloned.1.call-update) | async-done | bytes 786448
  377.5 4.9 reshape.199
  382.3 5.2 copy.34
  387.6 8.0 %all-to-all-start.3 = ((bf16[32,1,32,384]{3,2,1,0:T(8,128)(2,1)}), bf16[32,1,32,384]{3,2,1,0:T(8,128)(2,1)S(1)}, u32[]{:S(2)}, u32[]{:S(2)}) async-start(bf16[32,1,32,384]{3,2,1,0:T(8,128)(2,1)} %bitcast.19), calls=%async_computation.3 | async-start | bytes 1572864 | tf_op jit(solution)/shard_map/all_to_all | solution.py:36
  395.6 0.7 convert_element_type.63
  396.3 70.0 %reduce-scatter.7.cloned.1.call-done = bf16[384,1024]{1,0:T(8,128)(2,1)} async-done(((bf16[3072,1024]{1,0:T(8,128)(2,1)}), bf16[384,1024]{1,0:T(8,128)(2,1)}) %reduce-scatter.7.cloned.1.call-update) | async-done | bytes 786448
  466.3 4.9 reshape.197
  471.2 5.2 copy.32
  476.4 10.4 %all-to-all-start.1 = ((bf16[32,1,32,384]{3,2,1,0:T(8,128)(2,1)}), bf16[32,1,32,384]{3,2,1,0:T(8,128)(2,1)}, u32[]{:S(2)}, u32[]{:S(2)}) async-start(bf16[32,1,32,384]{3,2,1,0:T(8,128)(2,1)} %bitcast.11), calls=%async_computation.1 | async-start | bytes 1572864 | tf_op jit(solution)/shard_map/all_to_all | solution.py:36
  486.8 6.3 %convolution_bitcast_fusion = f32[1,256,3072]{2,1,0:T(8,128)} fusion(bf16[1024,256]{1,0:T(8,128)(2,1)S(1)} %get-tuple-element.19, bf16[1024,3072]{1,0:T(8,128)(2,1)} %bitcast.83), kind=kOutput, calls=%fused_computation.7 | convolution fusion | flops 1610612736 | bytes 9961472 | tf_op jit(solution)/shard_map/dot_general | solution.py:102
  493.1 6.3 %convolution_bitcast_fusion.1 = f32[1,3072,256]{2,1,0:T(8,128)} fusion(bf16[1024,3072]{1,0:T(8,128)(2,1)} %bitcast.94, bf16[1024,256]{1,0:T(8,128)(2,1)S(1)} %fusion.9), kind=kOutput, calls=%fused_computation.8 | convolution fusion | flops 1610612736 | bytes 9961472 | tf_op jit(solution)/shard_map/dot_general | solution.py:107
  499.4 0.2 bitcast_convert_fusion
  499.6 1.6 gather_fusion.3
  501.2 0.2 reshape.147
  501.5 0.1 reduce_sum.84
  501.6 0.5 reduce_sum.83
  502.3 0.2 fusion.21
  502.5 1.2 bitcast_convert_fusion.1
  503.8 2.3 gather_fusion.1
  506.1 1.4 reshape.144
  507.5 1.7 multiply_reduce_fusion
  509.2 28.0 %all-reduce = (f32[128]{0:T(128)S(1)}, f32[128]{0:T(128)S(1)}, f32[128,4]{1,0:T(8,128)S(1)}) all-reduce(f32[128]{0:T(128)S(1)} %fusion.21, f32[128]{0:T(128)S(1)} %reduce_sum.86, f32[128,4]{1,0:T(8,128)S(1)} %get-tuple-element.10), channel_id=1, replica_groups=mesh['ctx'=32,'tp'=8] {'tp'}, use_global_device_ids=true, to_apply=%region_16.17 | all-reduce | flops 768 | bytes 6144 | tf_op jit(solution)/shard_map/psum | solution.py:19
  537.2 0.7 copy.30
  537.8 1.6 subtract_convert_fusion
  539.4 0.8 fusion.25
  (49 shorter events, 0.6 us)
Async XLA Ops:
  7.2 143.1 %copy-start = (bf16[1,3072,256]{2,1,0:T(8,128)(2,1)S(1)}, bf16[1,3072,256]{2,1,0:T(8,128)(2,1)}, u32[]{:S(2)}) copy-start(bf16[1,3072,256]{2,1,0:T(8,128)(2,1)} %param.14) | copy-start | bytes 4718596
  7.2 143.0 %all-gather.3.cloned.1.call-start = ((), (), s32[]{:S(2)}) async-start(), calls=%async_computation.6 | async-start | bytes 7077888 | tf_op jit(solution)/shard_map/all_gather | solution.py:29
  10.8 34.1 %copy-start.8 = (s32[512,1]{0,1:T(1,128)}, s32[512,1]{0,1:T(1,128)S(1)}, u32[]{:S(2)}) copy-start(s32[512,1]{0,1:T(1,128)S(1)} %compare_select_fusion) | copy-start | bytes 6148
  29.0 17.5 %copy-start.10 = (f32[128]{0:T(128)}, f32[128]{0:T(128)S(1)}, u32[]{:S(2)}) copy-start(f32[128]{0:T(128)S(1)} %broadcast_multiply_fusion.3) | copy-start | bytes 1540
  44.9 1.5 copy-start.12
  45.7 0.6 copy-start.4
  78.0 137.4 %all-gather.5.cloned.1.call-start = ((), (), s32[]{:S(2)}) async-start(), calls=%async_computation.7 | async-start | bytes 7077888 | tf_op jit(solution)/shard_map/all_gather | solution.py:29
  96.5 280.9 %reduce-scatter.9.cloned.1.call-start = ((), (), s32[]{:S(2)}) async-start(), calls=%async_computation.9 | async-start | bytes 7077888
  293.0 1.4 copy-start.3
  293.1 173.2 %reduce-scatter.7.cloned.1.call-start = ((), (), s32[]{:S(2)}) async-start(), calls=%async_computation.8 | async-start | bytes 7077888
  382.3 13.3 %copy-start.6 = (bf16[128,384]{1,0:T(8,128)(2,1)S(1)}, bf16[128,384]{1,0:T(8,128)(2,1)}, u32[]{:S(2)}) copy-start(bf16[128,384]{1,0:T(8,128)(2,1)} %param.11) | copy-start | bytes 294916
  382.3 14.0 %copy-start.9 = (s32[512,1]{0,1:T(1,128)S(1)}, s32[512,1]{0,1:T(1,128)}, u32[]{:S(2)}) copy-start(s32[512,1]{0,1:T(1,128)} %copy-done.8) | copy-start | bytes 6148
  387.6 88.8 %all-to-all-start.3 = ((bf16[32,1,32,384]{3,2,1,0:T(8,128)(2,1)}), bf16[32,1,32,384]{3,2,1,0:T(8,128)(2,1)S(1)}, u32[]{:S(2)}, u32[]{:S(2)}) async-start(bf16[32,1,32,384]{3,2,1,0:T(8,128)(2,1)} %bitcast.19), calls=%async_computation.3 | async-start | bytes 1572864 | tf_op jit(solution)/shard_map/all_to_all | solution.py:36
  476.4 26.1 %all-to-all-start.1 = ((bf16[32,1,32,384]{3,2,1,0:T(8,128)(2,1)}), bf16[32,1,32,384]{3,2,1,0:T(8,128)(2,1)}, u32[]{:S(2)}, u32[]{:S(2)}) async-start(bf16[32,1,32,384]{3,2,1,0:T(8,128)(2,1)} %bitcast.11), calls=%async_computation.1 | async-start | bytes 1572864 | tf_op jit(solution)/shard_map/all_to_all | solution.py:36
  501.2 1.1 copy-start.2
  501.2 1.1 copy-start.11
  501.2 1.1 copy-start.13
  503.8 3.7 copy-start.5
  503.8 36.4 %copy-start.1 = (bf16[1,3072,256]{2,1,0:T(8,128)(2,1)S(1)}, bf16[1,3072,256]{2,1,0:T(8,128)(2,1)}, u32[]{:S(2)}) copy-start(bf16[1,3072,256]{2,1,0:T(8,128)(2,1)} %param.14) | copy-start | bytes 4718596
  506.1 33.3 %copy-start.7 = (bf16[128,384]{1,0:T(8,128)(2,1)S(1)}, bf16[128,384]{1,0:T(8,128)(2,1)}, u32[]{:S(2)}) copy-start(bf16[128,384]{1,0:T(8,128)(2,1)} %param.10) | copy-start | bytes 294916
Sparse Core Ops, SparseCore 0:
  78.1 72.0 all-gather.2
  152.1 63.2 all-gather.4
  293.2 84.2 reduce-scatter.8
  379.9 86.3 reduce-scatter.6
where the time goes:
time: 550 us; the launch traced here: 547 us
  waiting for transfers between devices  194 us (35%)
  local copies, waits for them, and re-layouts  178 us (32%)
  blocking collectives  96 us (17%)
  matrix products  32.5 us (6%)
  starting transfers between devices  19 us (3%)
  between operations  14.1 us (3%)
  other arithmetic  13.6 us (2%)
    unnamed x39, local copies, waits for them, and re-layouts  160 us
    all_gather x2, waiting for transfers between devices, send_out(): return lax.all_gather(arrived, 'tp', axis=3, tiled=True)  113 us
    unnamed x6, waiting for transfers between devices  80.8 us
    psum x3, blocking collectives, feature_sums(): return lax.psum(values, 'tp')  57.5 us
    all_to_all x2, blocking collectives, send_out(): lax.all_to_all(buffer, 'ctx', split_axis=0, concat_axis=0, tiled=True)  38.6 us
    all_to_all x2, starting transfers between devices, bring_back(): lax.all_to_all(summed.astype(jnp.bfloat16), 'ctx', split_axis=0, concat_a...  18.4 us
  transfers between devices with their start and end apart: 6, of which 4 were waited for; matrix products, arithmetic and copies ran while one was open for 21% of the time, Pallas kernels for 0%

commit v1 on v0

v1 whole, which is shorter than its diff:
```python
import functools

import jax
import jax.numpy as jnp
from jax import lax
from jax.experimental import pallas as pl
from jax.experimental.pallas import tpu as pltpu
from jax.sharding import Mesh, PartitionSpec as P

F32 = jnp.float32
BF16 = jnp.bfloat16
CTX = ("y", "zl", "x")
CORES = ((0, 1), (1, 0))


def gelu_value(x):
    return x * 0.5 * (1.0 + lax.erf(x * 0.7071067811865476))


def gelu_slope(x):
    return (
        0.5 * (1.0 + lax.erf(x * 0.7071067811865476))
        + x * jnp.exp(-0.5 * x * x) * 0.3989422804014327
    )


def swap_cores(v):
    return lax.ppermute(v, "core", CORES)


def swap_chips(v, r):
    return lax.ppermute(v, "zh", [(i, i ^ r) for i in range(4)])


def gather_features(v):
    mine = [v] + [swap_chips(v, r) for r in (1, 2, 3)]
    return mine + [swap_cores(m) for m in mine]


def select_rows(qt, slots):
    topk, tokens = qt.shape
    at = lax.broadcasted_iota(jnp.int32, (slots, tokens), 0)
    hit = at == qt[0:1, :]
    for k in range(1, topk):
        hit = jnp.logical_or(hit, at == qt[k : k + 1, :])
    return hit


def pack_first_kernel(order, qt_ref, *refs):
    parts, (out_ref, full_ref, stats_ref, low, pick) = refs[:8], refs[8:]
    step = pl.program_id(0)

    @pl.when(step == 0)
    def _():
        width = 8 * parts[0].shape[1]
        total = sum(jnp.sum(p[...].astype(F32), axis=1, keepdims=True) for p in parts)
        mean = total / width
        square = sum(
            jnp.sum(jnp.square(p[...].astype(F32) - mean), axis=1, keepdims=True) for p in parts
        )
        rstd = lax.rsqrt(square / width + 1e-05)
        for i, p in enumerate(parts):
            low[i] = ((p[...].astype(F32) - mean) * rstd).astype(BF16)
        lane = lax.broadcasted_iota(jnp.int32, stats_ref.shape, 1)
        stats_ref[...] = jnp.where(lane == 0, mean, rstd)
        pick[...] = jnp.where(select_rows(qt_ref[...], pick.shape[0]), 1.0, 0.0).astype(BF16)

    for i, p in enumerate(parts):

        @pl.when(step == i)
        def _(p=p):
            full_ref[...] = p[...]

    out_ref[...] = jnp.dot(pick[...], low[step], preferred_element_type=F32).astype(BF16)


def pack_grad_kernel(order, qt_ref, gt_ref, *refs):
    parts, (out_ref, full_ref, pick, gate) = refs[:8], refs[8:]
    step = pl.program_id(0)

    @pl.when(step == 0)
    def _():
        slots = pick.shape[0]
        qt, gt = qt_ref[...], gt_ref[...]
        pick[...] = jnp.where(select_rows(qt, slots), 1.0, 0.0).astype(BF16)
        at = lax.broadcasted_iota(jnp.int32, (slots, qt.shape[1]), 0)
        weight = jnp.zeros((slots, qt.shape[1]), F32)
        for k in range(qt.shape[0]):
            weight = weight + jnp.where(at == qt[k : k + 1, :], gt[k : k + 1, :], 0.0)
        gate[...] = jnp.sum(weight, axis=1, keepdims=True)

    for i, p in enumerate(parts):

        @pl.when(step == i)
        def _(p=p):
            full_ref[...] = p[...]
            rows = jnp.dot(pick[...], p[...], preferred_element_type=F32)
            out_ref[...] = (gate[...] * rows).astype(BF16)


def store_parts(step, value, keep_ref, give_ref):
    @pl.when(step < 4)
    def _():
        keep_ref[0] = value.astype(BF16)

    @pl.when(step >= 4)
    def _():
        give_ref[0] = value.astype(BF16)


def combine_out_kernel(order, q_ref, g_ref, rows_ref, full_ref, keep_ref, give_ref, inner_ref, high, rest, inner):
    step = pl.program_id(0)

    @pl.when(step == 0)
    def _():
        lane = lax.broadcasted_iota(jnp.int32, inner.shape, 1)
        weight = jnp.zeros(inner.shape, F32)
        for k in range(q_ref.shape[1]):
            weight = weight + jnp.where(lane == q_ref[:, k : k + 1], g_ref[:, k : k + 1], 0.0)
        top = weight.astype(BF16)
        high[...] = top
        rest[...] = (weight - top.astype(F32)).astype(BF16)
        inner[...] = jnp.zeros_like(inner)

    rows = rows_ref[...]
    value = jnp.dot(high[...], rows, preferred_element_type=F32) + jnp.dot(
        rest[...], rows, preferred_element_type=F32
    )
    store_parts(step, value, keep_ref, give_ref)
    inner[...] += lax.dot_general(
        full_ref[...], rows, (((1,), (1,)), ((), ())), preferred_element_type=F32
    )

    @pl.when(step == 7)
    def _():
        lane = lax.broadcasted_iota(jnp.int32, inner.shape, 1)
        place = lax.broadcasted_iota(jnp.int32, inner_ref.shape, 1)
        found = jnp.zeros(inner_ref.shape, F32)
        for k in range(q_ref.shape[1]):
            one = jnp.sum(
                jnp.where(lane == q_ref[:, k : k + 1], inner[...], 0.0), axis=1, keepdims=True
            )
            found = found + jnp.where(place == k, one, 0.0)
        inner_ref[...] = found


def combine_dx_kernel(order, q_ref, inner_ref, stats_ref, rows_ref, full_ref, keep_ref, give_ref, sums_ref, pick, sums):
    step = pl.program_id(0)

    @pl.when(step == 0)
    def _():
        lane = lax.broadcasted_iota(jnp.int32, pick.shape, 1)
        hit = lane == q_ref[:, 0:1]
        for k in range(1, q_ref.shape[1]):
            hit = jnp.logical_or(hit, lane == q_ref[:, k : k + 1])
        pick[...] = jnp.where(hit, 1.0, 0.0).astype(BF16)
        sums[...] = jnp.zeros_like(sums)

    value = jnp.dot(pick[...], rows_ref[...], preferred_element_type=F32)
    store_parts(step, value, keep_ref, give_ref)
    normed = (full_ref[...].astype(F32) - stats_ref[:, 0:1]) * stats_ref[:, 1:2]
    place = lax.broadcasted_iota(jnp.int32, sums.shape, 1)
    plain = jnp.sum(value, axis=1, keepdims=True)
    mixed = jnp.sum(value * normed, axis=1, keepdims=True)
    sums[...] += jnp.where(place == 4, plain, 0.0) + jnp.where(place == 5, mixed, 0.0)

    @pl.when(step == 7)
    def _():
        sums_ref[...] = sums[...] + inner_ref[...]


def whole(shape):
    return pl.BlockSpec(shape, lambda i, order: (0,) * len(shape))


def run(kernel, order, args, in_specs, out_shape, out_specs, scratch, flops, moved):
    return pl.pallas_call(
        kernel,
        grid_spec=pltpu.PrefetchScalarGridSpec(
            num_scalar_prefetch=1,
            grid=(8,),
            in_specs=in_specs,
            out_specs=out_specs,
            scratch_shapes=scratch,
        ),
        out_shape=out_shape,
        compiler_params=pltpu.CompilerParams(
            dimension_semantics=("arbitrary",), vmem_limit_bytes=24 * 2**20
        ),
        cost_estimate=pl.CostEstimate(flops=flops, bytes_accessed=moved, transcendentals=0),
    )(order, *args)


def on_device(
    stream_first, stream_second, grad_first, grad_second, expert_ids, gate_probs, w_in, w_out
):
    tokens, part = stream_first.shape
    topk = expert_ids.shape[1]
    width = part * 8
    experts = 32
    half = 16
    slots = experts * half
    core = lax.axis_index("core")
    zh = lax.axis_index("zh")

    expert = jnp.arange(experts, dtype=jnp.int32)
    match = expert_ids[:, :, None] == expert[None, None, :]
    named = jnp.any(match, axis=1).astype(BF16)
    earlier = jnp.tri(tokens, k=-1, dtype=BF16)
    before = jnp.dot(earlier, named, preferred_element_type=F32)
    rank = jnp.sum(jnp.where(match, before[:, None, :], 0.0), axis=2).astype(jnp.int32)
    q = jnp.where(rank % 2 == core, expert_ids * half + rank // 2, -1)
    qt = q.T
    gt = gate_probs.T
    lanes = jnp.arange(4, dtype=jnp.int32)
    columns = (jnp.bitwise_xor(zh, lanes)) * 2
    order = jnp.concatenate([columns + core, columns + (1 - core)]).astype(jnp.int32)

    first_parts = gather_features(stream_first)
    second_parts = gather_features(grad_second)

    block = pl.BlockSpec((slots, part), lambda i, order: (0, order[i]))
    token_block = pl.BlockSpec((tokens, part), lambda i, order: (0, order[i]))
    keep_spec = pl.BlockSpec((1, tokens, part), lambda i, order: (jnp.minimum(i, 3), 0, 0))
    give_spec = pl.BlockSpec((1, tokens, part), lambda i, order: (jnp.maximum(i - 4, 0), 0, 0))
    rows_shape = jax.ShapeDtypeStruct((slots, width), BF16)
    full_shape = jax.ShapeDtypeStruct((tokens, width), BF16)
    lane_shape = jax.ShapeDtypeStruct((tokens, 128), F32)
    parts_shape = jax.ShapeDtypeStruct((4, tokens, part), BF16)
    pick_flops = 2 * slots * tokens * width

    rows, first_full, stats = run(
        pack_first_kernel, order, (qt, *first_parts),
        [whole((topk, tokens))] + [whole((tokens, part))] * 8,
        (rows_shape, full_shape, lane_shape),
        (block, token_block, whole((tokens, 128))),
        [pltpu.VMEM((8, tokens, part), BF16), pltpu.VMEM((slots, tokens), BF16)],
        pick_flops, 2 * slots * width,
    )
    send = functools.partial(
        lax.all_to_all, axis_name=CTX, split_axis=0, concat_axis=0, tiled=True
    )
    x = send(rows)
    grad_rows, second_full = run(
        pack_grad_kernel, order, (qt, gt, *second_parts),
        [whole((topk, tokens))] * 2 + [whole((tokens, part))] * 8,
        (rows_shape, full_shape),
        (block, token_block),
        [pltpu.VMEM((slots, tokens), BF16), pltpu.VMEM((slots, 1), F32)],
        pick_flops, 2 * slots * width,
    )
    g = send(grad_rows)

    wi = jnp.concatenate([w_in[0], swap_cores(w_in[0])], axis=1)
    wo = jnp.concatenate([w_out[0], swap_cores(w_out[0])], axis=0)
    own = w_out.shape[1]

    preact = jnp.dot(x, wi, preferred_element_type=F32)
    hidden = gelu_value(preact).astype(BF16)
    result = jnp.dot(hidden, wo, preferred_element_type=F32).astype(BF16)
    back = send(result)
    grad_hidden = lax.dot_general(g, wo, (((1,), (1,)), ((), ())), preferred_element_type=F32)
    grad_pre = (grad_hidden * gelu_slope(preact)).astype(BF16)
    route_dx = lax.dot_general(
        grad_pre, wi, (((1,), (1,)), ((), ())), preferred_element_type=F32
    ).astype(BF16)
    back_dx = send(route_dx)

    rows_rows = (((0,), (0,)), ((), ()))
    out_give = lax.dot_general(hidden[:, own:], g, rows_rows, preferred_element_type=F32).astype(BF16)
    out_got = swap_cores(out_give)
    grad_w_out = lax.dot_general(
        hidden[:, :own], g, rows_rows, preferred_element_type=F32
    ) + out_got.astype(F32)
    in_give = lax.dot_general(x, grad_pre[:, own:], rows_rows, preferred_element_type=F32).astype(BF16)
    in_got = swap_cores(in_give)
    grad_w_in = lax.dot_general(
        x, grad_pre[:, :own], rows_rows, preferred_element_type=F32
    ) + in_got.astype(F32)

    def reduce_parts(keep, give):
        got = swap_cores(give)
        half_sum = [(keep[r].astype(F32) + got[r].astype(F32)) for r in range(4)]
        arrived = [swap_chips(half_sum[r].astype(BF16), r).astype(F32) for r in (1, 2, 3)]
        return half_sum[0] + arrived[0] + arrived[1] + arrived[2]

    keep, give, inner = run(
        combine_out_kernel, order, (q, gate_probs, back, second_full),
        [whole((tokens, topk))] * 2 + [block, token_block],
        (parts_shape, parts_shape, lane_shape),
        (keep_spec, give_spec, whole((tokens, 128))),
        [pltpu.VMEM((tokens, slots), BF16)] * 2 + [pltpu.VMEM((tokens, slots), F32)],
        3 * pick_flops, 2 * slots * width,
    )
    branch = reduce_parts(keep, give)
    stream_input = (stream_second.astype(F32) - branch).astype(BF16)

    keep, give, sums = run(
        combine_dx_kernel, order, (q, inner, stats, back_dx, first_full),
        [whole((tokens, topk))] + [whole((tokens, 128))] * 2 + [block, token_block],
        (parts_shape, parts_shape, lane_shape),
        (keep_spec, give_spec, whole((tokens, 128))),
        [pltpu.VMEM((tokens, slots), BF16), pltpu.VMEM((tokens, 128), F32)],
        pick_flops, 2 * slots * width,
    )
    sums = sums + swap_cores(sums)
    s1, s2, s3 = [swap_chips(sums, r) for r in (1, 2, 3)]
    sums = (sums + s1) + (s2 + s3)
    grad_normed = reduce_parts(keep, give)
    mean, rstd = stats[:, 0:1], stats[:, 1:2]
    normed = (stream_first.astype(F32) - mean) * rstd
    correction = grad_normed - sums[:, 4:5] / width - normed * (sums[:, 5:6] / width)
    grad_stream = (grad_first.astype(F32) + rstd * correction).astype(BF16)
    return stream_input, grad_stream, grad_w_in[None], grad_w_out[None], sums[:, :topk]


def solution(mesh):
    wide = Mesh(
        mesh.devices.reshape(4, 2, 4, 4, 2), ("y", "zl", "x", "zh", "core")
    )
    tp = ("zh", "core")
    in_specs = (
        P(CTX, tp),
        P(CTX, tp),
        P(CTX, tp),
        P(CTX, tp),
        P(CTX, None),
        P(CTX, None),
        P(CTX, None, tp),
        P(CTX, tp, None),
    )
    out_specs = (
        P(CTX, tp),
        P(CTX, tp),
        P(CTX, None, tp),
        P(CTX, tp, None),
        P(CTX, None),
    )
    return jax.shard_map(
        on_device, mesh=wide, in_specs=in_specs, out_specs=out_specs, check_vma=False
    )
```

time: 550 us -> 293 us (0.53)
  local copies, waits for them, and re-layouts: 178 us -> 13.5 us
  blocking collectives: 96 us -> 0 us
  waiting for transfers between devices: 194 us -> 132 us
  starting transfers between devices: 19 us -> 79.1 us
  Pallas kernels: 0 us -> 23.1 us
  between operations: 14.1 us -> 0.95 us
  other arithmetic: 13.6 us -> 4.16 us
    unnamed x39 -> x58, local copies, waits for them, and re-layouts: 160 us -> 13 us
    all_gather x2 -> x0, waiting for transfers between devices: 113 us -> none  [send_out(): return lax.all_gather(arrived, 'tp', axis=3, tiled=True)]
    unnamed x6 -> x0, waiting for transfers between devices: 80.8 us -> none
    all_to_all x2 -> x4, waiting for transfers between devices: 0.01 us -> 74.3 us  [the longest x1 30.5 us: on_device(): back = send(result)]
    psum x3 -> x0, blocking collectives: 57.5 us -> none  [feature_sums(): return lax.psum(values, 'tp')]
    ppermute x0 -> x30, waiting for transfers between devices: none -> 57.4 us  [the longest x15 51.3 us: swap_chips(): return lax.ppermute(v, 'zh', [(i, i ^ r) for i in range(4)])]
    ppermute x0 -> x30, starting transfers between devices: none -> 44.6 us  [the longest x15 27.3 us: swap_chips(): return lax.ppermute(v, 'zh', [(i, i ^ r) for i in range(4)])]
    all_to_all x2 -> x0, blocking collectives: 38.6 us -> none  [send_out(): lax.all_to_all(buffer, 'ctx', split_axis=0, concat_axis=0, tiled=True)]
  transfers between devices with their start and end apart: 6 -> 34, of which waited for: 4 -> 13; matrix products, arithmetic and copies ran while one was open for 21% -> 14% of each run, Pallas kernels for 0% -> 6%
where the time goes in v1:
time: 293 us; the launch traced here: 289 us
  waiting for transfers between devices  132 us (45%)
  starting transfers between devices  79.1 us (27%)
  matrix products  36.6 us (12%)
  Pallas kernels  23.1 us (8%)
  local copies, waits for them, and re-layouts  13.5 us (5%)
  other arithmetic  4.16 us (1%)
    ppermute x15, waiting for transfers between devices, swap_chips(): return lax.ppermute(v, 'zh', [(i, i ^ r) for i in range(4)])  51.3 us
    all_to_all x1, waiting for transfers between devices, on_device(): back = send(result)  30.5 us
    ppermute x15, starting transfers between devices, swap_chips(): return lax.ppermute(v, 'zh', [(i, i ^ r) for i in range(4)])  27.3 us
    all_to_all x1, waiting for transfers between devices, on_device(): g = send(grad_rows)  25 us
    pallas_call x4, Pallas kernels, run(): pl.pallas_call(kernel, grid_spec=pltpu.PrefetchScalarGridSpec(num_scalar_...  23.1 us
    all_to_all x1, waiting for transfers between devices, on_device(): back_dx = send(route_dx)  18.9 us
    ppermute x15, starting transfers between devices, swap_cores(): return lax.ppermute(v, 'core', CORES)  17.2 us
    unnamed x58, local copies, waits for them, and re-layouts  13 us
  transfers between devices with their start and end apart: 34, of which 13 were waited for; matrix products, arithmetic and copies ran while one was open for 14% of the time, Pallas kernels for 6%

profile of v1, /device:TPU:65, one launch (start us, length us, event | category | flops | bytes accessed | tf_op | source)
XLA Modules:
  0.0 289.0 jit_solution(1256879202468003372)
XLA Ops:
  0.7 6.3 %collective-permute-start.1 = (bf16[128,384]{1,0:T(8,128)(2,1)}, bf16[128,384]{1,0:T(8,128)(2,1)S(1)}, u32[]{:S(2)}, u32[]{:S(2)}) collective-permute-start(bf16[128,384]{1,0:T(8,128)(2,1)} %refs_0_.2), channel_id=1, source_target_pairs={{0,4},{2,6},{4,0},{6,2},{1,5},{3,7},{5,1},{7,3},{8,12},{10,14},{12... | collective-permute-start | bytes 294920 | tf_op jit(solution)/shard_map/ppermute | solution.py:32
  7.0 1.2 collective-permute-start.3
  8.2 0.7 fusion.38
  9.1 0.7 select_reduce_fusion
  10.1 0.7 multiply_add_fusion
  11.2 2.5 collective-permute-start.5
  13.6 3.5 %collective-permute-done.2.refs_3_ = bf16[128,384]{1,0:T(8,128)(2,1)S(1)} collective-permute-done((bf16[128,384]{1,0:T(8,128)(2,1)}, bf16[128,384]{1,0:T(8,128)(2,1)S(1)}, u32[]{:S(2)}, u32[]{:S(2)}) %collective-permute-start.2) | collective-permute-done | bytes 98336 | tf_op jit(solution)/shard_map/ppermute | solution.py:32
  17.1 0.9 collective-permute-start.6
  18.2 0.9 collective-permute-done.6.refs_7_
  19.0 0.9 copy-done.8
  19.9 5.9 %shard_map.119 = (bf16[512,3072]{1,0:T(8,128)(2,1)}, bf16[128,3072]{1,0:T(8,128)(2,1)S(1)}, f32[128,128]{1,0:T(8,128)S(1)}) custom-call(s32[8]{0:T(128)S(1)} %pad_add_fusion.order, s32[4,128]{1,0:T(4,128)S(1)} %copy.42.qt_ref, bf16[128,384]{1,0:T(8,128)(2,1)S(1)} %copy-done.8, bf16[128,384]{1,0:T(8,128)(2,1)S(1)} %collective-permute-done.refs_1_, ...), custom_call_target="tpu_custom_call" | custom-call | flops 402653184 | bytes 3145728 | tf_op jit(solution)/shard_map/pallas_call | solution.py:177
  25.8 0.9 copy-done.2
  26.7 7.3 %all-to-all-start = ((bf16[32,16,3072]{2,1,0:T(8,128)(2,1)}), bf16[32,16,3072]{2,1,0:T(8,128)(2,1)}, u32[]{:S(2)}, u32[]{:S(2)}) async-start(bf16[32,16,3072]{2,1,0:T(8,128)(2,1)} %bitcast.1), calls=%async_computation | async-start | bytes 6291456 | tf_op jit(solution)/shard_map/all_to_all | solution.py:243
  34.0 1.4 collective-permute-start.9
  35.4 4.3 %collective-permute-start.10 = (bf16[128,384]{1,0:T(8,128)(2,1)S(1)}, bf16[128,384]{1,0:T(8,128)(2,1)S(1)}, u32[]{:S(2)}, u32[]{:S(2)}) collective-permute-start(bf16[128,384]{1,0:T(8,128)(2,1)S(1)} %copy-done.13), channel_id=1, source_target_pairs={{0,4},{2,6},{4,0},{6,2},{1,5},{3,7},{5,1},{7,3},{8,12},{10,14},{12... | collective-permute-start | bytes 294920 | tf_op jit(solution)/shard_map/ppermute | solution.py:32
  39.7 1.5 collective-permute-start.12
  41.2 35.7 %collective-permute-done.9.refs_1_ = bf16[128,384]{1,0:T(8,128)(2,1)S(1)} collective-permute-done((bf16[128,384]{1,0:T(8,128)(2,1)S(1)}, bf16[128,384]{1,0:T(8,128)(2,1)S(1)}, u32[]{:S(2)}, u32[]{:S(2)}) %collective-permute-start.9) | collective-permute-done | bytes 98336 | tf_op jit(solution)/shard_map/ppermute | solution.py:32
  76.9 3.9 %collective-permute-start.13 = (bf16[128,384]{1,0:T(8,128)(2,1)S(1)}, bf16[128,384]{1,0:T(8,128)(2,1)S(1)}, u32[]{:S(2)}, u32[]{:S(2)}) collective-permute-start(bf16[128,384]{1,0:T(8,128)(2,1)S(1)} %collective-permute-done.9.refs_1_), channel_id=1, source_target_pairs={{0,1},{1,0},{2,3},{3,2},{4,5},{5,4},{6,7},{7,6},{8,9},{9,8},{10,11... | collective-permute-start | bytes 294920 | tf_op jit(solution)/shard_map/ppermute | solution.py:28
  80.9 0.4 collective-permute-start.15
  81.4 0.4 collective-permute-done.13.refs_5_
  82.3 5.1 %shard_map.120 = (bf16[512,3072]{1,0:T(8,128)(2,1)}, bf16[128,3072]{1,0:T(8,128)(2,1)S(1)}) custom-call(s32[8]{0:T(128)S(1)} %pad_add_fusion.order, s32[4,128]{1,0:T(4,128)S(1)} %copy.42.qt_ref, f32[4,128]{1,0:T(4,128)S(1)} %bitcast.67, bf16[128,384]{1,0:T(8,128)(2,1)S(1)} %copy-done.13, bf16[128,384]{1,0:T(8,128)(2,1)S(1)} %collective-permute-done.9.refs_1_, ...), custom_call_target="tpu_custom_call" | custom-call | flops 402653184 | bytes 3145728 | tf_op jit(solution)/shard_map/pallas_call | solution.py:177
  87.5 0.9 copy-done.14
  88.4 11.1 %all-to-all-start.2 = ((bf16[32,16,3072]{2,1,0:T(8,128)(2,1)}), bf16[32,16,3072]{2,1,0:T(8,128)(2,1)}, u32[]{:S(2)}, u32[]{:S(2)}) async-start(bf16[32,16,3072]{2,1,0:T(8,128)(2,1)} %bitcast.12), calls=%async_computation.2 | async-start | bytes 6291456 | tf_op jit(solution)/shard_map/all_to_all | solution.py:252
  99.5 0.9 collective-permute-start.7
  100.5 4.3 %collective-permute-done.7 = bf16[3072,256]{1,0:T(8,128)(2,1)S(1)} collective-permute-done((bf16[3072,256]{1,0:T(8,128)(2,1)}, bf16[3072,256]{1,0:T(8,128)(2,1)S(1)}, u32[]{:S(2)}, u32[]{:S(2)}) %collective-permute-start.7) | collective-permute-done | bytes 1572896 | tf_op jit(solution)/shard_map/ppermute | solution.py:28
  104.7 5.7 %multiply_convert_fusion = (bf16[512,512]{1,0:T(8,128)(2,1)S(1)}, f32[512,512]{1,0:T(8,128)}) fusion(bf16[512,3072]{1,0:T(8,128)(2,1)} %bitcast.2, bf16[3072,256]{1,0:T(8,128)(2,1)S(1)} %collective-permute-done.7, bf16[3072,256]{1,0:T(8,128)(2,1)} %bitcast.75), kind=kOutput, calls=%fused_computation.17 | convolution fusion | flops 1618214912 | bytes 7864320 | tf_op jit(solution)/shard_map/dot_general | solution.py:258
  110.5 0.8 copy-done.16
  111.2 0.6 copy-done.25
  111.8 3.5 %convolution_convert_fusion.1 = bf16[512,3072]{1,0:T(8,128)(2,1)} fusion(bf16[512,512]{1,0:T(8,128)(2,1)S(1)} %get-tuple-element.57, bf16[256,3072]{1,0:T(8,128)(2,1)S(1)} %collective-permute-done.8, bf16[256,3072]{1,0:T(8,128)(2,1)S(1)} %bitcast.73), kind=kOutput, calls=%fused_computation.1 | convolution fusion | flops 1618477056 | bytes 6815744 | tf_op jit(solution)/shard_map/dot_general | solution.py:260
  115.3 25.0 %all-to-all-done.2 = bf16[32,16,3072]{2,1,0:T(8,128)(2,1)} async-done(((bf16[32,16,3072]{2,1,0:T(8,128)(2,1)}), bf16[32,16,3072]{2,1,0:T(8,128)(2,1)}, u32[]{:S(2)}, u32[]{:S(2)}) %all-to-all-start.2) | async-done | bytes 3145760 | tf_op jit(solution)/shard_map/all_to_all | solution.py:252
  140.3 8.0 %all-to-all-start.1 = ((bf16[32,16,3072]{2,1,0:T(8,128)(2,1)}), bf16[32,16,3072]{2,1,0:T(8,128)(2,1)S(1)}, u32[]{:S(2)}, u32[]{:S(2)}) async-start(bf16[32,16,3072]{2,1,0:T(8,128)(2,1)} %bitcast.69), calls=%async_computation.1 | async-start | bytes 6291456 | tf_op jit(solution)/shard_map/all_to_all | solution.py:261
  148.3 5.3 %fusion.3 = bf16[512,512]{1,0:T(8,128)(2,1)S(1)} fusion(bf16[512,3072]{1,0:T(8,128)(2,1)} %bitcast.13, bf16[256,3072]{1,0:T(8,128)(2,1)} %copy-done.25, bf16[256,3072]{1,0:T(8,128)(2,1)} %bitcast.71, f32[512,512]{1,0:T(8,128)} %get-tuple-element.58), kind=kOutput, calls=%fused_computation.12 | convolution fusion | flops 1619525632 | bytes 7864320 | tf_op jit(solution)/shard_map/dot_general | solution.py:262
  153.6 0.8 copy-done.26
  154.4 3.5 %convolution_convert_fusion = bf16[512,3072]{1,0:T(8,128)(2,1)} fusion(bf16[512,512]{1,0:T(8,128)(2,1)S(1)} %fusion.3, bf16[3072,256]{1,0:T(8,128)(2,1)S(1)} %copy-done.24, bf16[3072,256]{1,0:T(8,128)(2,1)S(1)} %bitcast.76), kind=kOutput, calls=%fused_computation | convolution fusion | flops 1618477056 | bytes 6815744 | tf_op jit(solution)/shard_map/dot_general | solution.py:264
  157.9 30.5 %all-to-all-done.1 = bf16[32,16,3072]{2,1,0:T(8,128)(2,1)S(1)} async-done(((bf16[32,16,3072]{2,1,0:T(8,128)(2,1)}), bf16[32,16,3072]{2,1,0:T(8,128)(2,1)S(1)}, u32[]{:S(2)}, u32[]{:S(2)}) %all-to-all-start.1) | async-done | bytes 3145760 | tf_op jit(solution)/shard_map/all_to_all | solution.py:261
  188.4 1.7 copy-done
  190.1 8.1 %all-to-all-start.3 = ((bf16[32,16,3072]{2,1,0:T(8,128)(2,1)}), bf16[32,16,3072]{2,1,0:T(8,128)(2,1)S(1)}, u32[]{:S(2)}, u32[]{:S(2)}) async-start(bf16[32,16,3072]{2,1,0:T(8,128)(2,1)} %bitcast.68), calls=%async_computation.3 | async-start | bytes 6291456 | tf_op jit(solution)/shard_map/all_to_all | solution.py:267
  198.2 4.2 %convolution_convert_fusion.3 = bf16[3072,256]{1,0:T(8,128)(2,1)} fusion(bf16[512,3072]{1,0:T(8,128)(2,1)} %bitcast.2, bf16[512,512]{1,0:T(8,128)(2,1)} %copy-done.26), kind=kOutput, calls=%fused_computation.3 | convolution fusion | flops 806092800 | bytes 4980736 | tf_op jit(solution)/shard_map/dot_general | solution.py:275
  202.4 1.0 collective-permute-start.28
  203.4 4.1 %convolution_convert_fusion.2 = bf16[256,3072]{1,0:T(8,128)(2,1)} fusion(bf16[512,3072]{1,0:T(8,128)(2,1)} %bitcast.13, bf16[512,512]{1,0:T(8,128)(2,1)S(1)} %copy-done.17), kind=kOutput, calls=%fused_computation.2 | convolution fusion | flops 806092800 | bytes 4980736 | tf_op jit(solution)/shard_map/dot_general | solution.py:270
  207.8 1.9 copy-done.1
  209.6 1.1 copy-done.15
  210.8 6.6 %shard_map.121 = (bf16[4,128,384]{2,1,0:T(8,128)(2,1)S(1)}, bf16[4,128,384]{2,1,0:T(8,128)(2,1)S(1)}, f32[128,128]{1,0:T(8,128)S(1)}) custom-call(s32[8]{0:T(128)S(1)} %pad_add_fusion.order, s32[128,4]{1,0:T(8,128)S(1)} %fusion.41.q_ref, f32[128,4]{1,0:T(8,128)S(1)} %copy.44.g_ref, bf16[512,3072]{1,0:T(8,128)(2,1)S(1)} %bitcast.65, ...), custom_call_target="tpu_custom_call" | custom-call | flops 1207959552 | bytes 3145728 | tf_op jit(solution)/shard_map/pallas_call | solution.py:177
  217.3 0.7 copy-done.6
  218.1 0.7 copy-done.11
  218.8 18.9 %all-to-all-done.3 = bf16[32,16,3072]{2,1,0:T(8,128)(2,1)S(1)} async-done(((bf16[32,16,3072]{2,1,0:T(8,128)(2,1)}), bf16[32,16,3072]{2,1,0:T(8,128)(2,1)S(1)}, u32[]{:S(2)}, u32[]{:S(2)}) %all-to-all-start.3) | async-done | bytes 3145760 | tf_op jit(solution)/shard_map/all_to_all | solution.py:267
  237.7 1.1 copy-done.3
  238.9 5.6 %shard_map.122 = (bf16[4,128,384]{2,1,0:T(8,128)(2,1)S(1)}, bf16[4,128,384]{2,1,0:T(8,128)(2,1)}, f32[128,128]{1,0:T(8,128)S(1)}) custom-call(s32[8]{0:T(128)S(1)} %pad_add_fusion.order, s32[128,4]{1,0:T(8,128)S(1)} %fusion.41.q_ref, f32[128,128]{1,0:T(8,128)S(1)} %get-tuple-element.21.inner_ref, f32[128,128]{1,0:T(8,128)S(1)} %get-tuple-element.20.stats_ref, ...), custom_call_target="tpu_custom_call" | custom-call | flops 402653184 | bytes 3145728 | tf_op jit(solution)/shard_map/pallas_call | solution.py:177
  244.4 3.2 %collective-permute-start.24 = (f32[128,128]{1,0:T(8,128)S(1)}, f32[128,128]{1,0:T(8,128)S(1)}, u32[]{:S(2)}, u32[]{:S(2)}) collective-permute-start(f32[128,128]{1,0:T(8,128)S(1)} %get-tuple-element.26), channel_id=1, source_target_pairs={{0,1},{1,0},{2,3},{3,2},{4,5},{5,4},{6,7},{7,6},{8,9},{9,8},{10,11... | collective-permute-start | bytes 196616 | tf_op jit(solution)/shard_map/ppermute | solution.py:28
  247.6 5.0 %add_bitcast_fusion.1 = f32[1,3072,256]{2,1,0:T(8,128)} fusion(bf16[3072,256]{1,0:T(8,128)(2,1)} %collective-permute-done.28, bf16[512,3072]{1,0:T(8,128)(2,1)} %bitcast.2, bf16[512,512]{1,0:T(8,128)(2,1)S(1)} %copy-done.27), kind=kOutput, calls=%fused_computation.7 | convolution fusion | flops 806879232 | bytes 8126464 | tf_op jit(solution)/shard_map/dot_general | solution.py:277
  252.9 1.3 collective-permute-start.26
  254.2 2.5 collective-permute-start.27
  256.7 2.0 collective-permute-start.25
  258.7 5.0 %add_bitcast_fusion = f32[1,256,3072]{2,1,0:T(8,128)} fusion(bf16[256,3072]{1,0:T(8,128)(2,1)} %collective-permute-done.29, bf16[512,3072]{1,0:T(8,128)(2,1)} %bitcast.13, bf16[512,512]{1,0:T(8,128)(2,1)S(1)} %copy-done.18), kind=kOutput, calls=%fused_computation.6 | convolution fusion | flops 806879232 | bytes 8126464 | tf_op jit(solution)/shard_map/dot_general | solution.py:272
  263.7 1.2 collective-permute-start.20
  264.9 0.7 copy.45
  266.1 3.5 %collective-permute-start.18 = (bf16[128,384]{1,0:T(8,128)(2,1)S(1)}, bf16[128,384]{1,0:T(8,128)(2,1)S(1)}, u32[]{:S(2)}, u32[]{:S(2)}) collective-permute-start(bf16[128,384]{1,0:T(8,128)(2,1)S(1)} %get-tuple-element.56), channel_id=1, source_target_pairs={{0,4},{2,6},{4,0},{6,2},{1,5},{3,7},{5,1},{7,3},{8,12},{10,14},{12... | collective-permute-start | bytes 294920 | tf_op jit(solution)/shard_map/ppermute | solution.py:32
  269.6 2.0 collective-permute-start.17
  271.9 3.5 %collective-permute-start.22 = (bf16[128,384]{1,0:T(8,128)(2,1)S(1)}, bf16[128,384]{1,0:T(8,128)(2,1)S(1)}, u32[]{:S(2)}, u32[]{:S(2)}) collective-permute-start(bf16[128,384]{1,0:T(8,128)(2,1)S(1)} %get-tuple-element.53), channel_id=1, source_target_pairs={{0,4},{2,6},{4,0},{6,2},{1,5},{3,7},{5,1},{7,3},{8,12},{10,14},{12... | collective-permute-start | bytes 294920 | tf_op jit(solution)/shard_map/ppermute | solution.py:32
  275.4 8.4 %collective-permute-done.19 = bf16[128,384]{1,0:T(8,128)(2,1)S(1)} collective-permute-done((bf16[128,384]{1,0:T(8,128)(2,1)S(1)}, bf16[128,384]{1,0:T(8,128)(2,1)S(1)}, u32[]{:S(2)}, u32[]{:S(2)}) %collective-permute-start.19) | collective-permute-done | bytes 98336 | tf_op jit(solution)/shard_map/ppermute | solution.py:32
  283.9 0.7 fusion.28
  284.6 1.8 collective-permute-done.23
  286.4 1.8 collective-permute-done.21
  288.2 0.8 fusion.24
  (95 shorter events, 3.2 us)
Async XLA Ops:
  0.6 10.4 %collective-permute-start = (bf16[128,384]{1,0:T(8,128)(2,1)}, bf16[128,384]{1,0:T(8,128)(2,1)S(1)}, u32[]{:S(2)}, u32[]{:S(2)}) collective-permute-start(bf16[128,384]{1,0:T(8,128)(2,1)} %refs_0_.2), channel_id=1, source_target_pairs={{0,2},{2,0},{4,6},{6,4},{1,3},{3,1},{5,7},{7,5},{8,10},{10,8},{12,... | collective-permute-start | bytes 294920 | tf_op jit(solution)/shard_map/ppermute | solution.py:32
  0.7 10.4 %collective-permute-start.1 = (bf16[128,384]{1,0:T(8,128)(2,1)}, bf16[128,384]{1,0:T(8,128)(2,1)S(1)}, u32[]{:S(2)}, u32[]{:S(2)}) collective-permute-start(bf16[128,384]{1,0:T(8,128)(2,1)} %refs_0_.2), channel_id=1, source_target_pairs={{0,4},{2,6},{4,0},{6,2},{1,5},{3,7},{5,1},{7,3},{8,12},{10,14},{12... | collective-permute-start | bytes 294920 | tf_op jit(solution)/shard_map/ppermute | solution.py:32
  7.0 10.1 %collective-permute-start.2 = (bf16[128,384]{1,0:T(8,128)(2,1)}, bf16[128,384]{1,0:T(8,128)(2,1)S(1)}, u32[]{:S(2)}, u32[]{:S(2)}) collective-permute-start(bf16[128,384]{1,0:T(8,128)(2,1)} %refs_0_.2), channel_id=1, source_target_pairs={{0,6},{2,4},{4,2},{6,0},{1,7},{3,5},{5,3},{7,1},{8,14},{10,12},{12... | collective-permute-start | bytes 294920 | tf_op jit(solution)/shard_map/ppermute | solution.py:32
  7.0 11.1 %collective-permute-start.3 = (bf16[128,384]{1,0:T(8,128)(2,1)}, bf16[128,384]{1,0:T(8,128)(2,1)S(1)}, u32[]{:S(2)}, u32[]{:S(2)}) collective-permute-start(bf16[128,384]{1,0:T(8,128)(2,1)} %refs_0_.2), channel_id=1, source_target_pairs={{0,1},{1,0},{2,3},{3,2},{4,5},{5,4},{6,7},{7,6},{8,9},{9,8},{10,11... | collective-permute-start | bytes 294920 | tf_op jit(solution)/shard_map/ppermute | solution.py:28
  11.0 7.1 %collective-permute-start.4 = (bf16[128,384]{1,0:T(8,128)(2,1)S(1)}, bf16[128,384]{1,0:T(8,128)(2,1)S(1)}, u32[]{:S(2)}, u32[]{:S(2)}) collective-permute-start(bf16[128,384]{1,0:T(8,128)(2,1)S(1)} %collective-permute-done.refs_1_), channel_id=1, source_target_pairs={{0,1},{1,0},{2,3},{3,2},{4,5},{5,4},{6,7},{7,6},{8,9},{9,8},{10,11... | collective-permute-start | bytes 294920 | tf_op jit(solution)/shard_map/ppermute | solution.py:28
  11.2 7.0 %collective-permute-start.5 = (bf16[128,384]{1,0:T(8,128)(2,1)S(1)}, bf16[128,384]{1,0:T(8,128)(2,1)S(1)}, u32[]{:S(2)}, u32[]{:S(2)}) collective-permute-start(bf16[128,384]{1,0:T(8,128)(2,1)S(1)} %collective-permute-done.1.refs_2_), channel_id=1, source_target_pairs={{0,1},{1,0},{2,3},{3,2},{4,5},{5,4},{6,7},{7,6},{8,9},{9,8},{10,11... | collective-permute-start | bytes 294920 | tf_op jit(solution)/shard_map/ppermute | solution.py:28
  17.1 1.9 collective-permute-start.6
  19.0 0.9 copy-start.8
  25.8 0.9 copy-start.2
  26.7 7.3 %copy-start.13 = (bf16[128,384]{1,0:T(8,128)(2,1)S(1)}, bf16[128,384]{1,0:T(8,128)(2,1)}, u32[]{:S(2)}) copy-start(bf16[128,384]{1,0:T(8,128)(2,1)} %refs_0_.3) | copy-start | bytes 294916
  26.7 55.6 %copy-start.10 = (f32[128,4]{0,1:T(4,128)S(1)}, f32[128,4]{0,1:T(4,128)}, u32[]{:S(2)}) copy-start(f32[128,4]{0,1:T(4,128)} %param.13) | copy-start | bytes 6148
  26.7 60.8 %all-to-all-start = ((bf16[32,16,3072]{2,1,0:T(8,128)(2,1)}), bf16[32,16,3072]{2,1,0:T(8,128)(2,1)}, u32[]{:S(2)}, u32[]{:S(2)}) async-start(bf16[32,16,3072]{2,1,0:T(8,128)(2,1)} %bitcast.1), calls=%async_computation | async-start | bytes 6291456 | tf_op jit(solution)/shard_map/all_to_all | solution.py:243
  34.0 42.9 %collective-permute-start.9 = (bf16[128,384]{1,0:T(8,128)(2,1)S(1)}, bf16[128,384]{1,0:T(8,128)(2,1)S(1)}, u32[]{:S(2)}, u32[]{:S(2)}) collective-permute-start(bf16[128,384]{1,0:T(8,128)(2,1)S(1)} %copy-done.13), channel_id=1, source_target_pairs={{0,2},{2,0},{4,6},{6,4},{1,3},{3,1},{5,7},{7,5},{8,10},{10,8},{12,... | collective-permute-start | bytes 294920 | tf_op jit(solution)/shard_map/ppermute | solution.py:32
  35.4 45.5 %collective-permute-start.10 = (bf16[128,384]{1,0:T(8,128)(2,1)S(1)}, bf16[128,384]{1,0:T(8,128)(2,1)S(1)}, u32[]{:S(2)}, u32[]{:S(2)}) collective-permute-start(bf16[128,384]{1,0:T(8,128)(2,1)S(1)} %copy-done.13), channel_id=1, source_target_pairs={{0,4},{2,6},{4,0},{6,2},{1,5},{3,7},{5,1},{7,3},{8,12},{10,14},{12... | collective-permute-start | bytes 294920 | tf_op jit(solution)/shard_map/ppermute | solution.py:32
  39.7 41.3 %collective-permute-start.11 = (bf16[128,384]{1,0:T(8,128)(2,1)S(1)}, bf16[128,384]{1,0:T(8,128)(2,1)S(1)}, u32[]{:S(2)}, u32[]{:S(2)}) collective-permute-start(bf16[128,384]{1,0:T(8,128)(2,1)S(1)} %copy-done.13), channel_id=1, source_target_pairs={{0,6},{2,4},{4,2},{6,0},{1,7},{3,5},{5,3},{7,1},{8,14},{10,12},{12... | collective-permute-start | bytes 294920 | tf_op jit(solution)/shard_map/ppermute | solution.py:32
  39.7 41.6 %collective-permute-start.12 = (bf16[128,384]{1,0:T(8,128)(2,1)S(1)}, bf16[128,384]{1,0:T(8,128)(2,1)S(1)}, u32[]{:S(2)}, u32[]{:S(2)}) collective-permute-start(bf16[128,384]{1,0:T(8,128)(2,1)S(1)} %copy-done.13), channel_id=1, source_target_pairs={{0,1},{1,0},{2,3},{3,2},{4,5},{5,4},{6,7},{7,6},{8,9},{9,8},{10,11... | collective-permute-start | bytes 294920 | tf_op jit(solution)/shard_map/ppermute | solution.py:28
  76.9 4.9 %collective-permute-start.13 = (bf16[128,384]{1,0:T(8,128)(2,1)S(1)}, bf16[128,384]{1,0:T(8,128)(2,1)S(1)}, u32[]{:S(2)}, u32[]{:S(2)}) collective-permute-start(bf16[128,384]{1,0:T(8,128)(2,1)S(1)} %collective-permute-done.9.refs_1_), channel_id=1, source_target_pairs={{0,1},{1,0},{2,3},{3,2},{4,5},{5,4},{6,7},{7,6},{8,9},{9,8},{10,11... | collective-permute-start | bytes 294920 | tf_op jit(solution)/shard_map/ppermute | solution.py:28
  80.9 1.3 collective-permute-start.14
  80.9 1.4 collective-permute-start.15
  87.5 0.9 copy-start.14
  87.5 12.9 %copy-start.21 = (bf16[1,256,3072]{2,1,0:T(8,128)(2,1)S(1)}, bf16[1,256,3072]{2,1,0:T(8,128)(2,1)}, u32[]{:S(2)}) copy-start(bf16[1,256,3072]{2,1,0:T(8,128)(2,1)} %param.15) | copy-start | bytes 4718596
  88.4 51.9 %all-to-all-start.2 = ((bf16[32,16,3072]{2,1,0:T(8,128)(2,1)}), bf16[32,16,3072]{2,1,0:T(8,128)(2,1)}, u32[]{:S(2)}, u32[]{:S(2)}) async-start(bf16[32,16,3072]{2,1,0:T(8,128)(2,1)} %bitcast.12), calls=%async_computation.2 | async-start | bytes 6291456 | tf_op jit(solution)/shard_map/all_to_all | solution.py:252
  99.5 5.3 %collective-permute-start.7 = (bf16[3072,256]{1,0:T(8,128)(2,1)}, bf16[3072,256]{1,0:T(8,128)(2,1)S(1)}, u32[]{:S(2)}, u32[]{:S(2)}) collective-permute-start(bf16[3072,256]{1,0:T(8,128)(2,1)} %bitcast.74), channel_id=1, source_target_pairs={{0,1},{1,0},{2,3},{3,2},{4,5},{5,4},{6,7},{7,6},{8,9},{9,8},{10,11... | collective-permute-start | bytes 4718600 | tf_op jit(solution)/shard_map/ppermute | solution.py:28
  100.4 10.1 %collective-permute-start.8 = (bf16[256,3072]{1,0:T(8,128)(2,1)S(1)}, bf16[256,3072]{1,0:T(8,128)(2,1)S(1)}, u32[]{:S(2)}, u32[]{:S(2)}) collective-permute-start(bf16[256,3072]{1,0:T(8,128)(2,1)S(1)} %bitcast.72), channel_id=1, source_target_pairs={{0,1},{1,0},{2,3},{3,2},{4,5},{5,4},{6,7},{7,6},{8,9},{9,8},{10,11... | collective-permute-start | bytes 4718600 | tf_op jit(solution)/shard_map/ppermute | solution.py:28
  104.7 5.7 %copy-start.23 = (bf16[3072,256]{1,0:T(8,128)(2,1)}, bf16[3072,256]{1,0:T(8,128)(2,1)S(1)}, u32[]{:S(2)}) copy-start(bf16[3072,256]{1,0:T(8,128)(2,1)S(1)} %collective-permute-done.7) | copy-start | bytes 4718596
  110.4 0.8 copy-start.16
  110.4 1.4 copy-start.25
  140.3 48.1 %all-to-all-start.1 = ((bf16[32,16,3072]{2,1,0:T(8,128)(2,1)}), bf16[32,16,3072]{2,1,0:T(8,128)(2,1)S(1)}, u32[]{:S(2)}, u32[]{:S(2)}) async-start(bf16[32,16,3072]{2,1,0:T(8,128)(2,1)} %bitcast.69), calls=%async_computation.1 | async-start | bytes 6291456 | tf_op jit(solution)/shard_map/all_to_all | solution.py:261
  148.3 6.1 %copy-start.22 = (bf16[1,3072,256]{2,1,0:T(8,128)(2,1)S(1)}, bf16[1,3072,256]{2,1,0:T(8,128)(2,1)}, u32[]{:S(2)}) copy-start(bf16[1,3072,256]{2,1,0:T(8,128)(2,1)} %param.14) | copy-start | bytes 4718596
  148.3 6.1 %copy-start.24 = (bf16[3072,256]{1,0:T(8,128)(2,1)S(1)}, bf16[3072,256]{1,0:T(8,128)(2,1)}, u32[]{:S(2)}) copy-start(bf16[3072,256]{1,0:T(8,128)(2,1)} %copy-done.23) | copy-start | bytes 4718596
  153.6 0.8 copy-start.26
  188.4 1.7 copy-start
  190.1 47.7 %all-to-all-start.3 = ((bf16[32,16,3072]{2,1,0:T(8,128)(2,1)}), bf16[32,16,3072]{2,1,0:T(8,128)(2,1)S(1)}, u32[]{:S(2)}, u32[]{:S(2)}) async-start(bf16[32,16,3072]{2,1,0:T(8,128)(2,1)} %bitcast.68), calls=%async_computation.3 | async-start | bytes 6291456 | tf_op jit(solution)/shard_map/all_to_all | solution.py:267
  198.2 5.2 %copy-start.17 = (bf16[512,512]{1,0:T(8,128)(2,1)S(1)}, bf16[512,512]{1,0:T(8,128)(2,1)}, u32[]{:S(2)}) copy-start(bf16[512,512]{1,0:T(8,128)(2,1)} %copy-done.16) | copy-start | bytes 1572868
  202.4 45.2 %collective-permute-start.28 = (bf16[3072,256]{1,0:T(8,128)(2,1)}, bf16[3072,256]{1,0:T(8,128)(2,1)}, u32[]{:S(2)}, u32[]{:S(2)}) collective-permute-start(bf16[3072,256]{1,0:T(8,128)(2,1)} %convolution_convert_fusion.3), channel_id=1, source_target_pairs={{0,1},{1,0},{2,3},{3,2},{4,5},{5,4},{6,7},{7,6},{8,9},{9,8},{10,11... | collective-permute-start | bytes 4718600 | tf_op jit(solution)/shard_map/ppermute | solution.py:28
  207.5 51.2 %collective-permute-start.29 = (bf16[256,3072]{1,0:T(8,128)(2,1)}, bf16[256,3072]{1,0:T(8,128)(2,1)}, u32[]{:S(2)}, u32[]{:S(2)}) collective-permute-start(bf16[256,3072]{1,0:T(8,128)(2,1)} %convolution_convert_fusion.2), channel_id=1, source_target_pairs={{0,1},{1,0},{2,3},{3,2},{4,5},{5,4},{6,7},{7,6},{8,9},{9,8},{10,11... | collective-permute-start | bytes 4718600 | tf_op jit(solution)/shard_map/ppermute | solution.py:28
  207.7 1.9 copy-start.1
  209.6 1.1 copy-start.15
  217.3 0.7 copy-start.6
  218.1 0.7 copy-start.11
  237.7 1.1 copy-start.3
  238.9 8.8 %copy-start.27 = (bf16[512,512]{1,0:T(8,128)(2,1)S(1)}, bf16[512,512]{1,0:T(8,128)(2,1)}, u32[]{:S(2)}) copy-start(bf16[512,512]{1,0:T(8,128)(2,1)} %copy-done.26) | copy-start | bytes 1572868
  244.4 8.2 %copy-start.4 = (bf16[4,128,384]{2,1,0:T(8,128)(2,1)}, bf16[4,128,384]{2,1,0:T(8,128)(2,1)S(1)}, u32[]{:S(2)}) copy-start(bf16[4,128,384]{2,1,0:T(8,128)(2,1)S(1)} %get-tuple-element.24) | copy-start | bytes 1179652
  244.4 8.2 %copy-start.12 = (bf16[4,128,384]{2,1,0:T(8,128)(2,1)S(1)}, bf16[4,128,384]{2,1,0:T(8,128)(2,1)}, u32[]{:S(2)}) copy-start(bf16[4,128,384]{2,1,0:T(8,128)(2,1)} %copy-done.11) | copy-start | bytes 1179652
  244.4 14.2 %copy-start.18 = (bf16[512,512]{1,0:T(8,128)(2,1)S(1)}, bf16[512,512]{1,0:T(8,128)(2,1)}, u32[]{:S(2)}) copy-start(bf16[512,512]{1,0:T(8,128)(2,1)} %copy-done.16) | copy-start | bytes 1572868
  244.4 8.4 %collective-permute-start.24 = (f32[128,128]{1,0:T(8,128)S(1)}, f32[128,128]{1,0:T(8,128)S(1)}, u32[]{:S(2)}, u32[]{:S(2)}) collective-permute-start(f32[128,128]{1,0:T(8,128)S(1)} %get-tuple-element.26), channel_id=1, source_target_pairs={{0,1},{1,0},{2,3},{3,2},{4,5},{5,4},{6,7},{7,6},{8,9},{9,8},{10,11... | collective-permute-start | bytes 196616 | tf_op jit(solution)/shard_map/ppermute | solution.py:28
  252.7 13.1 %collective-permute-start.16 = (bf16[4,128,384]{2,1,0:T(8,128)(2,1)S(1)}, bf16[4,128,384]{2,1,0:T(8,128)(2,1)S(1)}, u32[]{:S(2)}, u32[]{:S(2)}) collective-permute-start(bf16[4,128,384]{2,1,0:T(8,128)(2,1)S(1)} %copy-done.12), channel_id=1, source_target_pairs={{0,1},{1,0},{2,3},{3,2},{4,5},{5,4},{6,7},{7,6},{8,9},{9,8},{10,11... | collective-permute-start | bytes 1179656 | tf_op jit(solution)/shard_map/ppermute | solution.py:28
  252.9 12.9 %copy-start.7 = (bf16[4,128,384]{2,1,0:T(8,128)(2,1)S(1)}, bf16[4,128,384]{2,1,0:T(8,128)(2,1)}, u32[]{:S(2)}) copy-start(bf16[4,128,384]{2,1,0:T(8,128)(2,1)} %copy-done.6) | copy-start | bytes 1179652
  252.9 18.7 %copy-start.5 = (bf16[4,128,384]{2,1,0:T(8,128)(2,1)S(1)}, bf16[4,128,384]{2,1,0:T(8,128)(2,1)}, u32[]{:S(2)}) copy-start(bf16[4,128,384]{2,1,0:T(8,128)(2,1)} %copy-done.4) | copy-start | bytes 1179652
  252.9 31.0 %copy-start.20 = (bf16[128,384]{1,0:T(8,128)(2,1)S(1)}, bf16[128,384]{1,0:T(8,128)(2,1)}, u32[]{:S(2)}) copy-start(bf16[128,384]{1,0:T(8,128)(2,1)} %param.9) | copy-start | bytes 294916
  252.9 35.3 %copy-start.9 = (bf16[128,384]{1,0:T(8,128)(2,1)S(1)}, bf16[128,384]{1,0:T(8,128)(2,1)}, u32[]{:S(2)}) copy-start(bf16[128,384]{1,0:T(8,128)(2,1)} %refs_0_.2) | copy-start | bytes 294916
  252.9 35.3 %copy-start.19 = (bf16[128,384]{1,0:T(8,128)(2,1)S(1)}, bf16[128,384]{1,0:T(8,128)(2,1)}, u32[]{:S(2)}) copy-start(bf16[128,384]{1,0:T(8,128)(2,1)} %param.10) | copy-start | bytes 294916
  252.9 12.0 %collective-permute-start.26 = (f32[128,128]{1,0:T(8,128)S(1)}, f32[128,128]{1,0:T(8,128)S(1)}, u32[]{:S(2)}, u32[]{:S(2)}) collective-permute-start(f32[128,128]{1,0:T(8,128)S(1)} %add.137), channel_id=1, source_target_pairs={{0,4},{2,6},{4,0},{6,2},{1,5},{3,7},{5,1},{7,3},{8,12},{10,14},{12... | collective-permute-start | bytes 196616 | tf_op jit(solution)/shard_map/ppermute | solution.py:32
  254.2 10.7 %collective-permute-start.27 = (f32[128,128]{1,0:T(8,128)S(1)}, f32[128,128]{1,0:T(8,128)S(1)}, u32[]{:S(2)}, u32[]{:S(2)}) collective-permute-start(f32[128,128]{1,0:T(8,128)S(1)} %add.137), channel_id=1, source_target_pairs={{0,6},{2,4},{4,2},{6,0},{1,7},{3,5},{5,3},{7,1},{8,14},{10,12},{12... | collective-permute-start | bytes 196616 | tf_op jit(solution)/shard_map/ppermute | solution.py:32
  256.7 8.2 %collective-permute-start.25 = (f32[128,128]{1,0:T(8,128)S(1)}, f32[128,128]{1,0:T(8,128)S(1)}, u32[]{:S(2)}, u32[]{:S(2)}) collective-permute-start(f32[128,128]{1,0:T(8,128)S(1)} %add.137), channel_id=1, source_target_pairs={{0,2},{2,0},{4,6},{6,4},{1,3},{3,1},{5,7},{7,5},{8,10},{10,8},{12,... | collective-permute-start | bytes 196616 | tf_op jit(solution)/shard_map/ppermute | solution.py:32
  263.7 7.9 %collective-permute-start.20 = (bf16[4,128,384]{2,1,0:T(8,128)(2,1)}, bf16[4,128,384]{2,1,0:T(8,128)(2,1)S(1)}, u32[]{:S(2)}, u32[]{:S(2)}) collective-permute-start(bf16[4,128,384]{2,1,0:T(8,128)(2,1)} %get-tuple-element.25), channel_id=1, source_target_pairs={{0,1},{1,0},{2,3},{3,2},{4,5},{5,4},{6,7},{7,6},{8,9},{9,8},{10,11... | collective-permute-start | bytes 1179656 | tf_op jit(solution)/shard_map/ppermute | solution.py:28
  265.9 18.0 %collective-permute-start.19 = (bf16[128,384]{1,0:T(8,128)(2,1)S(1)}, bf16[128,384]{1,0:T(8,128)(2,1)S(1)}, u32[]{:S(2)}, u32[]{:S(2)}) collective-permute-start(bf16[128,384]{1,0:T(8,128)(2,1)S(1)} %get-tuple-element.55), channel_id=1, source_target_pairs={{0,6},{2,4},{4,2},{6,0},{1,7},{3,5},{5,3},{7,1},{8,14},{10,12},{12... | collective-permute-start | bytes 294920 | tf_op jit(solution)/shard_map/ppermute | solution.py:32
  266.1 17.7 %collective-permute-start.18 = (bf16[128,384]{1,0:T(8,128)(2,1)S(1)}, bf16[128,384]{1,0:T(8,128)(2,1)S(1)}, u32[]{:S(2)}, u32[]{:S(2)}) collective-permute-start(bf16[128,384]{1,0:T(8,128)(2,1)S(1)} %get-tuple-element.56), channel_id=1, source_target_pairs={{0,4},{2,6},{4,0},{6,2},{1,5},{3,7},{5,1},{7,3},{8,12},{10,14},{12... | collective-permute-start | bytes 294920 | tf_op jit(solution)/shard_map/ppermute | solution.py:32
  269.6 14.2 %collective-permute-start.17 = (bf16[128,384]{1,0:T(8,128)(2,1)S(1)}, bf16[128,384]{1,0:T(8,128)(2,1)S(1)}, u32[]{:S(2)}, u32[]{:S(2)}) collective-permute-start(bf16[128,384]{1,0:T(8,128)(2,1)S(1)} %get-tuple-element.54), channel_id=1, source_target_pairs={{0,2},{2,0},{4,6},{6,4},{1,3},{3,1},{5,7},{7,5},{8,10},{10,8},{12,... | collective-permute-start | bytes 294920 | tf_op jit(solution)/shard_map/ppermute | solution.py:32
  271.7 14.7 %collective-permute-start.23 = (bf16[128,384]{1,0:T(8,128)(2,1)S(1)}, bf16[128,384]{1,0:T(8,128)(2,1)S(1)}, u32[]{:S(2)}, u32[]{:S(2)}) collective-permute-start(bf16[128,384]{1,0:T(8,128)(2,1)S(1)} %get-tuple-element.52), channel_id=1, source_target_pairs={{0,6},{2,4},{4,2},{6,0},{1,7},{3,5},{5,3},{7,1},{8,14},{10,12},{12... | collective-permute-start | bytes 294920 | tf_op jit(solution)/shard_map/ppermute | solution.py:32
  271.9 14.4 %collective-permute-start.22 = (bf16[128,384]{1,0:T(8,128)(2,1)S(1)}, bf16[128,384]{1,0:T(8,128)(2,1)S(1)}, u32[]{:S(2)}, u32[]{:S(2)}) collective-permute-start(bf16[128,384]{1,0:T(8,128)(2,1)S(1)} %get-tuple-element.53), channel_id=1, source_target_pairs={{0,4},{2,6},{4,0},{6,2},{1,5},{3,7},{5,1},{7,3},{8,12},{10,14},{12... | collective-permute-start | bytes 294920 | tf_op jit(solution)/shard_map/ppermute | solution.py:32
  283.8 4.4 %collective-permute-start.21 = (bf16[128,384]{1,0:T(8,128)(2,1)S(1)}, bf16[128,384]{1,0:T(8,128)(2,1)S(1)}, u32[]{:S(2)}, u32[]{:S(2)}) collective-permute-start(bf16[128,384]{1,0:T(8,128)(2,1)S(1)} %get-tuple-element.51), channel_id=1, source_target_pairs={{0,2},{2,0},{4,6},{6,4},{1,3},{3,1},{5,7},{7,5},{8,10},{10,8},{12,... | collective-permute-start | bytes 294920 | tf_op jit(solution)/shard_map/ppermute | solution.py:32

commit v2 on v1

--- a/solution.py
+++ b/solution.py
@@ -32,8 +32,12 @@
     return lax.ppermute(v, "zh", [(i, i ^ r) for i in range(4)])
 
 
+def gather_chips(v):
+    return [v] + [swap_chips(v, r) for r in (1, 2, 3)]
+
+
 def gather_features(v):
-    mine = [v] + [swap_chips(v, r) for r in (1, 2, 3)]
+    mine = gather_chips(v)
     return mine + [swap_cores(m) for m in mine]
 
 
@@ -46,9 +50,17 @@
     return hit
 
 
+def columns_of(core, mine, other):
+    first = core == 0
+    left = jnp.where(first, mine, other)
+    right = jnp.where(first, other, mine)
+    return jnp.concatenate([left, right], axis=1)
+
+
 def pack_first_kernel(order, qt_ref, *refs):
     parts, (out_ref, full_ref, stats_ref, low, pick) = refs[:8], refs[8:]
     step = pl.program_id(0)
+    core = order[4]
 
     @pl.when(step == 0)
     def _():
@@ -59,17 +71,18 @@
             jnp.sum(jnp.square(p[...].astype(F32) - mean), axis=1, keepdims=True) for p in parts
         )
         rstd = lax.rsqrt(square / width + 1e-05)
-        for i, p in enumerate(parts):
-            low[i] = ((p[...].astype(F32) - mean) * rstd).astype(BF16)
+        for i in range(4):
+            both = columns_of(core, parts[i][...].astype(F32), parts[4 + i][...].astype(F32))
+            low[i] = ((both - mean) * rstd).astype(BF16)
         lane = lax.broadcasted_iota(jnp.int32, stats_ref.shape, 1)
         stats_ref[...] = jnp.where(lane == 0, mean, rstd)
         pick[...] = jnp.where(select_rows(qt_ref[...], pick.shape[0]), 1.0, 0.0).astype(BF16)
 
-    for i, p in enumerate(parts):
+    for i in range(4):
 
         @pl.when(step == i)
-        def _(p=p):
-            full_ref[...] = p[...]
+        def _(i=i):
+            full_ref[...] = columns_of(core, parts[i][...].astype(F32), parts[4 + i][...].astype(F32)).astype(BF16)
 
     out_ref[...] = jnp.dot(pick[...], low[step], preferred_element_type=F32).astype(BF16)
 
@@ -77,6 +90,7 @@
 def pack_grad_kernel(order, qt_ref, gt_ref, *refs):
     parts, (out_ref, full_ref, pick, gate) = refs[:8], refs[8:]
     step = pl.program_id(0)
+    core = order[4]
 
     @pl.when(step == 0)
     def _():
@@ -89,27 +103,20 @@
             weight = weight + jnp.where(at == qt[k : k + 1, :], gt[k : k + 1, :], 0.0)
         gate[...] = jnp.sum(weight, axis=1, keepdims=True)
 
-    for i, p in enumerate(parts):
+    for i in range(4):
 
         @pl.when(step == i)
-        def _(p=p):
-            full_ref[...] = p[...]
-            rows = jnp.dot(pick[...], p[...], preferred_element_type=F32)
+        def _(i=i):
+            both = columns_of(core, parts[i][...].astype(F32), parts[4 + i][...].astype(F32)).astype(BF16)
+            full_ref[...] = both
+            rows = jnp.dot(pick[...], both, preferred_element_type=F32)
             out_ref[...] = (gate[...] * rows).astype(BF16)
-
-
-def store_parts(step, value, keep_ref, give_ref):
-    @pl.when(step < 4)
-    def _():
-        keep_ref[0] = value.astype(BF16)
-
-    @pl.when(step >= 4)
-    def _():
-        give_ref[0] = value.astype(BF16)
 
 
 def combine_out_kernel(order, q_ref, g_ref, rows_ref, full_ref, keep_ref, give_ref, inner_ref, high, rest, inner):
     step = pl.program_id(0)
+    part = keep_ref.shape[2]
+    first = order[4] == 0
 
     @pl.when(step == 0)
     def _():
@@ -126,15 +133,17 @@
     value = jnp.dot(high[...], rows, preferred_element_type=F32) + jnp.dot(
         rest[...], rows, preferred_element_type=F32
     )
-    store_parts(step, value, keep_ref, give_ref)
+    left, right = value[:, :part], value[:, part:]
+    keep_ref[0] = jnp.where(first, left, right).astype(BF16)
+    give_ref[0] = jnp.where(first, right, left).astype(BF16)
     inner[...] += lax.dot_general(
         full_ref[...], rows, (((1,), (1,)), ((), ())), preferred_element_type=F32
     )
 
-    @pl.when(step == 7)
+    @pl.when(step == 3)
     def _():
         lane = lax.broadcasted_iota(jnp.int32, inner.shape, 1)
-        place = lax.broadcasted_iota(jnp.int32, inner_ref.shape, 1)
+        place = lax.broadcasted_iota(jnp.int32, inner_ref.shape, 1) % 8
         found = jnp.zeros(inner_ref.shape, F32)
         for k in range(q_ref.shape[1]):
             one = jnp.sum(
@@ -146,6 +155,8 @@
 
 def combine_dx_kernel(order, q_ref, inner_ref, stats_ref, rows_ref, full_ref, keep_ref, give_ref, sums_ref, pick, sums):
     step = pl.program_id(0)
+    part = keep_ref.shape[2]
+    first = order[4] == 0
 
     @pl.when(step == 0)
     def _():
@@ -154,38 +165,57 @@
         for k in range(1, q_ref.shape[1]):
             hit = jnp.logical_or(hit, lane == q_ref[:, k : k + 1])
         pick[...] = jnp.where(hit, 1.0, 0.0).astype(BF16)
-        sums[...] = jnp.zeros_like(sums)
+        sums[...] = inner_ref[...]
 
     value = jnp.dot(pick[...], rows_ref[...], preferred_element_type=F32)
-    store_parts(step, value, keep_ref, give_ref)
+    left, right = value[:, :part], value[:, part:]
+    keep_ref[0] = jnp.where(first, left, right).astype(BF16)
+    give_ref[0] = jnp.where(first, right, left).astype(BF16)
     normed = (full_ref[...].astype(F32) - stats_ref[:, 0:1]) * stats_ref[:, 1:2]
-    place = lax.broadcasted_iota(jnp.int32, sums.shape, 1)
+    lane = lax.broadcasted_iota(jnp.int32, sums.shape, 1)
+    place = lane % 8
     plain = jnp.sum(value, axis=1, keepdims=True)
     mixed = jnp.sum(value * normed, axis=1, keepdims=True)
     sums[...] += jnp.where(place == 4, plain, 0.0) + jnp.where(place == 5, mixed, 0.0)
 
-    @pl.when(step == 7)
-    def _():
-        sums_ref[...] = sums[...] + inner_ref[...]
+    @pl.when(step == 3)
+    def _():
+        all_sums = sums[...]
+        high = all_sums.astype(BF16).astype(F32)
+        middle = (all_sums - high).astype(BF16).astype(F32)
+        lowest = all_sums - high - middle
+        sums_ref[...] = jnp.where(lane < 8, high, jnp.where(lane < 16, middle, lowest)).astype(BF16)
+
+
+def join_thirds(v):
+    v = v.astype(F32)
+    return (v[:, 0:8] + v[:, 8:16]) + v[:, 16:24]
+
+
+def split_thirds(v):
+    high = lax.reduce_precision(v, 8, 7)
+    middle = lax.reduce_precision(v - high, 8, 7)
+    lowest = v - high - middle
+    return jnp.pad(jnp.concatenate([high, middle, lowest], axis=1).astype(BF16), ((0, 0), (0, 104)))
 
 
 def whole(shape):
     return pl.BlockSpec(shape, lambda i, order: (0,) * len(shape))
 
 
-def run(kernel, order, args, in_specs, out_shape, out_specs, scratch, flops, moved):
+def run(kernel, order, args, in_specs, out_shape, out_specs, scratch, flops, moved, limit=None):
     return pl.pallas_call(
         kernel,
         grid_spec=pltpu.PrefetchScalarGridSpec(
             num_scalar_prefetch=1,
-            grid=(8,),
+            grid=(4,),
             in_specs=in_specs,
             out_specs=out_specs,
             scratch_shapes=scratch,
         ),
         out_shape=out_shape,
         compiler_params=pltpu.CompilerParams(
-            dimension_semantics=("arbitrary",), vmem_limit_bytes=24 * 2**20
+            dimension_semantics=("arbitrary",), vmem_limit_bytes=limit
         ),
         cost_estimate=pl.CostEstimate(flops=flops, bytes_accessed=moved, transcendentals=0),
     )(order, *args)
@@ -212,17 +242,14 @@
     q = jnp.where(rank % 2 == core, expert_ids * half + rank // 2, -1)
     qt = q.T
     gt = gate_probs.T
-    lanes = jnp.arange(4, dtype=jnp.int32)
-    columns = (jnp.bitwise_xor(zh, lanes)) * 2
-    order = jnp.concatenate([columns + core, columns + (1 - core)]).astype(jnp.int32)
+    order = jnp.append(jnp.bitwise_xor(zh, jnp.arange(4, dtype=jnp.int32)), core).astype(jnp.int32)
 
     first_parts = gather_features(stream_first)
-    second_parts = gather_features(grad_second)
-
-    block = pl.BlockSpec((slots, part), lambda i, order: (0, order[i]))
-    token_block = pl.BlockSpec((tokens, part), lambda i, order: (0, order[i]))
-    keep_spec = pl.BlockSpec((1, tokens, part), lambda i, order: (jnp.minimum(i, 3), 0, 0))
-    give_spec = pl.BlockSpec((1, tokens, part), lambda i, order: (jnp.maximum(i - 4, 0), 0, 0))
+    second_parts = gather_chips(grad_second)
+
+    block = pl.BlockSpec((slots, 2 * part), lambda i, order: (0, order[i]))
+    token_block = pl.BlockSpec((tokens, 2 * part), lambda i, order: (0, order[i]))
+    step_block = pl.BlockSpec((1, tokens, part), lambda i, order: (i, 0, 0))
     rows_shape = jax.ShapeDtypeStruct((slots, width), BF16)
     full_shape = jax.ShapeDtypeStruct((tokens, width), BF16)
     lane_shape = jax.ShapeDtypeStruct((tokens, 128), F32)
@@ -234,20 +261,22 @@
         [whole((topk, tokens))] + [whole((tokens, part))] * 8,
         (rows_shape, full_shape, lane_shape),
         (block, token_block, whole((tokens, 128))),
-        [pltpu.VMEM((8, tokens, part), BF16), pltpu.VMEM((slots, tokens), BF16)],
-        pick_flops, 2 * slots * width,
+        [pltpu.VMEM((4, tokens, 2 * part), BF16), pltpu.VMEM((slots, tokens), BF16)],
+        pick_flops, 2 * slots * width, 24 * 2**20,
     )
     send = functools.partial(
         lax.all_to_all, axis_name=CTX, split_axis=0, concat_axis=0, tiled=True
     )
+    rows, *second_parts = lax.optimization_barrier((rows, *second_parts))
     x = send(rows)
+    second_parts = second_parts + [swap_cores(p) for p in second_parts]
     grad_rows, second_full = run(
         pack_grad_kernel, order, (qt, gt, *second_parts),
         [whole((topk, tokens))] * 2 + [whole((tokens, part))] * 8,
         (rows_shape, full_shape),
         (block, token_block),
         [pltpu.VMEM((slots, tokens), BF16), pltpu.VMEM((slots, 1), F32)],
-        pick_flops, 2 * slots * width,
+        pick_flops, 2 * slots * width, 24 * 2**20,
     )
     g = send(grad_rows)
 
@@ -265,6 +294,17 @@
         grad_pre, wi, (((1,), (1,)), ((), ())), preferred_element_type=F32
     ).astype(BF16)
     back_dx = send(route_dx)
+
+    keep_out, give_out, inner = run(
+        combine_out_kernel, order, (q, gate_probs, back, second_full),
+        [whole((tokens, topk))] * 2 + [block, token_block],
+        (parts_shape, parts_shape, lane_shape),
+        (step_block, step_block, whole((tokens, 128))),
+        [pltpu.VMEM((tokens, slots), BF16)] * 2 + [pltpu.VMEM((tokens, slots), F32)],
+        3 * pick_flops, 2 * slots * width,
+    )
+    got_out = swap_cores(give_out)
+    half_out = [keep_out[r].astype(F32) + got_out[r].astype(F32) for r in range(4)]
 
     rows_rows = (((0,), (0,)), ((), ()))
     out_give = lax.dot_general(hidden[:, own:], g, rows_rows, preferred_element_type=F32).astype(BF16)
@@ -278,35 +318,34 @@
         x, grad_pre[:, :own], rows_rows, preferred_element_type=F32
     ) + in_got.astype(F32)
 
-    def reduce_parts(keep, give):
-        got = swap_cores(give)
-        half_sum = [(keep[r].astype(F32) + got[r].astype(F32)) for r in range(4)]
-        arrived = [swap_chips(half_sum[r].astype(BF16), r).astype(F32) for r in (1, 2, 3)]
-        return half_sum[0] + arrived[0] + arrived[1] + arrived[2]
-
-    keep, give, inner = run(
-        combine_out_kernel, order, (q, gate_probs, back, second_full),
-        [whole((tokens, topk))] * 2 + [block, token_block],
-        (parts_shape, parts_shape, lane_shape),
-        (keep_spec, give_spec, whole((tokens, 128))),
-        [pltpu.VMEM((tokens, slots), BF16)] * 2 + [pltpu.VMEM((tokens, slots), F32)],
-        3 * pick_flops, 2 * slots * width,
-    )
-    branch = reduce_parts(keep, give)
-    stream_input = (stream_second.astype(F32) - branch).astype(BF16)
-
+    back_dx, half_out, grad_w_in, grad_w_out = lax.optimization_barrier(
+        (back_dx, half_out, grad_w_in, grad_w_out)
+    )
     keep, give, sums = run(
         combine_dx_kernel, order, (q, inner, stats, back_dx, first_full),
         [whole((tokens, topk))] + [whole((tokens, 128))] * 2 + [block, token_block],
-        (parts_shape, parts_shape, lane_shape),
-        (keep_spec, give_spec, whole((tokens, 128))),
+        (parts_shape, parts_shape, jax.ShapeDtypeStruct((tokens, 128), BF16)),
+        (step_block, step_block, whole((tokens, 128))),
         [pltpu.VMEM((tokens, slots), BF16), pltpu.VMEM((tokens, 128), F32)],
-        pick_flops, 2 * slots * width,
-    )
-    sums = sums + swap_cores(sums)
-    s1, s2, s3 = [swap_chips(sums, r) for r in (1, 2, 3)]
+        pick_flops, 2 * slots * width, 24 * 2**20,
+    )
+    got, got_sums = swap_cores(give), swap_cores(sums)
+    half_sum = [keep[r].astype(F32) + got[r].astype(F32) for r in range(4)]
+    sums = join_thirds(sums) + join_thirds(got_sums)
+    thirds = split_thirds(sums)
+    others = [
+        swap_chips(
+            jnp.concatenate([half_sum[r].astype(BF16), half_out[r].astype(BF16), thirds], axis=1), r
+        )
+        for r in (1, 2, 3)
+    ]
+    s1, s2, s3 = [join_thirds(o[:, 2 * part :]) for o in others]
     sums = (sums + s1) + (s2 + s3)
-    grad_normed = reduce_parts(keep, give)
+    grad_normed, branch = half_sum[0], half_out[0]
+    for o in others:
+        grad_normed = grad_normed + o[:, :part].astype(F32)
+        branch = branch + o[:, part : 2 * part].astype(F32)
+    stream_input = (stream_second.astype(F32) - branch).astype(BF16)
     mean, rstd = stats[:, 0:1], stats[:, 1:2]
     normed = (stream_first.astype(F32) - mean) * rstd
     correction = grad_normed - sums[:, 4:5] / width - normed * (sums[:, 5:6] / width)

time: 293 us -> 263 us (0.90)
  starting transfers between devices: 79.1 us -> 65.6 us
  Pallas kernels: 23.1 us -> 17.4 us
  local copies, waits for them, and re-layouts: 13.5 us -> 7.98 us
  waiting for transfers between devices: 132 us -> 127 us
    all_to_all x1, waiting for transfers between devices: 0.01 us -> 34.7 us  [on_device(): x = send(rows)]
    ppermute x15 -> x9, waiting for transfers between devices: 51.3 us -> 18.1 us  [swap_chips(): return lax.ppermute(v, 'zh', [(i, i ^ r) for i in range(4)])]
    all_to_all x1, waiting for transfers between devices: 18.9 us -> 11.3 us  [on_device(): back_dx = send(route_dx)]
    ppermute x15 -> x9, starting transfers between devices: 27.3 us -> 21.1 us  [swap_chips(): return lax.ppermute(v, 'zh', [(i, i ^ r) for i in range(4)])]
    ppermute x15, starting transfers between devices: 17.2 us -> 11.3 us  [swap_cores(): return lax.ppermute(v, 'core', CORES)]
    pallas_call x4, Pallas kernels: 23.1 us -> 17.4 us  [run(): pl.pallas_call(kernel, grid_spec=pltpu.PrefetchScalarGridSpec(num_scalar_...]
    unnamed x58 -> x60, local copies, waits for them, and re-layouts: 13 us -> 7.45 us
    all_to_all x1, starting transfers between devices: 11.1 us -> 7.37 us  [on_device(): g = send(grad_rows)]
  transfers between devices with their start and end apart: 34 -> 28, of which waited for: 13 -> 16; matrix products, arithmetic and copies ran while one was open for 14% -> 15% of each run, Pallas kernels for 6% -> 6%
where the time goes in v2:
time: 263 us; the launch traced here: 260 us
  waiting for transfers between devices  127 us (48%)
  starting transfers between devices  65.6 us (25%)
  matrix products  34.1 us (13%)
  Pallas kernels  17.4 us (7%)
  local copies, waits for them, and re-layouts  7.98 us (3%)
  other arithmetic  6.26 us (2%)
    all_to_all x1, waiting for transfers between devices, on_device(): x = send(rows)  34.7 us
    all_to_all x1, waiting for transfers between devices, on_device(): back = send(result)  30.7 us
    all_to_all x1, waiting for transfers between devices, on_device(): g = send(grad_rows)  25.2 us
    ppermute x9, starting transfers between devices, swap_chips(): return lax.ppermute(v, 'zh', [(i, i ^ r) for i in range(4)])  21.1 us
    ppermute x9, waiting for transfers between devices, swap_chips(): return lax.ppermute(v, 'zh', [(i, i ^ r) for i in range(4)])  18.1 us
    pallas_call x4, Pallas kernels, run(): pl.pallas_call(kernel, grid_spec=pltpu.PrefetchScalarGridSpec(num_scalar_...  17.4 us
    all_to_all x1, waiting for transfers between devices, on_device(): back_dx = send(route_dx)  11.3 us
    ppermute x15, starting transfers between devices, swap_cores(): return lax.ppermute(v, 'core', CORES)  11.3 us
  transfers between devices with their start and end apart: 28, of which 16 were waited for; matrix products, arithmetic and copies ran while one was open for 15% of the time, Pallas kernels for 6%

profile of v2, /device:TPU:65, one launch (start us, length us, event | category | flops | bytes accessed | tf_op | source)
XLA Modules:
  0.0 259.6 jit_solution(8270206041548776062)
XLA Ops:
  0.7 6.3 %collective-permute-start.1 = (bf16[128,384]{1,0:T(8,128)(2,1)}, bf16[128,384]{1,0:T(8,128)(2,1)S(1)}, u32[]{:S(2)}, u32[]{:S(2)}) collective-permute-start(bf16[128,384]{1,0:T(8,128)(2,1)} %refs_0_.1), channel_id=1, source_target_pairs={{0,4},{2,6},{4,0},{6,2},{1,5},{3,7},{5,1},{7,3},{8,12},{10,14},{12... | collective-permute-start | bytes 294920 | tf_op jit(solution)/shard_map/ppermute | solution.py:32
  7.0 1.2 collective-permute-start.3
  8.2 1.2 collective-permute-start.7
  9.4 0.7 fusion.39
  10.1 0.2 fusion.40
  10.3 0.7 select_reduce_fusion
  11.3 0.7 multiply_add_fusion
  12.2 0.3 collective-permute-start.4
  12.6 5.5 %collective-permute-start.8 = (bf16[128,384]{1,0:T(8,128)(2,1)}, bf16[128,384]{1,0:T(8,128)(2,1)S(1)}, u32[]{:S(2)}, u32[]{:S(2)}) collective-permute-start(bf16[128,384]{1,0:T(8,128)(2,1)} %refs_0_.2), channel_id=1, source_target_pairs={{0,4},{2,6},{4,0},{6,2},{1,5},{3,7},{5,1},{7,3},{8,12},{10,14},{12... | collective-permute-start | bytes 294920 | tf_op jit(solution)/shard_map/ppermute | solution.py:32
  18.0 2.2 collective-permute-start.9
  20.2 0.4 collective-permute-start.5
  20.8 0.8 collective-permute-done.5.refs_6_
  21.6 0.4 collective-permute-done.6.refs_7_
  22.0 0.9 copy-done.5
  22.8 4.5 %shard_map.119 = (bf16[512,3072]{1,0:T(8,128)(2,1)}, bf16[128,3072]{1,0:T(8,128)(2,1)S(1)}, f32[128,128]{1,0:T(8,128)S(1)}) custom-call(s32[5]{0:T(128)S(1)} %pad_add_fusion.order, s32[4,128]{1,0:T(4,128)S(1)} %copy.56.qt_ref, bf16[128,384]{1,0:T(8,128)(2,1)S(1)} %copy-done.5, bf16[128,384]{1,0:T(8,128)(2,1)S(1)} %collective-permute-done.refs_1_, ...), custom_call_target="tpu_custom_call" | custom-call | flops 402653184 | bytes 3145728 | tf_op jit(solution)/shard_map/pallas_call | solution.py:207
  27.3 0.9 copy-done
  28.3 8.8 %all-to-all-start.1 = ((bf16[32,16,3072]{2,1,0:T(8,128)(2,1)}), bf16[32,16,3072]{2,1,0:T(8,128)(2,1)}, u32[]{:S(2)}, u32[]{:S(2)}) async-start(bf16[32,16,3072]{2,1,0:T(8,128)(2,1)} %bitcast.6), calls=%async_computation.1 | async-start | bytes 6291456 | tf_op jit(solution)/shard_map/all_to_all | solution.py:271
  37.1 0.5 collective-permute-start.10
  37.7 0.4 collective-permute-start.12
  38.2 0.3 collective-permute-done.10.refs_4_
  38.5 0.4 collective-permute-done.11.refs_5_
  39.1 0.4 collective-permute-done.13.refs_7_
  39.4 3.7 %shard_map.120 = (bf16[512,3072]{1,0:T(8,128)(2,1)}, bf16[128,3072]{1,0:T(8,128)(2,1)S(1)}) custom-call(s32[5]{0:T(128)S(1)} %pad_add_fusion.order, s32[4,128]{1,0:T(4,128)S(1)} %copy.56.qt_ref, f32[4,128]{1,0:T(4,128)S(1)} %bitcast.57, bf16[128,384]{1,0:T(8,128)(2,1)S(1)} %copy-done.11, bf16[128,384]{1,0:T(8,128)(2,1)S(1)} %collective-permute-done.7.refs_1_, ...), custom_call_target="tpu_custom_call" | custom-call | flops 402653184 | bytes 3145728 | tf_op jit(solution)/shard_map/pallas_call | solution.py:207
  43.1 0.9 copy-done.12
  44.0 34.7 %all-to-all-done.1 = bf16[32,16,3072]{2,1,0:T(8,128)(2,1)} async-done(((bf16[32,16,3072]{2,1,0:T(8,128)(2,1)}), bf16[32,16,3072]{2,1,0:T(8,128)(2,1)}, u32[]{:S(2)}, u32[]{:S(2)}) %all-to-all-start.1) | async-done | bytes 3145760 | tf_op jit(solution)/shard_map/all_to_all | solution.py:271
  78.6 7.4 %all-to-all-start = ((bf16[32,16,3072]{2,1,0:T(8,128)(2,1)}), bf16[32,16,3072]{2,1,0:T(8,128)(2,1)S(1)}, u32[]{:S(2)}, u32[]{:S(2)}) async-start(bf16[32,16,3072]{2,1,0:T(8,128)(2,1)} %bitcast.3), calls=%async_computation | async-start | bytes 6291456 | tf_op jit(solution)/shard_map/all_to_all | solution.py:281
  86.0 1.1 collective-permute-start.15
  87.2 3.1 %collective-permute-done.15 = bf16[3072,256]{1,0:T(8,128)(2,1)S(1)} collective-permute-done((bf16[3072,256]{1,0:T(8,128)(2,1)}, bf16[3072,256]{1,0:T(8,128)(2,1)S(1)}, u32[]{:S(2)}, u32[]{:S(2)}) %collective-permute-start.15) | collective-permute-done | bytes 1572896 | tf_op jit(solution)/shard_map/ppermute | solution.py:28
  90.4 5.8 %multiply_convert_fusion = (bf16[512,512]{1,0:T(8,128)(2,1)S(1)}, f32[512,512]{1,0:T(8,128)}) fusion(bf16[512,3072]{1,0:T(8,128)(2,1)} %bitcast.7, bf16[3072,256]{1,0:T(8,128)(2,1)S(1)} %collective-permute-done.15, bf16[3072,256]{1,0:T(8,128)(2,1)} %bitcast.70), kind=kOutput, calls=%fused_computation.17 | convolution fusion | flops 1618214912 | bytes 7864320 | tf_op jit(solution)/shard_map/dot_general | solution.py:287
  96.1 0.8 copy-done.15
  96.9 0.6 copy-done.28
  97.5 3.5 %convolution_convert_fusion = bf16[512,3072]{1,0:T(8,128)(2,1)} fusion(bf16[512,512]{1,0:T(8,128)(2,1)S(1)} %get-tuple-element.95, bf16[256,3072]{1,0:T(8,128)(2,1)S(1)} %collective-permute-done.14, bf16[256,3072]{1,0:T(8,128)(2,1)S(1)} %bitcast.68), kind=kOutput, calls=%fused_computation | convolution fusion | flops 1618477056 | bytes 6815744 | tf_op jit(solution)/shard_map/dot_general | solution.py:289
  101.0 25.2 %all-to-all-done = bf16[32,16,3072]{2,1,0:T(8,128)(2,1)S(1)} async-done(((bf16[32,16,3072]{2,1,0:T(8,128)(2,1)}), bf16[32,16,3072]{2,1,0:T(8,128)(2,1)S(1)}, u32[]{:S(2)}, u32[]{:S(2)}) %all-to-all-start) | async-done | bytes 3145760 | tf_op jit(solution)/shard_map/all_to_all | solution.py:281
  126.1 8.2 %all-to-all-start.3 = ((bf16[32,16,3072]{2,1,0:T(8,128)(2,1)}), bf16[32,16,3072]{2,1,0:T(8,128)(2,1)}, u32[]{:S(2)}, u32[]{:S(2)}) async-start(bf16[32,16,3072]{2,1,0:T(8,128)(2,1)} %bitcast.63), calls=%async_computation.3 | async-start | bytes 6291456 | tf_op jit(solution)/shard_map/all_to_all | solution.py:290
  134.3 4.5 %fusion.3 = bf16[512,512]{1,0:T(8,128)(2,1)S(1)} fusion(bf16[512,3072]{1,0:T(8,128)(2,1)S(1)} %bitcast.58, bf16[256,3072]{1,0:T(8,128)(2,1)} %copy-done.28, bf16[256,3072]{1,0:T(8,128)(2,1)} %bitcast.67, f32[512,512]{1,0:T(8,128)} %get-tuple-element.96), kind=kOutput, calls=%fused_computation.12 | convolution fusion | flops 1619525632 | bytes 7864320 | tf_op jit(solution)/shard_map/dot_general | solution.py:291
  138.9 0.8 copy-done.21
  139.6 3.5 %convolution_convert_fusion.1 = bf16[512,3072]{1,0:T(8,128)(2,1)} fusion(bf16[512,512]{1,0:T(8,128)(2,1)S(1)} %fusion.3, bf16[3072,256]{1,0:T(8,128)(2,1)S(1)} %copy-done.27, bf16[3072,256]{1,0:T(8,128)(2,1)S(1)} %bitcast.71), kind=kOutput, calls=%fused_computation.1 | convolution fusion | flops 1618477056 | bytes 6815744 | tf_op jit(solution)/shard_map/dot_general | solution.py:293
  143.2 30.7 %all-to-all-done.3 = bf16[32,16,3072]{2,1,0:T(8,128)(2,1)} async-done(((bf16[32,16,3072]{2,1,0:T(8,128)(2,1)}), bf16[32,16,3072]{2,1,0:T(8,128)(2,1)}, u32[]{:S(2)}, u32[]{:S(2)}) %all-to-all-start.3) | async-done | bytes 3145760 | tf_op jit(solution)/shard_map/all_to_all | solution.py:290
  173.9 8.9 %all-to-all-start.2 = ((bf16[32,16,3072]{2,1,0:T(8,128)(2,1)}), bf16[32,16,3072]{2,1,0:T(8,128)(2,1)S(1)}, u32[]{:S(2)}, u32[]{:S(2)}) async-start(bf16[32,16,3072]{2,1,0:T(8,128)(2,1)} %bitcast.62), calls=%async_computation.2 | async-start | bytes 6291456 | tf_op jit(solution)/shard_map/all_to_all | solution.py:296
  182.8 4.2 %convolution_convert_fusion.3 = bf16[3072,256]{1,0:T(8,128)(2,1)} fusion(bf16[512,3072]{1,0:T(8,128)(2,1)} %bitcast.7, bf16[512,512]{1,0:T(8,128)(2,1)} %copy-done.21), kind=kOutput, calls=%fused_computation.3 | convolution fusion | flops 806092800 | bytes 4980736 | tf_op jit(solution)/shard_map/dot_general | solution.py:315
  187.1 1.2 collective-permute-start.17
  188.3 2.2 convolution_convert_fusion.2
  190.5 0.7 copy.57.g_ref
  191.2 0.5 collective-permute-done.17
  191.7 5.1 %convert_add_fusion.1 = f32[3072,256]{1,0:T(8,128)} fusion(bf16[3072,256]{1,0:T(8,128)(2,1)} %collective-permute-done.17, bf16[512,3072]{1,0:T(8,128)(2,1)} %bitcast.7, bf16[512,512]{1,0:T(8,128)(2,1)} %copy-done.21), kind=kOutput, calls=%fused_computation.7 | convolution fusion | flops 806879232 | bytes 8126464 | tf_op jit(solution)/shard_map/dot_general | solution.py:317
  196.8 6.6 %shard_map.121 = (bf16[4,128,384]{2,1,0:T(8,128)(2,1)}, bf16[4,128,384]{2,1,0:T(8,128)(2,1)}, f32[128,128]{1,0:T(8,128)}) custom-call(s32[5]{0:T(128)} %copy-done.9, s32[128,4]{1,0:T(8,128)} %copy-done.2, f32[128,4]{1,0:T(8,128)} %copy.57.g_ref, bf16[512,3072]{1,0:T(8,128)(2,1)} %bitcast.12.rows_ref, bf16[128,3072]{1,0:T(8,128)(2,1)} %copy-done.12), custom_call_target="tpu_custom_call" | custom-call | flops 1207959552 | bytes 3145728 | tf_op jit(solution)/shard_map/pallas_call | solution.py:207
  203.4 0.5 collective-permute-start.16
  203.9 5.1 %convert_add_fusion = f32[256,3072]{1,0:T(8,128)} fusion(bf16[256,3072]{1,0:T(8,128)(2,1)} %collective-permute-done.18, bf16[512,3072]{1,0:T(8,128)(2,1)} %bitcast.59, bf16[512,512]{1,0:T(8,128)(2,1)} %copy-done.15), kind=kOutput, calls=%fused_computation.6 | convolution fusion | flops 806879232 | bytes 8126464 | tf_op jit(solution)/shard_map/dot_general | solution.py:312
  209.0 0.7 add_bitcast_fusion.3
  209.7 0.7 add_bitcast_fusion
  210.5 11.3 %all-to-all-done.2 = bf16[32,16,3072]{2,1,0:T(8,128)(2,1)S(1)} async-done(((bf16[32,16,3072]{2,1,0:T(8,128)(2,1)}), bf16[32,16,3072]{2,1,0:T(8,128)(2,1)S(1)}, u32[]{:S(2)}, u32[]{:S(2)}) %all-to-all-start.2) | async-done | bytes 3145760 | tf_op jit(solution)/shard_map/all_to_all | solution.py:296
  221.8 1.1 copy-done.1
  222.9 2.7 %shard_map.122 = (bf16[4,128,384]{2,1,0:T(8,128)(2,1)S(1)}, bf16[4,128,384]{2,1,0:T(8,128)(2,1)S(1)}, bf16[128,128]{1,0:T(8,128)(2,1)S(1)}) custom-call(s32[5]{0:T(128)S(1)} %copy-done.10, s32[128,4]{1,0:T(8,128)S(1)} %copy-done.3, f32[128,128]{1,0:T(8,128)S(1)} %copy-done.7, f32[128,128]{1,0:T(8,128)S(1)} %get-tuple-element.40.stats_ref, ...), custom_call_target="tpu_custom_call" | custom-call | flops 402653184 | bytes 3145728 | tf_op jit(solution)/shard_map/pallas_call | solution.py:207
  225.7 5.0 %collective-permute-start.20 = (bf16[128,128]{1,0:T(8,128)(2,1)S(1)}, bf16[128,128]{1,0:T(8,128)(2,1)S(1)}, u32[]{:S(2)}, u32[]{:S(2)}) collective-permute-start(bf16[128,128]{1,0:T(8,128)(2,1)S(1)} %get-tuple-element.46), channel_id=1, source_target_pairs={{0,1},{1,0},{2,3},{3,2},{4,5},{5,4},{6,7},{7,6},{8,9},{9,8},{10,11... | collective-permute-start | bytes 98312 | tf_op jit(solution)/shard_map/ppermute | solution.py:28
  230.8 0.7 collective-permute-done.20
  231.9 0.6 collective-permute-done.19
  232.6 3.7 %collective-permute-start.23 = (bf16[128,896]{1,0:T(8,128)(2,1)S(1)}, bf16[128,896]{1,0:T(8,128)(2,1)S(1)}, u32[]{:S(2)}, u32[]{:S(2)}) collective-permute-start(bf16[128,896]{1,0:T(8,128)(2,1)S(1)} %get-tuple-element.94), channel_id=1, source_target_pairs={{0,6},{2,4},{4,2},{6,0},{1,7},{3,5},{5,3},{7,1},{8,14},{10,12},{12... | collective-permute-start | bytes 688136 | tf_op jit(solution)/shard_map/ppermute | solution.py:32
  236.3 0.7 collective-permute-start.22
  237.2 1.6 collective-permute-start.21
  238.8 15.7 %collective-permute-done.23 = bf16[128,896]{1,0:T(8,128)(2,1)S(1)} collective-permute-done((bf16[128,896]{1,0:T(8,128)(2,1)S(1)}, bf16[128,896]{1,0:T(8,128)(2,1)S(1)}, u32[]{:S(2)}, u32[]{:S(2)}) %collective-permute-start.23) | collective-permute-done | bytes 229408 | tf_op jit(solution)/shard_map/ppermute | solution.py:32
  254.5 2.3 collective-permute-done.22
  257.0 0.2 fusion.31
  257.2 0.7 copy.58
  257.9 1.7 fusion.24
  (93 shorter events, 2.2 us)
Async XLA Ops:
  0.6 11.6 %collective-permute-start = (bf16[128,384]{1,0:T(8,128)(2,1)}, bf16[128,384]{1,0:T(8,128)(2,1)S(1)}, u32[]{:S(2)}, u32[]{:S(2)}) collective-permute-start(bf16[128,384]{1,0:T(8,128)(2,1)} %refs_0_.1), channel_id=1, source_target_pairs={{0,2},{2,0},{4,6},{6,4},{1,3},{3,1},{5,7},{7,5},{8,10},{10,8},{12,... | collective-permute-start | bytes 294920 | tf_op jit(solution)/shard_map/ppermute | solution.py:32
  0.7 11.8 %collective-permute-start.1 = (bf16[128,384]{1,0:T(8,128)(2,1)}, bf16[128,384]{1,0:T(8,128)(2,1)S(1)}, u32[]{:S(2)}, u32[]{:S(2)}) collective-permute-start(bf16[128,384]{1,0:T(8,128)(2,1)} %refs_0_.1), channel_id=1, source_target_pairs={{0,4},{2,6},{4,0},{6,2},{1,5},{3,7},{5,1},{7,3},{8,12},{10,14},{12... | collective-permute-start | bytes 294920 | tf_op jit(solution)/shard_map/ppermute | solution.py:32
  7.0 11.0 %collective-permute-start.2 = (bf16[128,384]{1,0:T(8,128)(2,1)}, bf16[128,384]{1,0:T(8,128)(2,1)S(1)}, u32[]{:S(2)}, u32[]{:S(2)}) collective-permute-start(bf16[128,384]{1,0:T(8,128)(2,1)} %refs_0_.1), channel_id=1, source_target_pairs={{0,6},{2,4},{4,2},{6,0},{1,7},{3,5},{5,3},{7,1},{8,14},{10,12},{12... | collective-permute-start | bytes 294920 | tf_op jit(solution)/shard_map/ppermute | solution.py:32
  7.0 13.2 %collective-permute-start.3 = (bf16[128,384]{1,0:T(8,128)(2,1)}, bf16[128,384]{1,0:T(8,128)(2,1)S(1)}, u32[]{:S(2)}, u32[]{:S(2)}) collective-permute-start(bf16[128,384]{1,0:T(8,128)(2,1)} %refs_0_.1), channel_id=1, source_target_pairs={{0,1},{1,0},{2,3},{3,2},{4,5},{5,4},{6,7},{7,6},{8,9},{9,8},{10,11... | collective-permute-start | bytes 294920 | tf_op jit(solution)/shard_map/ppermute | solution.py:28
  8.2 20.0 %collective-permute-start.7 = (bf16[128,384]{1,0:T(8,128)(2,1)}, bf16[128,384]{1,0:T(8,128)(2,1)S(1)}, u32[]{:S(2)}, u32[]{:S(2)}) collective-permute-start(bf16[128,384]{1,0:T(8,128)(2,1)} %refs_0_.2), channel_id=1, source_target_pairs={{0,2},{2,0},{4,6},{6,4},{1,3},{3,1},{5,7},{7,5},{8,10},{10,8},{12,... | collective-permute-start | bytes 294920 | tf_op jit(solution)/shard_map/ppermute | solution.py:32
  12.2 16.1 %copy-start.2 = (s32[128,4]{1,0:T(8,128)}, s32[128,4]{1,0:T(8,128)S(1)}, u32[]{:S(2)}) copy-start(s32[128,4]{1,0:T(8,128)S(1)} %fusion.42.q_ref) | copy-start | bytes 6148
  12.2 8.4 %collective-permute-start.4 = (bf16[128,384]{1,0:T(8,128)(2,1)S(1)}, bf16[128,384]{1,0:T(8,128)(2,1)S(1)}, u32[]{:S(2)}, u32[]{:S(2)}) collective-permute-start(bf16[128,384]{1,0:T(8,128)(2,1)S(1)} %collective-permute-done.refs_1_), channel_id=1, source_target_pairs={{0,1},{1,0},{2,3},{3,2},{4,5},{5,4},{6,7},{7,6},{8,9},{9,8},{10,11... | collective-permute-start | bytes 294920 | tf_op jit(solution)/shard_map/ppermute | solution.py:28
  12.6 15.7 %collective-permute-start.8 = (bf16[128,384]{1,0:T(8,128)(2,1)}, bf16[128,384]{1,0:T(8,128)(2,1)S(1)}, u32[]{:S(2)}, u32[]{:S(2)}) collective-permute-start(bf16[128,384]{1,0:T(8,128)(2,1)} %refs_0_.2), channel_id=1, source_target_pairs={{0,4},{2,6},{4,0},{6,2},{1,5},{3,7},{5,1},{7,3},{8,12},{10,14},{12... | collective-permute-start | bytes 294920 | tf_op jit(solution)/shard_map/ppermute | solution.py:32
  18.0 10.2 %collective-permute-start.9 = (bf16[128,384]{1,0:T(8,128)(2,1)}, bf16[128,384]{1,0:T(8,128)(2,1)S(1)}, u32[]{:S(2)}, u32[]{:S(2)}) collective-permute-start(bf16[128,384]{1,0:T(8,128)(2,1)} %refs_0_.2), channel_id=1, source_target_pairs={{0,6},{2,4},{4,2},{6,0},{1,7},{3,5},{5,3},{7,1},{8,14},{10,12},{12... | collective-permute-start | bytes 294920 | tf_op jit(solution)/shard_map/ppermute | solution.py:32
  20.2 1.4 collective-permute-start.5
  20.6 1.3 collective-permute-start.6
  20.8 18.6 %copy-start.9 = (s32[5]{0:T(128)}, s32[5]{0:T(128)S(1)}, u32[]{:S(2)}) copy-start(s32[5]{0:T(128)S(1)} %pad_add_fusion.order) | copy-start | bytes 64
  21.9 0.9 copy-start.5
  27.3 0.9 copy-start
  28.3 8.8 %copy-start.11 = (bf16[128,384]{1,0:T(8,128)(2,1)S(1)}, bf16[128,384]{1,0:T(8,128)(2,1)}, u32[]{:S(2)}) copy-start(bf16[128,384]{1,0:T(8,128)(2,1)} %refs_0_.2) | copy-start | bytes 294916
  28.3 11.1 %copy-start.8 = (f32[128,4]{0,1:T(4,128)S(1)}, f32[128,4]{0,1:T(4,128)}, u32[]{:S(2)}) copy-start(f32[128,4]{0,1:T(4,128)} %param.13) | copy-start | bytes 6148
  28.3 50.4 %all-to-all-start.1 = ((bf16[32,16,3072]{2,1,0:T(8,128)(2,1)}), bf16[32,16,3072]{2,1,0:T(8,128)(2,1)}, u32[]{:S(2)}, u32[]{:S(2)}) async-start(bf16[32,16,3072]{2,1,0:T(8,128)(2,1)} %bitcast.6), calls=%async_computation.1 | async-start | bytes 6291456 | tf_op jit(solution)/shard_map/all_to_all | solution.py:271
  37.1 1.5 collective-permute-start.10
  37.6 1.3 collective-permute-start.11
  37.7 1.4 collective-permute-start.12
  38.1 1.3 collective-permute-start.13
  43.1 0.9 copy-start.12
  78.6 47.5 %all-to-all-start = ((bf16[32,16,3072]{2,1,0:T(8,128)(2,1)}), bf16[32,16,3072]{2,1,0:T(8,128)(2,1)S(1)}, u32[]{:S(2)}, u32[]{:S(2)}) async-start(bf16[32,16,3072]{2,1,0:T(8,128)(2,1)} %bitcast.3), calls=%async_computation | async-start | bytes 6291456 | tf_op jit(solution)/shard_map/all_to_all | solution.py:281
  86.0 4.3 %collective-permute-start.15 = (bf16[3072,256]{1,0:T(8,128)(2,1)}, bf16[3072,256]{1,0:T(8,128)(2,1)S(1)}, u32[]{:S(2)}, u32[]{:S(2)}) collective-permute-start(bf16[3072,256]{1,0:T(8,128)(2,1)} %bitcast.69), channel_id=1, source_target_pairs={{0,1},{1,0},{2,3},{3,2},{4,5},{5,4},{6,7},{7,6},{8,9},{9,8},{10,11... | collective-permute-start | bytes 4718600 | tf_op jit(solution)/shard_map/ppermute | solution.py:28
  87.1 9.0 %collective-permute-start.14 = (bf16[256,3072]{1,0:T(8,128)(2,1)}, bf16[256,3072]{1,0:T(8,128)(2,1)S(1)}, u32[]{:S(2)}, u32[]{:S(2)}) collective-permute-start(bf16[256,3072]{1,0:T(8,128)(2,1)} %bitcast.66), channel_id=1, source_target_pairs={{0,1},{1,0},{2,3},{3,2},{4,5},{5,4},{6,7},{7,6},{8,9},{9,8},{10,11... | collective-permute-start | bytes 4718600 | tf_op jit(solution)/shard_map/ppermute | solution.py:28
  90.4 5.8 %copy-start.26 = (bf16[3072,256]{1,0:T(8,128)(2,1)}, bf16[3072,256]{1,0:T(8,128)(2,1)S(1)}, u32[]{:S(2)}) copy-start(bf16[3072,256]{1,0:T(8,128)(2,1)S(1)} %collective-permute-done.15) | copy-start | bytes 4718596
  90.4 7.1 %copy-start.24 = (bf16[1,256,3072]{2,1,0:T(8,128)(2,1)S(1)}, bf16[1,256,3072]{2,1,0:T(8,128)(2,1)}, u32[]{:S(2)}) copy-start(bf16[1,256,3072]{2,1,0:T(8,128)(2,1)} %param.15) | copy-start | bytes 4718596
  96.1 0.8 copy-start.15
  96.1 1.4 copy-start.28
  126.1 8.2 %copy-start.13 = (bf16[32,16,3072]{2,1,0:T(8,128)(2,1)}, bf16[32,16,3072]{2,1,0:T(8,128)(2,1)S(1)}, u32[]{:S(2)}) copy-start(bf16[32,16,3072]{2,1,0:T(8,128)(2,1)S(1)} %all-to-all-done) | copy-start | bytes 9437188
  126.1 47.8 %all-to-all-start.3 = ((bf16[32,16,3072]{2,1,0:T(8,128)(2,1)}), bf16[32,16,3072]{2,1,0:T(8,128)(2,1)}, u32[]{:S(2)}, u32[]{:S(2)}) async-start(bf16[32,16,3072]{2,1,0:T(8,128)(2,1)} %bitcast.63), calls=%async_computation.3 | async-start | bytes 6291456 | tf_op jit(solution)/shard_map/all_to_all | solution.py:290
  134.3 5.3 %copy-start.25 = (bf16[1,3072,256]{2,1,0:T(8,128)(2,1)S(1)}, bf16[1,3072,256]{2,1,0:T(8,128)(2,1)}, u32[]{:S(2)}) copy-start(bf16[1,3072,256]{2,1,0:T(8,128)(2,1)} %param.14) | copy-start | bytes 4718596
  134.3 5.3 %copy-start.27 = (bf16[3072,256]{1,0:T(8,128)(2,1)S(1)}, bf16[3072,256]{1,0:T(8,128)(2,1)}, u32[]{:S(2)}) copy-start(bf16[3072,256]{1,0:T(8,128)(2,1)} %copy-done.26) | copy-start | bytes 4718596
  138.8 0.8 copy-start.21
  173.9 47.9 %all-to-all-start.2 = ((bf16[32,16,3072]{2,1,0:T(8,128)(2,1)}), bf16[32,16,3072]{2,1,0:T(8,128)(2,1)S(1)}, u32[]{:S(2)}, u32[]{:S(2)}) async-start(bf16[32,16,3072]{2,1,0:T(8,128)(2,1)} %bitcast.62), calls=%async_computation.2 | async-start | bytes 6291456 | tf_op jit(solution)/shard_map/all_to_all | solution.py:296
  182.8 5.5 %copy-start.14 = (bf16[32,16,3072]{2,1,0:T(8,128)(2,1)S(1)}, bf16[32,16,3072]{2,1,0:T(8,128)(2,1)}, u32[]{:S(2)}) copy-start(bf16[32,16,3072]{2,1,0:T(8,128)(2,1)} %copy-done.13) | copy-start | bytes 9437188
  182.8 5.5 %copy-start.16 = (bf16[512,512]{1,0:T(8,128)(2,1)S(1)}, bf16[512,512]{1,0:T(8,128)(2,1)}, u32[]{:S(2)}) copy-start(bf16[512,512]{1,0:T(8,128)(2,1)} %copy-done.15) | copy-start | bytes 1572868
  187.1 4.6 %collective-permute-start.17 = (bf16[3072,256]{1,0:T(8,128)(2,1)}, bf16[3072,256]{1,0:T(8,128)(2,1)}, u32[]{:S(2)}, u32[]{:S(2)}) collective-permute-start(bf16[3072,256]{1,0:T(8,128)(2,1)} %convolution_convert_fusion.3), channel_id=1, source_target_pairs={{0,1},{1,0},{2,3},{3,2},{4,5},{5,4},{6,7},{7,6},{8,9},{9,8},{10,11... | collective-permute-start | bytes 4718600 | tf_op jit(solution)/shard_map/ppermute | solution.py:28
  190.5 13.4 %collective-permute-start.18 = (bf16[256,3072]{1,0:T(8,128)(2,1)}, bf16[256,3072]{1,0:T(8,128)(2,1)}, u32[]{:S(2)}, u32[]{:S(2)}) collective-permute-start(bf16[256,3072]{1,0:T(8,128)(2,1)} %convolution_convert_fusion.2), channel_id=1, source_target_pairs={{0,1},{1,0},{2,3},{3,2},{4,5},{5,4},{6,7},{7,6},{8,9},{9,8},{10,11... | collective-permute-start | bytes 4718600 | tf_op jit(solution)/shard_map/ppermute | solution.py:28
  203.4 5.6 %copy-start.20 = (bf16[4,128,384]{2,1,0:T(8,128)(2,1)S(1)}, bf16[4,128,384]{2,1,0:T(8,128)(2,1)}, u32[]{:S(2)}) copy-start(bf16[4,128,384]{2,1,0:T(8,128)(2,1)} %get-tuple-element.36) | copy-start | bytes 1179652
  203.4 18.4 %copy-start.3 = (s32[128,4]{1,0:T(8,128)S(1)}, s32[128,4]{1,0:T(8,128)}, u32[]{:S(2)}) copy-start(s32[128,4]{1,0:T(8,128)} %copy-done.2) | copy-start | bytes 6148
  203.4 18.4 %copy-start.7 = (f32[128,128]{1,0:T(8,128)S(1)}, f32[128,128]{1,0:T(8,128)}, u32[]{:S(2)}) copy-start(f32[128,128]{1,0:T(8,128)} %get-tuple-element.39.inner_ref) | copy-start | bytes 196612
  203.4 18.4 %copy-start.10 = (s32[5]{0:T(128)S(1)}, s32[5]{0:T(128)}, u32[]{:S(2)}) copy-start(s32[5]{0:T(128)} %copy-done.9) | copy-start | bytes 64
  203.4 5.6 %collective-permute-start.16 = (bf16[4,128,384]{2,1,0:T(8,128)(2,1)}, bf16[4,128,384]{2,1,0:T(8,128)(2,1)S(1)}, u32[]{:S(2)}, u32[]{:S(2)}) collective-permute-start(bf16[4,128,384]{2,1,0:T(8,128)(2,1)} %get-tuple-element.37), channel_id=1, source_target_pairs={{0,1},{1,0},{2,3},{3,2},{4,5},{5,4},{6,7},{7,6},{8,9},{9,8},{10,11... | collective-permute-start | bytes 1179656 | tf_op jit(solution)/shard_map/ppermute | solution.py:28
  221.8 1.1 copy-start.1
  222.9 9.6 %copy-start.18 = (bf16[128,384]{1,0:T(8,128)(2,1)S(1)}, bf16[128,384]{1,0:T(8,128)(2,1)}, u32[]{:S(2)}) copy-start(bf16[128,384]{1,0:T(8,128)(2,1)} %get-tuple-element.47) | copy-start | bytes 294916
  222.9 9.6 %copy-start.19 = (bf16[128,384]{1,0:T(8,128)(2,1)S(1)}, bf16[128,384]{1,0:T(8,128)(2,1)}, u32[]{:S(2)}) copy-start(bf16[128,384]{1,0:T(8,128)(2,1)} %get-tuple-element.45) | copy-start | bytes 294916
  225.6 11.5 %copy-start.4 = (bf16[4,128,384]{2,1,0:T(8,128)(2,1)}, bf16[4,128,384]{2,1,0:T(8,128)(2,1)S(1)}, u32[]{:S(2)}) copy-start(bf16[4,128,384]{2,1,0:T(8,128)(2,1)S(1)} %get-tuple-element.43) | copy-start | bytes 1179652
  225.6 32.2 %copy-start.6 = (bf16[128,384]{1,0:T(8,128)(2,1)S(1)}, bf16[128,384]{1,0:T(8,128)(2,1)}, u32[]{:S(2)}) copy-start(bf16[128,384]{1,0:T(8,128)(2,1)} %refs_0_.1) | copy-start | bytes 294916
  225.6 32.2 %copy-start.17 = (f32[128,384]{1,0:T(8,128)S(1)}, f32[128,384]{1,0:T(8,128)}, u32[]{:S(2)}) copy-start(f32[128,384]{1,0:T(8,128)} %add_bitcast_fusion.3) | copy-start | bytes 589828
  225.7 32.2 %copy-start.22 = (bf16[128,384]{1,0:T(8,128)(2,1)S(1)}, bf16[128,384]{1,0:T(8,128)(2,1)}, u32[]{:S(2)}) copy-start(bf16[128,384]{1,0:T(8,128)(2,1)} %param.10) | copy-start | bytes 294916
  225.7 32.2 %copy-start.23 = (bf16[128,384]{1,0:T(8,128)(2,1)S(1)}, bf16[128,384]{1,0:T(8,128)(2,1)}, u32[]{:S(2)}) copy-start(bf16[128,384]{1,0:T(8,128)(2,1)} %param.9) | copy-start | bytes 294916
  225.7 5.9 %collective-permute-start.20 = (bf16[128,128]{1,0:T(8,128)(2,1)S(1)}, bf16[128,128]{1,0:T(8,128)(2,1)S(1)}, u32[]{:S(2)}, u32[]{:S(2)}) collective-permute-start(bf16[128,128]{1,0:T(8,128)(2,1)S(1)} %get-tuple-element.46), channel_id=1, source_target_pairs={{0,1},{1,0},{2,3},{3,2},{4,5},{5,4},{6,7},{7,6},{8,9},{9,8},{10,11... | collective-permute-start | bytes 98312 | tf_op jit(solution)/shard_map/ppermute | solution.py:28
  230.7 1.7 collective-permute-start.19
  232.6 21.9 %collective-permute-start.23 = (bf16[128,896]{1,0:T(8,128)(2,1)S(1)}, bf16[128,896]{1,0:T(8,128)(2,1)S(1)}, u32[]{:S(2)}, u32[]{:S(2)}) collective-permute-start(bf16[128,896]{1,0:T(8,128)(2,1)S(1)} %get-tuple-element.94), channel_id=1, source_target_pairs={{0,6},{2,4},{4,2},{6,0},{1,7},{3,5},{5,3},{7,1},{8,14},{10,12},{12... | collective-permute-start | bytes 688136 | tf_op jit(solution)/shard_map/ppermute | solution.py:32
  236.3 20.5 %collective-permute-start.22 = (bf16[128,896]{1,0:T(8,128)(2,1)S(1)}, bf16[128,896]{1,0:T(8,128)(2,1)S(1)}, u32[]{:S(2)}, u32[]{:S(2)}) collective-permute-start(bf16[128,896]{1,0:T(8,128)(2,1)S(1)} %get-tuple-element.93), channel_id=1, source_target_pairs={{0,4},{2,6},{4,0},{6,2},{1,5},{3,7},{5,1},{7,3},{8,12},{10,14},{12... | collective-permute-start | bytes 688136 | tf_op jit(solution)/shard_map/ppermute | solution.py:32
  237.2 19.7 %collective-permute-start.21 = (bf16[128,896]{1,0:T(8,128)(2,1)S(1)}, bf16[128,896]{1,0:T(8,128)(2,1)S(1)}, u32[]{:S(2)}, u32[]{:S(2)}) collective-permute-start(bf16[128,896]{1,0:T(8,128)(2,1)S(1)} %get-tuple-element.92), channel_id=1, source_target_pairs={{0,2},{2,0},{4,6},{6,4},{1,3},{3,1},{5,7},{7,5},{8,10},{10,8},{12,... | collective-permute-start | bytes 688136 | tf_op jit(solution)/shard_map/ppermute | solution.py:32

commit v3 on v2

v3 whole, which is shorter than its diff:
```python
import functools

import jax
import jax.numpy as jnp
from jax import lax
from jax.experimental import pallas as pl
from jax.experimental.pallas import tpu as pltpu
from jax.sharding import Mesh, PartitionSpec as P

F32 = jnp.float32
BF16 = jnp.bfloat16
CTX = ("y", "zl", "x")
CORES = ((0, 1), (1, 0))


def gelu_value(x):
    return x * 0.5 * (1.0 + lax.erf(x * 0.7071067811865476))


def gelu_slope(x):
    return (
        0.5 * (1.0 + lax.erf(x * 0.7071067811865476))
        + x * jnp.exp(-0.5 * x * x) * 0.3989422804014327
    )


def swap_cores(v):
    return lax.ppermute(v, "core", CORES)


def swap_chips(v, r):
    return lax.ppermute(v, "zh", [(i, i ^ r) for i in range(4)])


def gather_chips(v):
    return [v] + [swap_chips(v, r) for r in (1, 2, 3)]


def gather_features(v):
    mine = gather_chips(v)
    return mine + [swap_cores(m) for m in mine]


def select_rows(qt, slots):
    topk, tokens = qt.shape
    at = lax.broadcasted_iota(jnp.int32, (slots, tokens), 0)
    hit = at == qt[0:1, :]
    for k in range(1, topk):
        hit = jnp.logical_or(hit, at == qt[k : k + 1, :])
    return hit


def columns_of(core, mine, other):
    first = core == 0
    left = jnp.where(first, mine, other)
    right = jnp.where(first, other, mine)
    return jnp.concatenate([left, right], axis=1)


def pack_kernel(order, qt_ref, gt_ref, *refs):
    parts, (out_ref, first_ref, second_ref, stats_ref, low, pick, gate) = refs[:8], refs[8:]
    step = pl.program_id(0)
    core = order[4]
    slots = pick.shape[0]
    half = out_ref.shape[1] // 2

    @pl.when(step == 0)
    def _():
        width = 8 * parts[0].shape[2]
        total = sum(jnp.sum(p[0].astype(F32), axis=1, keepdims=True) for p in parts)
        mean = total / width
        square = sum(
            jnp.sum(jnp.square(p[0].astype(F32) - mean), axis=1, keepdims=True) for p in parts
        )
        rstd = lax.rsqrt(square / width + 1e-05)
        for i in range(4):
            both = columns_of(core, parts[i][0].astype(F32), parts[4 + i][0].astype(F32))
            low[i] = ((both - mean) * rstd).astype(BF16)
        lane = lax.broadcasted_iota(jnp.int32, stats_ref.shape, 1)
        stats_ref[...] = jnp.where(lane == 0, mean, rstd)
        qt, gt = qt_ref[...], gt_ref[...]
        pick[...] = jnp.where(select_rows(qt, slots), 1.0, 0.0).astype(BF16)
        at = lax.broadcasted_iota(jnp.int32, (slots, qt.shape[1]), 0)
        weight = jnp.zeros((slots, qt.shape[1]), F32)
        for k in range(qt.shape[0]):
            weight = weight + jnp.where(at == qt[k : k + 1, :], gt[k : k + 1, :], 0.0)
        gate[...] = jnp.sum(weight, axis=1, keepdims=True)

    rows = jnp.dot(pick[...], low[step], preferred_element_type=F32).astype(BF16)
    out_ref[:, :half, :] = rows.reshape(-1, half, rows.shape[1])

    for i in range(4):

        @pl.when(step == i)
        def _(i=i):
            mine, other = parts[i], parts[4 + i]
            first_ref[...] = columns_of(core, mine[0].astype(F32), other[0].astype(F32)).astype(BF16)
            both = columns_of(core, mine[1].astype(F32), other[1].astype(F32)).astype(BF16)
            second_ref[...] = both
            raw = jnp.dot(pick[...], both, preferred_element_type=F32)
            scaled = (gate[...] * raw).astype(BF16)
            out_ref[:, half:, :] = scaled.reshape(-1, half, scaled.shape[1])


def expert_kernel(x_ref, g_ref, wi_a, wi_b, wo_a, wo_b, out_ref, hidden_ref, pre_ref):
    blocks, half, width = x_ref.shape
    own = wi_a.shape[1]
    wide = width // 4
    x = x_ref[...].reshape(blocks * half, width)
    g = g_ref[...].reshape(blocks * half, width)
    last = (((1,), (1,)), ((), ()))
    hidden, grad_pre = [], []
    for wi, wo in ((wi_a, wo_a), (wi_b, wo_b)):
        preact = jnp.dot(x, wi[...], preferred_element_type=F32)
        hidden.append(gelu_value(preact).astype(BF16))
        grad_hidden = lax.dot_general(g, wo[...], last, preferred_element_type=F32)
        grad_pre.append((grad_hidden * gelu_slope(preact)).astype(BF16))
    hidden_ref[:, :own], hidden_ref[:, own:] = hidden
    pre_ref[:, :own], pre_ref[:, own:] = grad_pre
    for n in range(4):
        at = slice(n * wide, (n + 1) * wide)
        value = jnp.dot(hidden[0], wo_a[:, at], preferred_element_type=F32) + jnp.dot(
            hidden[1], wo_b[:, at], preferred_element_type=F32
        )
        out_ref[:, :half, at] = value.astype(BF16).reshape(blocks, half, wide)
        value = lax.dot_general(
            grad_pre[0], wi_a[at, :], last, preferred_element_type=F32
        ) + lax.dot_general(grad_pre[1], wi_b[at, :], last, preferred_element_type=F32)
        out_ref[:, half:, at] = value.astype(BF16).reshape(blocks, half, wide)


def combine_kernel(order, q_ref, g_ref, stats_ref, out_rows, dx_rows, first_ref, second_ref, keep_ref, give_ref, sums_ref, high, rest, pick, inner, sums):
    step = pl.program_id(0)
    part = keep_ref.shape[2] // 2
    slots = pick.shape[1]
    topk = q_ref.shape[1]
    first = order[4] == 0

    @pl.when(step == 0)
    def _():
        lane = lax.broadcasted_iota(jnp.int32, inner.shape, 1)
        weight = jnp.zeros(inner.shape, F32)
        for k in range(topk):
            weight = weight + jnp.where(lane == q_ref[:, k : k + 1], g_ref[:, k : k + 1], 0.0)
        top = weight.astype(BF16)
        high[...] = top
        rest[...] = (weight - top.astype(F32)).astype(BF16)
        hit = lane == q_ref[:, 0:1]
        for k in range(1, topk):
            hit = jnp.logical_or(hit, lane == q_ref[:, k : k + 1])
        pick[...] = jnp.where(hit, 1.0, 0.0).astype(BF16)
        inner[...] = jnp.zeros_like(inner)
        sums[...] = jnp.zeros_like(sums)

    def store(value, at):
        left, right = value[:, :part], value[:, part:]
        keep_ref[0, :, at : at + part] = jnp.where(first, left, right).astype(BF16)
        give_ref[0, :, at : at + part] = jnp.where(first, right, left).astype(BF16)

    rows = out_rows[...].reshape(slots, 2 * part)
    value = jnp.dot(high[...], rows, preferred_element_type=F32) + jnp.dot(
        rest[...], rows, preferred_element_type=F32
    )
    store(value, 0)
    inner[...] += lax.dot_general(
        second_ref[...], rows, (((1,), (1,)), ((), ())), preferred_element_type=F32
    )
    value = jnp.dot(pick[...], dx_rows[...].reshape(slots, 2 * part), preferred_element_type=F32)
    store(value, part)
    normed = (first_ref[...].astype(F32) - stats_ref[:, 0:1]) * stats_ref[:, 1:2]
    lane = lax.broadcasted_iota(jnp.int32, sums.shape, 1)
    place = lane % 8
    plain = jnp.sum(value, axis=1, keepdims=True)
    mixed = jnp.sum(value * normed, axis=1, keepdims=True)
    sums[...] += jnp.where(place == 4, plain, 0.0) + jnp.where(place == 5, mixed, 0.0)

    @pl.when(step == 3)
    def _():
        slot = lax.broadcasted_iota(jnp.int32, inner.shape, 1)
        all_sums = sums[...]
        for k in range(topk):
            one = jnp.sum(
                jnp.where(slot == q_ref[:, k : k + 1], inner[...], 0.0), axis=1, keepdims=True
            )
            all_sums = all_sums + jnp.where(place == k, one, 0.0)
        top = all_sums.astype(BF16).astype(F32)
        middle = (all_sums - top).astype(BF16).astype(F32)
        lowest = all_sums - top - middle
        sums_ref[...] = jnp.where(lane < 8, top, jnp.where(lane < 16, middle, lowest)).astype(BF16)


def join_thirds(v):
    v = v.astype(F32)
    return (v[:, 0:8] + v[:, 8:16]) + v[:, 16:24]


def split_thirds(v):
    high = lax.reduce_precision(v, 8, 7)
    middle = lax.reduce_precision(v - high, 8, 7)
    lowest = v - high - middle
    return jnp.pad(jnp.concatenate([high, middle, lowest], axis=1).astype(BF16), ((0, 0), (0, 104)))


def whole(shape):
    return pl.BlockSpec(shape, lambda i, order: (0,) * len(shape))


def run(kernel, order, args, in_specs, out_shape, out_specs, scratch, flops, moved, limit=None):
    return pl.pallas_call(
        kernel,
        grid_spec=pltpu.PrefetchScalarGridSpec(
            num_scalar_prefetch=1,
            grid=(4,),
            in_specs=in_specs,
            out_specs=out_specs,
            scratch_shapes=scratch,
        ),
        out_shape=out_shape,
        compiler_params=pltpu.CompilerParams(
            dimension_semantics=("arbitrary",), vmem_limit_bytes=limit
        ),
        cost_estimate=pl.CostEstimate(flops=flops, bytes_accessed=moved, transcendentals=0),
    )(order, *args)


def on_device(
    stream_first, stream_second, grad_first, grad_second, expert_ids, gate_probs, w_in, w_out
):
    tokens, part = stream_first.shape
    topk = expert_ids.shape[1]
    width = part * 8
    experts = 32
    half = 16
    slots = experts * half
    core = lax.axis_index("core")
    zh = lax.axis_index("zh")

    expert = jnp.arange(experts, dtype=jnp.int32)
    match = expert_ids[:, :, None] == expert[None, None, :]
    named = jnp.any(match, axis=1).astype(BF16)
    earlier = jnp.tri(tokens, k=-1, dtype=BF16)
    before = jnp.dot(earlier, named, preferred_element_type=F32)
    rank = jnp.sum(jnp.where(match, before[:, None, :], 0.0), axis=2).astype(jnp.int32)
    q = jnp.where(rank % 2 == core, expert_ids * half + rank // 2, -1)
    qt = q.T
    gt = gate_probs.T
    order = jnp.append(jnp.bitwise_xor(zh, jnp.arange(4, dtype=jnp.int32)), core).astype(jnp.int32)

    streams = gather_features(jnp.stack([stream_first, grad_second]))

    token_block = pl.BlockSpec((tokens, 2 * part), lambda i, order: (0, order[i]))
    step_block = pl.BlockSpec((1, tokens, 2 * part), lambda i, order: (i, 0, 0))
    rows_shape = jax.ShapeDtypeStruct((experts, 2 * half, width), BF16)
    full_shape = jax.ShapeDtypeStruct((tokens, width), BF16)
    lane_shape = jax.ShapeDtypeStruct((tokens, 128), F32)
    parts_shape = jax.ShapeDtypeStruct((4, tokens, 2 * part), BF16)
    pick_flops = 2 * slots * tokens * width

    def rows_block(n):
        return pl.BlockSpec((experts, half, 2 * part), lambda i, order: (0, n, order[i]))

    rows, first_full, second_full, stats = run(
        pack_kernel, order, (qt, gt, *streams),
        [whole((topk, tokens))] * 2 + [whole((2, tokens, part))] * 8,
        (rows_shape, full_shape, full_shape, lane_shape),
        (
            pl.BlockSpec((experts, 2 * half, 2 * part), lambda i, order: (0, 0, order[i])),
            token_block, token_block, whole((tokens, 128)),
        ),
        [
            pltpu.VMEM((4, tokens, 2 * part), BF16),
            pltpu.VMEM((slots, tokens), BF16),
            pltpu.VMEM((slots, 1), F32),
        ],
        2 * pick_flops, 4 * slots * width, 24 * 2**20,
    )
    send = functools.partial(
        lax.all_to_all, axis_name=CTX, split_axis=0, concat_axis=0, tiled=True
    )
    wi, wo = w_in[0], w_out[0]
    gates = jnp.pad(gate_probs, ((0, 0), (0, 128 - topk)))
    rows, gates, wi_b, wo_b = lax.optimization_barrier(
        (rows, gates, swap_cores(wi), swap_cores(wo))
    )
    arrived = send(rows)

    own = wo.shape[0]
    step_rows = experts // 2

    def source_block(n):
        return pl.BlockSpec((step_rows, half, width), lambda i: (i, n, 0))

    def fixed(shape):
        return pl.BlockSpec(shape, lambda i: (0, 0))

    unit_block = pl.BlockSpec((step_rows * half, 2 * own), lambda i: (i, 0))
    unit_shape = jax.ShapeDtypeStruct((slots, 2 * own), BF16)
    results, hidden, grad_pre = pl.pallas_call(
        expert_kernel,
        grid=(2,),
        in_specs=[
            source_block(0), source_block(1),
            fixed((width, own)), fixed((width, own)), fixed((own, width)), fixed((own, width)),
        ],
        out_specs=(
            pl.BlockSpec((step_rows, 2 * half, width), lambda i: (i, 0, 0)), unit_block, unit_block
        ),
        out_shape=(rows_shape, unit_shape, unit_shape),
        compiler_params=pltpu.CompilerParams(
            dimension_semantics=("arbitrary",), vmem_limit_bytes=60 * 2**20
        ),
        cost_estimate=pl.CostEstimate(
            flops=16 * slots * own * width, bytes_accessed=12 * slots * width, transcendentals=0
        ),
    )(arrived, arrived, wi, wi_b, wo, wo_b)
    back = send(results)

    keep, give, sums = run(
        combine_kernel, order, (q, gates, stats, back, back, first_full, second_full),
        [whole((tokens, topk))]
        + [whole((tokens, 128))] * 2
        + [rows_block(0), rows_block(1), token_block, token_block],
        (parts_shape, parts_shape, jax.ShapeDtypeStruct((tokens, 128), BF16)),
        (step_block, step_block, whole((tokens, 128))),
        [pltpu.VMEM((tokens, slots), BF16)] * 3
        + [pltpu.VMEM((tokens, slots), F32), pltpu.VMEM((tokens, 128), F32)],
        4 * pick_flops, 4 * slots * width, 24 * 2**20,
    )
    got, got_sums = swap_cores(give), swap_cores(sums)
    halves = [keep[r].astype(F32) + got[r].astype(F32) for r in range(4)]
    sums = join_thirds(sums) + join_thirds(got_sums)
    thirds = split_thirds(sums)
    sent = [jnp.concatenate([halves[r].astype(BF16), thirds], axis=1) for r in (1, 2, 3)]
    arrived, hidden, grad_pre, *sent = lax.optimization_barrier((arrived, hidden, grad_pre, *sent))
    others = [swap_chips(v, r) for r, v in zip((1, 2, 3), sent)]

    x = arrived[:, :half].reshape(slots, width)
    g = arrived[:, half:].reshape(slots, width)
    rows_rows = (((0,), (0,)), ((), ()))
    out_give = lax.dot_general(hidden[:, own:], g, rows_rows, preferred_element_type=F32).astype(BF16)
    out_got = swap_cores(out_give)
    grad_w_out = lax.dot_general(
        hidden[:, :own], g, rows_rows, preferred_element_type=F32
    ) + out_got.astype(F32)
    in_give = lax.dot_general(x, grad_pre[:, own:], rows_rows, preferred_element_type=F32).astype(BF16)
    in_got = swap_cores(in_give)
    grad_w_in = lax.dot_general(
        x, grad_pre[:, :own], rows_rows, preferred_element_type=F32
    ) + in_got.astype(F32)

    *others, grad_w_in, grad_w_out = lax.optimization_barrier((*others, grad_w_in, grad_w_out))
    s1, s2, s3 = [join_thirds(o[:, 2 * part :]) for o in others]
    sums = (sums + s1) + (s2 + s3)
    total = halves[0]
    for o in others:
        total = total + o[:, : 2 * part].astype(F32)
    branch, grad_normed = total[:, :part], total[:, part:]
    stream_input = (stream_second.astype(F32) - branch).astype(BF16)
    mean, rstd = stats[:, 0:1], stats[:, 1:2]
    normed = (stream_first.astype(F32) - mean) * rstd
    correction = grad_normed - sums[:, 4:5] / width - normed * (sums[:, 5:6] / width)
    grad_stream = (grad_first.astype(F32) + rstd * correction).astype(BF16)
    return stream_input, grad_stream, grad_w_in[None], grad_w_out[None], sums[:, :topk]


def solution(mesh):
    wide = Mesh(
        mesh.devices.reshape(4, 2, 4, 4, 2), ("y", "zl", "x", "zh", "core")
    )
    tp = ("zh", "core")
    in_specs = (
        P(CTX, tp),
        P(CTX, tp),
        P(CTX, tp),
        P(CTX, tp),
        P(CTX, None),
        P(CTX, None),
        P(CTX, None, tp),
        P(CTX, tp, None),
    )
    out_specs = (
        P(CTX, tp),
        P(CTX, tp),
        P(CTX, None, tp),
        P(CTX, tp, None),
        P(CTX, None),
    )
    return jax.shard_map(
        on_device, mesh=wide, in_specs=in_specs, out_specs=out_specs, check_vma=False
    )
```

time: 263 us -> 250 us (0.951)
  blocking collectives: 0 us -> 158 us
  waiting for transfers between devices: 127 us -> 30.5 us
  starting transfers between devices: 65.6 us -> 20.4 us
  matrix products: 34.1 us -> 7.59 us
  Pallas kernels: 17.4 us -> 23.2 us
  local copies, waits for them, and re-layouts: 7.98 us -> 3.73 us
    all_to_all x0 -> x2, blocking collectives: none -> 158 us  [the longest x1 79 us: on_device(): arrived = send(rows)]
    all_to_all x4 -> x0, waiting for transfers between devices: 102 us -> none  [the longest x1 34.7 us: on_device(): x = send(rows)]
    all_to_all x4 -> x0, starting transfers between devices: 33.2 us -> none  [the longest x1 8.93 us: on_device(): back_dx = send(route_dx)]
    dot_general x4 -> x0, matrix products: 17.2 us -> none  [the longest x1 5.75 us: on_device(): preact = jnp.dot(x, wi, preferred_element_type=F32)]
    pallas_call x0 -> x1, Pallas kernels: none -> 12.5 us  [on_device(): pl.pallas_call(expert_kernel, grid=(2,), in_specs=[source_block(0), sourc...]
    ppermute x9 -> x6, waiting for transfers between devices: 18.1 us -> 27.3 us  [swap_chips(): return lax.ppermute(v, 'zh', [(i, i ^ r) for i in range(4)])]
    ppermute x9 -> x6, starting transfers between devices: 21.1 us -> 12.1 us  [swap_chips(): return lax.ppermute(v, 'zh', [(i, i ^ r) for i in range(4)])]
    pallas_call x4 -> x2, Pallas kernels: 17.4 us -> 10.6 us  [run(): pl.pallas_call(kernel, grid_spec=pltpu.PrefetchScalarGridSpec(num_scalar_...]
  transfers between devices with their start and end apart: 28 -> 16, of which waited for: 16 -> 7; matrix products, arithmetic and copies ran while one was open for 15% -> 5% of each run, Pallas kernels for 6% -> 2%
where the time goes in v3:
time: 250 us; the launch traced here: 249 us
  blocking collectives  158 us (63%)
  waiting for transfers between devices  30.5 us (12%)
  Pallas kernels  23.2 us (9%)
  starting transfers between devices  20.4 us (8%)
  matrix products  7.59 us (3%)
  other arithmetic  4.99 us (2%)
  local copies, waits for them, and re-layouts  3.73 us (1%)
    all_to_all x1, blocking collectives, on_device(): arrived = send(rows)  79 us
    all_to_all x1, blocking collectives, on_device(): back = send(results)  78.7 us
    ppermute x6, waiting for transfers between devices, swap_chips(): return lax.ppermute(v, 'zh', [(i, i ^ r) for i in range(4)])  27.3 us
    pallas_call x1, Pallas kernels, on_device(): pl.pallas_call(expert_kernel, grid=(2,), in_specs=[source_block(0), sourc...  12.5 us
    ppermute x6, starting transfers between devices, swap_chips(): return lax.ppermute(v, 'zh', [(i, i ^ r) for i in range(4)])  12.1 us
    pallas_call x2, Pallas kernels, run(): pl.pallas_call(kernel, grid_spec=pltpu.PrefetchScalarGridSpec(num_scalar_...  10.6 us
    ppermute x10, starting transfers between devices, swap_cores(): return lax.ppermute(v, 'core', CORES)  8.24 us
  transfers between devices with their start and end apart: 16, of which 7 were waited for; matrix products, arithmetic and copies ran while one was open for 5% of the time, Pallas kernels for 2%

profile of v3, /device:TPU:65, one launch (start us, length us, event | category | flops | bytes accessed | tf_op | source)
XLA Modules:
  0.0 248.9 jit_solution(5759992101981127038)
XLA Ops:
  0.6 0.8 collective-permute-start.7
  1.4 0.1 collective-permute-start.8
  1.5 1.0 pad_maximum_fusion.3.refs_0_
  2.5 1.2 collective-permute-start
  3.7 5.2 %collective-permute-start.1 = (bf16[2,128,384]{2,1,0:T(8,128)(2,1)S(1)}, bf16[2,128,384]{2,1,0:T(8,128)(2,1)S(1)}, u32[]{:S(2)}, u32[]{:S(2)}) collective-permute-start(bf16[2,128,384]{2,1,0:T(8,128)(2,1)S(1)} %pad_maximum_fusion.3.refs_0_), channel_id=1, source_target_pairs={{0,4},{2,6},{4,0},{6,2},{1,5},{3,7},{5,1},{7,3},{8,12},{10,14},{12... | collective-permute-start | bytes 589832 | tf_op jit(solution)/shard_map/ppermute | solution.py:32
  8.8 0.0 collective-permute-start.2
  8.8 0.7 fusion.31
  9.5 0.2 fusion.32
  9.7 0.7 select_reduce_fusion
  10.5 0.1 copy.48
  10.6 0.1 copy.49
  10.7 0.7 multiply_add_fusion
  11.4 0.1 copy.50
  11.5 8.2 %collective-permute-done.refs_1_ = bf16[2,128,384]{2,1,0:T(8,128)(2,1)S(1)} collective-permute-done((bf16[2,128,384]{2,1,0:T(8,128)(2,1)S(1)}, bf16[2,128,384]{2,1,0:T(8,128)(2,1)S(1)}, u32[]{:S(2)}, u32[]{:S(2)}) %collective-permute-start) | collective-permute-done | bytes 196640 | tf_op jit(solution)/shard_map/ppermute | solution.py:32
  19.7 0.7 collective-permute-start.3
  20.5 0.1 copy.51.qt_ref
  20.5 0.8 copy.52
  21.3 0.0 collective-permute-done.1.refs_2_
  21.4 1.6 collective-permute-start.4
  22.9 2.6 %collective-permute-done.2.refs_3_ = bf16[2,128,384]{2,1,0:T(8,128)(2,1)S(1)} collective-permute-done((bf16[2,128,384]{2,1,0:T(8,128)(2,1)S(1)}, bf16[2,128,384]{2,1,0:T(8,128)(2,1)S(1)}, u32[]{:S(2)}, u32[]{:S(2)}) %collective-permute-start.2) | collective-permute-done | bytes 196640 | tf_op jit(solution)/shard_map/ppermute | solution.py:32
  25.5 2.6 %collective-permute-start.5 = (bf16[2,128,384]{2,1,0:T(8,128)(2,1)S(1)}, bf16[2,128,384]{2,1,0:T(8,128)(2,1)S(1)}, u32[]{:S(2)}, u32[]{:S(2)}) collective-permute-start(bf16[2,128,384]{2,1,0:T(8,128)(2,1)S(1)} %collective-permute-done.1.refs_2_), channel_id=1, source_target_pairs={{0,1},{1,0},{2,3},{3,2},{4,5},{5,4},{6,7},{7,6},{8,9},{9,8},{10,11... | collective-permute-start | bytes 589832 | tf_op jit(solution)/shard_map/ppermute | solution.py:28
  28.1 0.0 collective-permute-done.3.refs_4_
  28.1 0.0 collective-permute-start.6
  28.1 0.1 pad_add_fusion.order
  28.2 0.0 collective-permute-done.4.refs_5_
  28.2 1.0 collective-permute-done.5.refs_6_
  29.1 0.4 collective-permute-done.6.refs_7_
  29.5 0.7 copy-done
  30.2 5.2 %shard_map.119 = (bf16[32,32,3072]{2,1,0:T(8,128)(2,1)S(1)}, bf16[128,3072]{1,0:T(8,128)(2,1)S(1)}, bf16[128,3072]{1,0:T(8,128)(2,1)S(1)}, f32[128,128]{1,0:T(8,128)S(1)}) custom-call(s32[5]{0:T(128)S(1)} %pad_add_fusion.order, s32[4,128]{1,0:T(4,128)S(1)} %copy.51.qt_ref, f32[4,128]{1,0:T(4,128)S(1)} %bitcast.30, ...), custom_call_target="tpu_custom_call" | custom-call | flops 805306368 | bytes 6291456 | tf_op jit(solution)/shard_map/pallas_call | solution.py:209
  35.4 0.0 collective-permute-done.7.wi_b
  35.4 0.0 collective-permute-done.8.wo_b
  35.4 79.0 %all_to_all.10.x_ref.g_ref = bf16[32,32,3072]{2,1,0:T(8,128)(2,1)} all-to-all(bf16[32,32,3072]{2,1,0:T(8,128)(2,1)S(1)} %get-tuple-element.33), channel_id=1, replica_groups=mesh['y'=4,'zl'=2,'x'=4,'zh'=4,'core'=2] {'y','zl','x'}, dimensions={0} | all-to-all | bytes 12582912 | tf_op jit(solution)/shard_map/all_to_all | solution.py:285
  114.4 12.5 %shard_map.120 = (bf16[32,32,3072]{2,1,0:T(8,128)(2,1)}, bf16[512,512]{1,0:T(8,128)(2,1)}, bf16[512,512]{1,0:T(8,128)(2,1)}) custom-call(bf16[32,32,3072]{2,1,0:T(8,128)(2,1)} %all_to_all.10.x_ref.g_ref, bf16[32,32,3072]{2,1,0:T(8,128)(2,1)} %all_to_all.10.x_ref.g_ref, bf16[3072,256]{1,0:T(8,128)(2,1)} %bitcast.43, ...), custom_call_target="tpu_custom_call" | custom-call | flops 6442450944 | bytes 18874368 | tf_op jit(solution)/shard_map/pallas_call | solution.py:298
  126.9 78.7 %all_to_all.11.out_rows.dx_rows = bf16[32,32,3072]{2,1,0:T(8,128)(2,1)S(1)} all-to-all(bf16[32,32,3072]{2,1,0:T(8,128)(2,1)} %get-tuple-element.36), channel_id=1, replica_groups=mesh['y'=4,'zl'=2,'x'=4,'zh'=4,'core'=2] {'y','zl','x'}, dimensions={0} | all-to-all | bytes 12582912 | tf_op jit(solution)/shard_map/all_to_all | solution.py:316
  205.6 5.5 %shard_map.121 = (bf16[4,128,768]{2,1,0:T(8,128)(2,1)S(1)}, bf16[4,128,768]{2,1,0:T(8,128)(2,1)S(1)}, bf16[128,128]{1,0:T(8,128)(2,1)S(1)}) custom-call(s32[5]{0:T(128)S(1)} %pad_add_fusion.order, s32[128,4]{1,0:T(8,128)S(1)} %fusion.34.q_ref, f32[128,128]{1,0:T(8,128)S(1)} %pad.8.g_ref, f32[128,128]{1,0:T(8,128)S(1)} %get-tuple-element.32.stats_ref, ...), custom_call_target="tpu_custom_call" | custom-call | flops 1610612736 | bytes 6291456 | tf_op jit(solution)/shard_map/pallas_call | solution.py:209
  211.0 1.8 collective-permute-start.9
  212.8 0.1 collective-permute-start.10
  212.9 1.9 collective-permute-done.10
  214.8 0.1 reduce-precision_convert_fusion.1
  214.9 0.1 fusion.37
  215.0 0.0 collective-permute-done.9
  215.0 0.1 fusion.14
  215.2 0.1 pad_maximum_fusion
  215.3 0.0 copy-start.3
  215.3 0.8 fusion.40
  216.1 0.2 copy-done.3
  216.3 1.0 convolution_convert_fusion.1
  217.4 0.5 collective-permute-start.14
  217.8 1.0 convolution_convert_fusion
  218.8 0.2 collective-permute-start.15
  219.0 0.2 slice_reduce_fusion.1
  219.2 1.1 collective-permute-start.11
  220.3 3.9 %collective-permute-start.12 = (bf16[128,896]{1,0:T(8,128)(2,1)S(1)}, bf16[128,896]{1,0:T(8,128)(2,1)S(1)}, u32[]{:S(2)}, u32[]{:S(2)}) collective-permute-start(bf16[128,896]{1,0:T(8,128)(2,1)S(1)} %get-tuple-element.45), channel_id=1, source_target_pairs={{0,4},{2,6},{4,0},{6,2},{1,5},{3,7},{5,1},{7,3},{8,12},{10,14},{12... | collective-permute-start | bytes 688136 | tf_op jit(solution)/shard_map/ppermute | solution.py:32
  224.2 0.8 collective-permute-start.13
  225.0 2.7 %convert_add_fusion.1 = f32[3072,256]{1,0:T(8,128)} fusion(bf16[3072,256]{1,0:T(8,128)(2,1)S(1)} %collective-permute-done.14, bf16[512,3072]{1,0:T(8,128)(2,1)S(1)} %bitcast.36, bf16[512,512]{1,0:T(8,128)(2,1)S(1)} %copy-done.3), kind=kOutput, calls=%fused_computation.3 | convolution fusion | flops 806879232 | bytes 8126464 | tf_op jit(solution)/shard_map/dot_general | solution.py:347
  227.7 0.0 collective-permute-done.15
  227.7 2.7 %convert_add_fusion = f32[256,3072]{1,0:T(8,128)} fusion(bf16[256,3072]{1,0:T(8,128)(2,1)S(1)} %collective-permute-done.15, bf16[512,3072]{1,0:T(8,128)(2,1)S(1)} %bitcast.32, bf16[512,512]{1,0:T(8,128)(2,1)S(1)} %copy-done.1), kind=kOutput, calls=%fused_computation.2 | convolution fusion | flops 806879232 | bytes 8126464 | tf_op jit(solution)/shard_map/dot_general | solution.py:342
  230.3 9.4 %collective-permute-done.11 = bf16[128,896]{1,0:T(8,128)(2,1)S(1)} collective-permute-done((bf16[128,896]{1,0:T(8,128)(2,1)S(1)}, bf16[128,896]{1,0:T(8,128)(2,1)S(1)}, u32[]{:S(2)}, u32[]{:S(2)}) %collective-permute-start.11) | collective-permute-done | bytes 229408 | tf_op jit(solution)/shard_map/ppermute | solution.py:32
  239.7 7.2 %collective-permute-done.13 = bf16[128,896]{1,0:T(8,128)(2,1)S(1)} collective-permute-done((bf16[128,896]{1,0:T(8,128)(2,1)S(1)}, bf16[128,896]{1,0:T(8,128)(2,1)S(1)}, u32[]{:S(2)}, u32[]{:S(2)}) %collective-permute-start.13) | collective-permute-done | bytes 229408 | tf_op jit(solution)/shard_map/ppermute | solution.py:32
  246.9 0.2 fusion.25
  247.1 0.2 fusion.23
  247.3 0.7 copy.53
  247.9 0.1 fusion.1
  248.1 0.8 fusion.18
  (26 shorter events, 0.2 us)
Async XLA Ops:
  0.6 34.7 %collective-permute-start.7 = (bf16[3072,256]{1,0:T(8,128)(2,1)}, bf16[3072,256]{1,0:T(8,128)(2,1)}, u32[]{:S(2)}, u32[]{:S(2)}) collective-permute-start(bf16[3072,256]{1,0:T(8,128)(2,1)} %bitcast.42), channel_id=1, source_target_pairs={{0,1},{1,0},{2,3},{3,2},{4,5},{5,4},{6,7},{7,6},{8,9},{9,8},{10,11... | collective-permute-start | bytes 4718600 | tf_op jit(solution)/shard_map/ppermute | solution.py:28
  1.4 34.0 %collective-permute-start.8 = (bf16[256,3072]{1,0:T(8,128)(2,1)}, bf16[256,3072]{1,0:T(8,128)(2,1)}, u32[]{:S(2)}, u32[]{:S(2)}) collective-permute-start(bf16[256,3072]{1,0:T(8,128)(2,1)} %bitcast.44), channel_id=1, source_target_pairs={{0,1},{1,0},{2,3},{3,2},{4,5},{5,4},{6,7},{7,6},{8,9},{9,8},{10,11... | collective-permute-start | bytes 4718600 | tf_op jit(solution)/shard_map/ppermute | solution.py:28
  2.5 17.2 %collective-permute-start = (bf16[2,128,384]{2,1,0:T(8,128)(2,1)S(1)}, bf16[2,128,384]{2,1,0:T(8,128)(2,1)S(1)}, u32[]{:S(2)}, u32[]{:S(2)}) collective-permute-start(bf16[2,128,384]{2,1,0:T(8,128)(2,1)S(1)} %pad_maximum_fusion.3.refs_0_), channel_id=1, source_target_pairs={{0,2},{2,0},{4,6},{6,4},{1,3},{3,1},{5,7},{7,5},{8,10},{10,8},{12,... | collective-permute-start | bytes 589832 | tf_op jit(solution)/shard_map/ppermute | solution.py:32
  3.7 17.7 %collective-permute-start.1 = (bf16[2,128,384]{2,1,0:T(8,128)(2,1)S(1)}, bf16[2,128,384]{2,1,0:T(8,128)(2,1)S(1)}, u32[]{:S(2)}, u32[]{:S(2)}) collective-permute-start(bf16[2,128,384]{2,1,0:T(8,128)(2,1)S(1)} %pad_maximum_fusion.3.refs_0_), channel_id=1, source_target_pairs={{0,4},{2,6},{4,0},{6,2},{1,5},{3,7},{5,1},{7,3},{8,12},{10,14},{12... | collective-permute-start | bytes 589832 | tf_op jit(solution)/shard_map/ppermute | solution.py:32
  8.8 16.7 %collective-permute-start.2 = (bf16[2,128,384]{2,1,0:T(8,128)(2,1)S(1)}, bf16[2,128,384]{2,1,0:T(8,128)(2,1)S(1)}, u32[]{:S(2)}, u32[]{:S(2)}) collective-permute-start(bf16[2,128,384]{2,1,0:T(8,128)(2,1)S(1)} %pad_maximum_fusion.3.refs_0_), channel_id=1, source_target_pairs={{0,6},{2,4},{4,2},{6,0},{1,7},{3,5},{5,3},{7,1},{8,14},{10,12},{12... | collective-permute-start | bytes 589832 | tf_op jit(solution)/shard_map/ppermute | solution.py:32
  19.7 8.4 %collective-permute-start.3 = (bf16[2,128,384]{2,1,0:T(8,128)(2,1)S(1)}, bf16[2,128,384]{2,1,0:T(8,128)(2,1)S(1)}, u32[]{:S(2)}, u32[]{:S(2)}) collective-permute-start(bf16[2,128,384]{2,1,0:T(8,128)(2,1)S(1)} %pad_maximum_fusion.3.refs_0_), channel_id=1, source_target_pairs={{0,1},{1,0},{2,3},{3,2},{4,5},{5,4},{6,7},{7,6},{8,9},{9,8},{10,11... | collective-permute-start | bytes 589832 | tf_op jit(solution)/shard_map/ppermute | solution.py:28
  21.4 6.8 %collective-permute-start.4 = (bf16[2,128,384]{2,1,0:T(8,128)(2,1)S(1)}, bf16[2,128,384]{2,1,0:T(8,128)(2,1)S(1)}, u32[]{:S(2)}, u32[]{:S(2)}) collective-permute-start(bf16[2,128,384]{2,1,0:T(8,128)(2,1)S(1)} %collective-permute-done.refs_1_), channel_id=1, source_target_pairs={{0,1},{1,0},{2,3},{3,2},{4,5},{5,4},{6,7},{7,6},{8,9},{9,8},{10,11... | collective-permute-start | bytes 589832 | tf_op jit(solution)/shard_map/ppermute | solution.py:28
  25.5 3.6 %collective-permute-start.5 = (bf16[2,128,384]{2,1,0:T(8,128)(2,1)S(1)}, bf16[2,128,384]{2,1,0:T(8,128)(2,1)S(1)}, u32[]{:S(2)}, u32[]{:S(2)}) collective-permute-start(bf16[2,128,384]{2,1,0:T(8,128)(2,1)S(1)} %collective-permute-done.1.refs_2_), channel_id=1, source_target_pairs={{0,1},{1,0},{2,3},{3,2},{4,5},{5,4},{6,7},{7,6},{8,9},{9,8},{10,11... | collective-permute-start | bytes 589832 | tf_op jit(solution)/shard_map/ppermute | solution.py:28
  28.1 1.4 collective-permute-start.6
  29.5 0.7 copy-start
  205.6 9.7 %slice-start = ((s8[6291456]{0:T(1024)(128)(4,1)}), s8[4194304]{0:T(1024)(128)(4,1)S(1)}, s32[]{:S(2)}) async-start(s8[6291456]{0:T(1024)(128)(4,1)} %bitcast.33), calls=%async_computation.2 | async-start | bytes 8388608
  205.6 9.7 %slice-start.1 = ((s8[6291456]{0:T(1024)(128)(4,1)}), s8[2097152]{0:T(1024)(128)(4,1)S(1)}, s32[]{:S(2)}) async-start(s8[6291456]{0:T(1024)(128)(4,1)} %bitcast.33), calls=%async_computation.3 | async-start | bytes 4194304
  211.0 4.0 %collective-permute-start.9 = (bf16[4,128,768]{2,1,0:T(8,128)(2,1)S(1)}, bf16[4,128,768]{2,1,0:T(8,128)(2,1)S(1)}, u32[]{:S(2)}, u32[]{:S(2)}) collective-permute-start(bf16[4,128,768]{2,1,0:T(8,128)(2,1)S(1)} %get-tuple-element.40), channel_id=1, source_target_pairs={{0,1},{1,0},{2,3},{3,2},{4,5},{5,4},{6,7},{7,6},{8,9},{9,8},{10,11... | collective-permute-start | bytes 2359304 | tf_op jit(solution)/shard_map/ppermute | solution.py:28
  212.8 2.0 collective-permute-start.10
  215.3 1.0 copy-start.3
  216.3 1.5 copy-start.1
  217.4 7.6 %collective-permute-start.14 = (bf16[3072,256]{1,0:T(8,128)(2,1)S(1)}, bf16[3072,256]{1,0:T(8,128)(2,1)S(1)}, u32[]{:S(2)}, u32[]{:S(2)}) collective-permute-start(bf16[3072,256]{1,0:T(8,128)(2,1)S(1)} %convolution_convert_fusion.1), channel_id=1, source_target_pairs={{0,1},{1,0},{2,3},{3,2},{4,5},{5,4},{6,7},{7,6},{8,9},{9,8},{10,11... | collective-permute-start | bytes 4718600 | tf_op jit(solution)/shard_map/ppermute | solution.py:28
  218.8 8.9 %collective-permute-start.15 = (bf16[256,3072]{1,0:T(8,128)(2,1)S(1)}, bf16[256,3072]{1,0:T(8,128)(2,1)S(1)}, u32[]{:S(2)}, u32[]{:S(2)}) collective-permute-start(bf16[256,3072]{1,0:T(8,128)(2,1)S(1)} %convolution_convert_fusion), channel_id=1, source_target_pairs={{0,1},{1,0},{2,3},{3,2},{4,5},{5,4},{6,7},{7,6},{8,9},{9,8},{10,11... | collective-permute-start | bytes 4718600 | tf_op jit(solution)/shard_map/ppermute | solution.py:28
  219.2 20.5 %collective-permute-start.11 = (bf16[128,896]{1,0:T(8,128)(2,1)S(1)}, bf16[128,896]{1,0:T(8,128)(2,1)S(1)}, u32[]{:S(2)}, u32[]{:S(2)}) collective-permute-start(bf16[128,896]{1,0:T(8,128)(2,1)S(1)} %get-tuple-element.44), channel_id=1, source_target_pairs={{0,2},{2,0},{4,6},{6,4},{1,3},{3,1},{5,7},{7,5},{8,10},{10,8},{12,... | collective-permute-start | bytes 688136 | tf_op jit(solution)/shard_map/ppermute | solution.py:32
  220.3 19.4 %collective-permute-start.12 = (bf16[128,896]{1,0:T(8,128)(2,1)S(1)}, bf16[128,896]{1,0:T(8,128)(2,1)S(1)}, u32[]{:S(2)}, u32[]{:S(2)}) collective-permute-start(bf16[128,896]{1,0:T(8,128)(2,1)S(1)} %get-tuple-element.45), channel_id=1, source_target_pairs={{0,4},{2,6},{4,0},{6,2},{1,5},{3,7},{5,1},{7,3},{8,12},{10,14},{12... | collective-permute-start | bytes 688136 | tf_op jit(solution)/shard_map/ppermute | solution.py:32
  224.2 22.7 %collective-permute-start.13 = (bf16[128,896]{1,0:T(8,128)(2,1)S(1)}, bf16[128,896]{1,0:T(8,128)(2,1)S(1)}, u32[]{:S(2)}, u32[]{:S(2)}) collective-permute-start(bf16[128,896]{1,0:T(8,128)(2,1)S(1)} %get-tuple-element.46), channel_id=1, source_target_pairs={{0,6},{2,4},{4,2},{6,0},{1,7},{3,5},{5,3},{7,1},{8,14},{10,12},{12... | collective-permute-start | bytes 688136 | tf_op jit(solution)/shard_map/ppermute | solution.py:32
  227.7 20.4 %copy-start.2 = (bf16[128,384]{1,0:T(8,128)(2,1)S(1)}, bf16[128,384]{1,0:T(8,128)(2,1)}, u32[]{:S(2)}) copy-start(bf16[128,384]{1,0:T(8,128)(2,1)} %param.8) | copy-start | bytes 294916
  227.7 20.4 %copy-start.4 = (bf16[128,384]{1,0:T(8,128)(2,1)S(1)}, bf16[128,384]{1,0:T(8,128)(2,1)}, u32[]{:S(2)}) copy-start(bf16[128,384]{1,0:T(8,128)(2,1)} %param.10) | copy-start | bytes 294916
  227.7 20.4 %copy-start.5 = (bf16[128,384]{1,0:T(8,128)(2,1)S(1)}, bf16[128,384]{1,0:T(8,128)(2,1)}, u32[]{:S(2)}) copy-start(bf16[128,384]{1,0:T(8,128)(2,1)} %param.9) | copy-start | bytes 294916

commit v4 on v3

--- a/solution.py
+++ b/solution.py
@@ -307,7 +307,7 @@
         ),
         out_shape=(rows_shape, unit_shape, unit_shape),
         compiler_params=pltpu.CompilerParams(
-            dimension_semantics=("arbitrary",), vmem_limit_bytes=60 * 2**20
+            dimension_semantics=("arbitrary",), vmem_limit_bytes=32 * 2**20
         ),
         cost_estimate=pl.CostEstimate(
             flops=16 * slots * own * width, bytes_accessed=12 * slots * width, transcendentals=0

time: 250 us -> 245 us (0.980)
  Pallas kernels: 23.2 us -> 19.4 us
    pallas_call x1, Pallas kernels: 12.5 us -> 8.76 us  [on_device(): pl.pallas_call(expert_kernel, grid=(2,), in_specs=[source_block(0), sourc...]
where the time goes in v4:
time: 245 us
  blocking collectives  158 us (64%)
  waiting for transfers between devices  30.5 us (12%)
  starting transfers between devices  20.4 us (8%)
  Pallas kernels  19.4 us (8%)
  matrix products  7.59 us (3%)
  other arithmetic  4.99 us (2%)
  local copies, waits for them, and re-layouts  3.35 us (1%)
    all_to_all x1, blocking collectives, on_device(): arrived = send(rows)  79.2 us
    all_to_all x1, blocking collectives, on_device(): back = send(results)  78.5 us
    ppermute x6, waiting for transfers between devices, swap_chips(): return lax.ppermute(v, 'zh', [(i, i ^ r) for i in range(4)])  27.3 us
    ppermute x6, starting transfers between devices, swap_chips(): return lax.ppermute(v, 'zh', [(i, i ^ r) for i in range(4)])  12.1 us
    pallas_call x2, Pallas kernels, run(): pl.pallas_call(kernel, grid_spec=pltpu.PrefetchScalarGridSpec(num_scalar_...  10.6 us
    pallas_call x1, Pallas kernels, on_device(): pl.pallas_call(expert_kernel, grid=(2,), in_specs=[source_block(0), sourc...  8.76 us
    ppermute x10, starting transfers between devices, swap_cores(): return lax.ppermute(v, 'core', CORES)  8.24 us
  transfers between devices with their start and end apart: 16, of which 7 were waited for; matrix products, arithmetic and copies ran while one was open for 5% of the time, Pallas kernels for 2%

profile of v4, /device:TPU:65, one launch (start us, length us, event | category | flops | bytes accessed | tf_op | source)
XLA Modules:
  0.0 244.7 jit_solution(12786832529946878528)
XLA Ops:
  0.6 0.8 collective-permute-start.7
  1.4 0.1 collective-permute-start.8
  1.5 1.0 pad_maximum_fusion.3.refs_0_
  2.5 1.2 collective-permute-start
  3.7 5.2 %collective-permute-start.1 = (bf16[2,128,384]{2,1,0:T(8,128)(2,1)S(1)}, bf16[2,128,384]{2,1,0:T(8,128)(2,1)S(1)}, u32[]{:S(2)}, u32[]{:S(2)}) collective-permute-start(bf16[2,128,384]{2,1,0:T(8,128)(2,1)S(1)} %pad_maximum_fusion.3.refs_0_), channel_id=1, source_target_pairs={{0,4},{2,6},{4,0},{6,2},{1,5},{3,7},{5,1},{7,3},{8,12},{10,14},{12... | collective-permute-start | bytes 589832 | tf_op jit(solution)/shard_map/ppermute | solution.py:32
  8.8 0.0 collective-permute-start.2
  8.8 0.7 fusion.31
  9.5 0.2 fusion.32
  9.7 0.7 select_reduce_fusion
  10.5 0.1 copy.48
  10.6 0.1 copy.49
  10.7 0.7 multiply_add_fusion
  11.4 0.1 copy.50
  11.5 8.2 %collective-permute-done.refs_1_ = bf16[2,128,384]{2,1,0:T(8,128)(2,1)S(1)} collective-permute-done((bf16[2,128,384]{2,1,0:T(8,128)(2,1)S(1)}, bf16[2,128,384]{2,1,0:T(8,128)(2,1)S(1)}, u32[]{:S(2)}, u32[]{:S(2)}) %collective-permute-start) | collective-permute-done | bytes 196640 | tf_op jit(solution)/shard_map/ppermute | solution.py:32
  19.7 0.7 collective-permute-start.3
  20.5 0.1 copy.51.qt_ref
  20.5 0.8 copy.52
  21.3 0.0 collective-permute-done.1.refs_2_
  21.4 1.6 collective-permute-start.4
  22.9 2.6 %collective-permute-done.2.refs_3_ = bf16[2,128,384]{2,1,0:T(8,128)(2,1)S(1)} collective-permute-done((bf16[2,128,384]{2,1,0:T(8,128)(2,1)S(1)}, bf16[2,128,384]{2,1,0:T(8,128)(2,1)S(1)}, u32[]{:S(2)}, u32[]{:S(2)}) %collective-permute-start.2) | collective-permute-done | bytes 196640 | tf_op jit(solution)/shard_map/ppermute | solution.py:32
  25.5 2.6 %collective-permute-start.5 = (bf16[2,128,384]{2,1,0:T(8,128)(2,1)S(1)}, bf16[2,128,384]{2,1,0:T(8,128)(2,1)S(1)}, u32[]{:S(2)}, u32[]{:S(2)}) collective-permute-start(bf16[2,128,384]{2,1,0:T(8,128)(2,1)S(1)} %collective-permute-done.1.refs_2_), channel_id=1, source_target_pairs={{0,1},{1,0},{2,3},{3,2},{4,5},{5,4},{6,7},{7,6},{8,9},{9,8},{10,11... | collective-permute-start | bytes 589832 | tf_op jit(solution)/shard_map/ppermute | solution.py:28
  28.1 0.0 collective-permute-done.3.refs_4_
  28.1 0.0 collective-permute-start.6
  28.1 0.1 pad_add_fusion.order
  28.2 0.0 collective-permute-done.4.refs_5_
  28.2 1.0 collective-permute-done.5.refs_6_
  29.1 0.4 collective-permute-done.6.refs_7_
  29.5 0.7 copy-done
  30.2 5.2 %shard_map.119 = (bf16[32,32,3072]{2,1,0:T(8,128)(2,1)S(1)}, bf16[128,3072]{1,0:T(8,128)(2,1)S(1)}, bf16[128,3072]{1,0:T(8,128)(2,1)S(1)}, f32[128,128]{1,0:T(8,128)S(1)}) custom-call(s32[5]{0:T(128)S(1)} %pad_add_fusion.order, s32[4,128]{1,0:T(4,128)S(1)} %copy.51.qt_ref, f32[4,128]{1,0:T(4,128)S(1)} %bitcast.30, ...), custom_call_target="tpu_custom_call" | custom-call | flops 805306368 | bytes 6291456 | tf_op jit(solution)/shard_map/pallas_call | solution.py:209
  35.4 0.0 collective-permute-done.7.wi_b
  35.4 0.0 collective-permute-done.8.wo_b
  35.4 0.0 copy-start.1
  35.4 0.0 copy-start.2
  35.4 79.2 %all_to_all.10.x_ref.g_ref = bf16[32,32,3072]{2,1,0:T(8,128)(2,1)S(1)} all-to-all(bf16[32,32,3072]{2,1,0:T(8,128)(2,1)S(1)} %get-tuple-element.33), channel_id=1, replica_groups=mesh['y'=4,'zl'=2,'x'=4,'zh'=4,'core'=2] {'y','zl','x'}, dimensions={0} | all-to-all | bytes 12582912 | tf_op jit(solution)/shard_map/all_to_all | solution.py:285
  114.6 8.8 %shard_map.120 = (bf16[32,32,3072]{2,1,0:T(8,128)(2,1)S(1)}, bf16[512,512]{1,0:T(8,128)(2,1)S(1)}, bf16[512,512]{1,0:T(8,128)(2,1)S(1)}) custom-call(bf16[32,32,3072]{2,1,0:T(8,128)(2,1)S(1)} %all_to_all.10.x_ref.g_ref, bf16[32,32,3072]{2,1,0:T(8,128)(2,1)S(1)} %all_to_all.10.x_ref.g_ref, bf16[3072,256]{1,0:T(8,128)(2,1)S(1)} %bitcast.32, ...), custom_call_target="tpu_custom_call" | custom-call | flops 6442450944 | bytes 18874368 | tf_op jit(solution)/shard_map/pallas_call | solution.py:298
  123.3 78.5 %all_to_all.11.out_rows.dx_rows = bf16[32,32,3072]{2,1,0:T(8,128)(2,1)S(1)} all-to-all(bf16[32,32,3072]{2,1,0:T(8,128)(2,1)S(1)} %get-tuple-element.36), channel_id=1, replica_groups=mesh['y'=4,'zl'=2,'x'=4,'zh'=4,'core'=2] {'y','zl','x'}, dimensions={0} | all-to-all | bytes 12582912 | tf_op jit(solution)/shard_map/all_to_all | solution.py:316
  201.8 5.5 %shard_map.121 = (bf16[4,128,768]{2,1,0:T(8,128)(2,1)S(1)}, bf16[4,128,768]{2,1,0:T(8,128)(2,1)S(1)}, bf16[128,128]{1,0:T(8,128)(2,1)S(1)}) custom-call(s32[5]{0:T(128)S(1)} %pad_add_fusion.order, s32[128,4]{1,0:T(8,128)S(1)} %fusion.34.q_ref, f32[128,128]{1,0:T(8,128)S(1)} %pad.8.g_ref, f32[128,128]{1,0:T(8,128)S(1)} %get-tuple-element.32.stats_ref, ...), custom_call_target="tpu_custom_call" | custom-call | flops 1610612736 | bytes 6291456 | tf_op jit(solution)/shard_map/pallas_call | solution.py:209
  207.3 1.7 collective-permute-start.9
  209.0 0.1 collective-permute-start.10
  209.1 1.9 collective-permute-done.10
  211.0 0.1 reduce-precision_convert_fusion.1
  211.2 0.1 fusion.37
  211.3 0.0 collective-permute-done.9
  211.3 0.1 fusion.14
  211.4 0.1 pad_maximum_fusion
  211.5 0.6 fusion.40
  212.1 1.0 convolution_convert_fusion.1
  213.2 0.5 collective-permute-start.14
  213.6 1.0 convolution_convert_fusion
  214.6 0.2 collective-permute-start.15
  214.8 0.2 slice_reduce_fusion.1
  215.0 1.1 collective-permute-start.11
  216.2 3.8 %collective-permute-start.12 = (bf16[128,896]{1,0:T(8,128)(2,1)S(1)}, bf16[128,896]{1,0:T(8,128)(2,1)S(1)}, u32[]{:S(2)}, u32[]{:S(2)}) collective-permute-start(bf16[128,896]{1,0:T(8,128)(2,1)S(1)} %get-tuple-element.45), channel_id=1, source_target_pairs={{0,4},{2,6},{4,0},{6,2},{1,5},{3,7},{5,1},{7,3},{8,12},{10,14},{12... | collective-permute-start | bytes 688136 | tf_op jit(solution)/shard_map/ppermute | solution.py:32
  219.9 0.8 collective-permute-start.13
  220.8 2.7 %convert_add_fusion.1 = f32[3072,256]{1,0:T(8,128)} fusion(bf16[3072,256]{1,0:T(8,128)(2,1)S(1)} %collective-permute-done.14, bf16[512,3072]{1,0:T(8,128)(2,1)S(1)} %bitcast.38, bf16[512,512]{1,0:T(8,128)(2,1)S(1)} %get-tuple-element.48), kind=kOutput, calls=%fused_computation.3 | convolution fusion | flops 806879232 | bytes 8126464 | tf_op jit(solution)/shard_map/dot_general | solution.py:347
  223.5 0.0 collective-permute-done.15
  223.5 2.7 %convert_add_fusion = f32[256,3072]{1,0:T(8,128)} fusion(bf16[256,3072]{1,0:T(8,128)(2,1)S(1)} %collective-permute-done.15, bf16[512,3072]{1,0:T(8,128)(2,1)S(1)} %bitcast.36, bf16[512,512]{1,0:T(8,128)(2,1)S(1)} %get-tuple-element.49), kind=kOutput, calls=%fused_computation.2 | convolution fusion | flops 806879232 | bytes 8126464 | tf_op jit(solution)/shard_map/dot_general | solution.py:342
  226.1 9.4 %collective-permute-done.11 = bf16[128,896]{1,0:T(8,128)(2,1)S(1)} collective-permute-done((bf16[128,896]{1,0:T(8,128)(2,1)S(1)}, bf16[128,896]{1,0:T(8,128)(2,1)S(1)}, u32[]{:S(2)}, u32[]{:S(2)}) %collective-permute-start.11) | collective-permute-done | bytes 229408 | tf_op jit(solution)/shard_map/ppermute | solution.py:32
  235.6 7.1 %collective-permute-done.13 = bf16[128,896]{1,0:T(8,128)(2,1)S(1)} collective-permute-done((bf16[128,896]{1,0:T(8,128)(2,1)S(1)}, bf16[128,896]{1,0:T(8,128)(2,1)S(1)}, u32[]{:S(2)}, u32[]{:S(2)}) %collective-permute-start.13) | collective-permute-done | bytes 229408 | tf_op jit(solution)/shard_map/ppermute | solution.py:32
  242.7 0.2 fusion.25
  242.9 0.2 fusion.23
  243.1 0.7 copy.53
  243.7 0.1 fusion.1
  243.9 0.8 fusion.18
  (21 shorter events, 0.2 us)
Async XLA Ops:
  0.6 34.7 %collective-permute-start.7 = (bf16[3072,256]{1,0:T(8,128)(2,1)}, bf16[3072,256]{1,0:T(8,128)(2,1)S(1)}, u32[]{:S(2)}, u32[]{:S(2)}) collective-permute-start(bf16[3072,256]{1,0:T(8,128)(2,1)} %bitcast.31), channel_id=1, source_target_pairs={{0,1},{1,0},{2,3},{3,2},{4,5},{5,4},{6,7},{7,6},{8,9},{9,8},{10,11... | collective-permute-start | bytes 4718600 | tf_op jit(solution)/shard_map/ppermute | solution.py:28
  1.4 34.0 %collective-permute-start.8 = (bf16[256,3072]{1,0:T(8,128)(2,1)}, bf16[256,3072]{1,0:T(8,128)(2,1)}, u32[]{:S(2)}, u32[]{:S(2)}) collective-permute-start(bf16[256,3072]{1,0:T(8,128)(2,1)} %bitcast.33), channel_id=1, source_target_pairs={{0,1},{1,0},{2,3},{3,2},{4,5},{5,4},{6,7},{7,6},{8,9},{9,8},{10,11... | collective-permute-start | bytes 4718600 | tf_op jit(solution)/shard_map/ppermute | solution.py:28
  2.5 17.2 %collective-permute-start = (bf16[2,128,384]{2,1,0:T(8,128)(2,1)S(1)}, bf16[2,128,384]{2,1,0:T(8,128)(2,1)S(1)}, u32[]{:S(2)}, u32[]{:S(2)}) collective-permute-start(bf16[2,128,384]{2,1,0:T(8,128)(2,1)S(1)} %pad_maximum_fusion.3.refs_0_), channel_id=1, source_target_pairs={{0,2},{2,0},{4,6},{6,4},{1,3},{3,1},{5,7},{7,5},{8,10},{10,8},{12,... | collective-permute-start | bytes 589832 | tf_op jit(solution)/shard_map/ppermute | solution.py:32
  3.7 17.7 %collective-permute-start.1 = (bf16[2,128,384]{2,1,0:T(8,128)(2,1)S(1)}, bf16[2,128,384]{2,1,0:T(8,128)(2,1)S(1)}, u32[]{:S(2)}, u32[]{:S(2)}) collective-permute-start(bf16[2,128,384]{2,1,0:T(8,128)(2,1)S(1)} %pad_maximum_fusion.3.refs_0_), channel_id=1, source_target_pairs={{0,4},{2,6},{4,0},{6,2},{1,5},{3,7},{5,1},{7,3},{8,12},{10,14},{12... | collective-permute-start | bytes 589832 | tf_op jit(solution)/shard_map/ppermute | solution.py:32
  8.8 16.7 %collective-permute-start.2 = (bf16[2,128,384]{2,1,0:T(8,128)(2,1)S(1)}, bf16[2,128,384]{2,1,0:T(8,128)(2,1)S(1)}, u32[]{:S(2)}, u32[]{:S(2)}) collective-permute-start(bf16[2,128,384]{2,1,0:T(8,128)(2,1)S(1)} %pad_maximum_fusion.3.refs_0_), channel_id=1, source_target_pairs={{0,6},{2,4},{4,2},{6,0},{1,7},{3,5},{5,3},{7,1},{8,14},{10,12},{12... | collective-permute-start | bytes 589832 | tf_op jit(solution)/shard_map/ppermute | solution.py:32
  19.7 8.4 %collective-permute-start.3 = (bf16[2,128,384]{2,1,0:T(8,128)(2,1)S(1)}, bf16[2,128,384]{2,1,0:T(8,128)(2,1)S(1)}, u32[]{:S(2)}, u32[]{:S(2)}) collective-permute-start(bf16[2,128,384]{2,1,0:T(8,128)(2,1)S(1)} %pad_maximum_fusion.3.refs_0_), channel_id=1, source_target_pairs={{0,1},{1,0},{2,3},{3,2},{4,5},{5,4},{6,7},{7,6},{8,9},{9,8},{10,11... | collective-permute-start | bytes 589832 | tf_op jit(solution)/shard_map/ppermute | solution.py:28
  21.4 6.8 %collective-permute-start.4 = (bf16[2,128,384]{2,1,0:T(8,128)(2,1)S(1)}, bf16[2,128,384]{2,1,0:T(8,128)(2,1)S(1)}, u32[]{:S(2)}, u32[]{:S(2)}) collective-permute-start(bf16[2,128,384]{2,1,0:T(8,128)(2,1)S(1)} %collective-permute-done.refs_1_), channel_id=1, source_target_pairs={{0,1},{1,0},{2,3},{3,2},{4,5},{5,4},{6,7},{7,6},{8,9},{9,8},{10,11... | collective-permute-start | bytes 589832 | tf_op jit(solution)/shard_map/ppermute | solution.py:28
  25.5 3.6 %collective-permute-start.5 = (bf16[2,128,384]{2,1,0:T(8,128)(2,1)S(1)}, bf16[2,128,384]{2,1,0:T(8,128)(2,1)S(1)}, u32[]{:S(2)}, u32[]{:S(2)}) collective-permute-start(bf16[2,128,384]{2,1,0:T(8,128)(2,1)S(1)} %collective-permute-done.1.refs_2_), channel_id=1, source_target_pairs={{0,1},{1,0},{2,3},{3,2},{4,5},{5,4},{6,7},{7,6},{8,9},{9,8},{10,11... | collective-permute-start | bytes 589832 | tf_op jit(solution)/shard_map/ppermute | solution.py:28
  28.1 1.4 collective-permute-start.6
  29.5 0.7 copy-start
  35.4 79.2 %copy-start.1 = (bf16[1,3072,256]{2,1,0:T(8,128)(2,1)S(1)}, bf16[1,3072,256]{2,1,0:T(8,128)(2,1)}, u32[]{:S(2)}) copy-start(bf16[1,3072,256]{2,1,0:T(8,128)(2,1)} %param.14) | copy-start | bytes 4718596
  35.4 79.2 %copy-start.2 = (bf16[1,256,3072]{2,1,0:T(8,128)(2,1)S(1)}, bf16[1,256,3072]{2,1,0:T(8,128)(2,1)}, u32[]{:S(2)}) copy-start(bf16[1,256,3072]{2,1,0:T(8,128)(2,1)} %param.15) | copy-start | bytes 4718596
  207.3 4.0 %collective-permute-start.9 = (bf16[4,128,768]{2,1,0:T(8,128)(2,1)S(1)}, bf16[4,128,768]{2,1,0:T(8,128)(2,1)S(1)}, u32[]{:S(2)}, u32[]{:S(2)}) collective-permute-start(bf16[4,128,768]{2,1,0:T(8,128)(2,1)S(1)} %get-tuple-element.40), channel_id=1, source_target_pairs={{0,1},{1,0},{2,3},{3,2},{4,5},{5,4},{6,7},{7,6},{8,9},{9,8},{10,11... | collective-permute-start | bytes 2359304 | tf_op jit(solution)/shard_map/ppermute | solution.py:28
  209.0 2.0 collective-permute-start.10
  213.2 7.6 %collective-permute-start.14 = (bf16[3072,256]{1,0:T(8,128)(2,1)S(1)}, bf16[3072,256]{1,0:T(8,128)(2,1)S(1)}, u32[]{:S(2)}, u32[]{:S(2)}) collective-permute-start(bf16[3072,256]{1,0:T(8,128)(2,1)S(1)} %convolution_convert_fusion.1), channel_id=1, source_target_pairs={{0,1},{1,0},{2,3},{3,2},{4,5},{5,4},{6,7},{7,6},{8,9},{9,8},{10,11... | collective-permute-start | bytes 4718600 | tf_op jit(solution)/shard_map/ppermute | solution.py:28
  214.6 8.8 %collective-permute-start.15 = (bf16[256,3072]{1,0:T(8,128)(2,1)S(1)}, bf16[256,3072]{1,0:T(8,128)(2,1)S(1)}, u32[]{:S(2)}, u32[]{:S(2)}) collective-permute-start(bf16[256,3072]{1,0:T(8,128)(2,1)S(1)} %convolution_convert_fusion), channel_id=1, source_target_pairs={{0,1},{1,0},{2,3},{3,2},{4,5},{5,4},{6,7},{7,6},{8,9},{9,8},{10,11... | collective-permute-start | bytes 4718600 | tf_op jit(solution)/shard_map/ppermute | solution.py:28
  215.0 20.5 %collective-permute-start.11 = (bf16[128,896]{1,0:T(8,128)(2,1)S(1)}, bf16[128,896]{1,0:T(8,128)(2,1)S(1)}, u32[]{:S(2)}, u32[]{:S(2)}) collective-permute-start(bf16[128,896]{1,0:T(8,128)(2,1)S(1)} %get-tuple-element.44), channel_id=1, source_target_pairs={{0,2},{2,0},{4,6},{6,4},{1,3},{3,1},{5,7},{7,5},{8,10},{10,8},{12,... | collective-permute-start | bytes 688136 | tf_op jit(solution)/shard_map/ppermute | solution.py:32
  216.2 19.4 %collective-permute-start.12 = (bf16[128,896]{1,0:T(8,128)(2,1)S(1)}, bf16[128,896]{1,0:T(8,128)(2,1)S(1)}, u32[]{:S(2)}, u32[]{:S(2)}) collective-permute-start(bf16[128,896]{1,0:T(8,128)(2,1)S(1)} %get-tuple-element.45), channel_id=1, source_target_pairs={{0,4},{2,6},{4,0},{6,2},{1,5},{3,7},{5,1},{7,3},{8,12},{10,14},{12... | collective-permute-start | bytes 688136 | tf_op jit(solution)/shard_map/ppermute | solution.py:32
  219.9 22.8 %collective-permute-start.13 = (bf16[128,896]{1,0:T(8,128)(2,1)S(1)}, bf16[128,896]{1,0:T(8,128)(2,1)S(1)}, u32[]{:S(2)}, u32[]{:S(2)}) collective-permute-start(bf16[128,896]{1,0:T(8,128)(2,1)S(1)} %get-tuple-element.46), channel_id=1, source_target_pairs={{0,6},{2,4},{4,2},{6,0},{1,7},{3,5},{5,3},{7,1},{8,14},{10,12},{12... | collective-permute-start | bytes 688136 | tf_op jit(solution)/shard_map/ppermute | solution.py:32
  223.5 20.4 %copy-start.3 = (bf16[128,384]{1,0:T(8,128)(2,1)S(1)}, bf16[128,384]{1,0:T(8,128)(2,1)}, u32[]{:S(2)}) copy-start(bf16[128,384]{1,0:T(8,128)(2,1)} %param.8) | copy-start | bytes 294916
  223.5 20.4 %copy-start.4 = (bf16[128,384]{1,0:T(8,128)(2,1)S(1)}, bf16[128,384]{1,0:T(8,128)(2,1)}, u32[]{:S(2)}) copy-start(bf16[128,384]{1,0:T(8,128)(2,1)} %param.10) | copy-start | bytes 294916
  223.5 20.4 %copy-start.5 = (bf16[128,384]{1,0:T(8,128)(2,1)S(1)}, bf16[128,384]{1,0:T(8,128)(2,1)}, u32[]{:S(2)}) copy-start(bf16[128,384]{1,0:T(8,128)(2,1)} %param.9) | copy-start | bytes 294916

commit v5 on v4

--- a/solution.py
+++ b/solution.py
@@ -285,19 +285,21 @@
     arrived = send(rows)
 
     own = wo.shape[0]
-    step_rows = experts // 2
+    step_rows = experts
 
     def source_block(n):
-        return pl.BlockSpec((step_rows, half, width), lambda i: (i, n, 0))
+        return pl.BlockSpec(
+            (step_rows, half, width), lambda i: (i, n, 0), pipeline_mode=pl.Buffered(1)
+        )
 
     def fixed(shape):
-        return pl.BlockSpec(shape, lambda i: (0, 0))
+        return pl.BlockSpec(shape, lambda i: (0, 0), pipeline_mode=pl.Buffered(1))
 
     unit_block = pl.BlockSpec((step_rows * half, 2 * own), lambda i: (i, 0))
     unit_shape = jax.ShapeDtypeStruct((slots, 2 * own), BF16)
     results, hidden, grad_pre = pl.pallas_call(
         expert_kernel,
-        grid=(2,),
+        grid=(1,),
         in_specs=[
             source_block(0), source_block(1),
             fixed((width, own)), fixed((width, own)), fixed((own, width)), fixed((own, width)),

time: 245 us -> 246 us (level)
  no operation moved by 1% of the time
where the time goes in v5:
time: 246 us; the launch traced here: 245 us
  blocking collectives  158 us (64%)
  waiting for transfers between devices  30.5 us (12%)
  starting transfers between devices  20.6 us (8%)
  Pallas kernels  19.3 us (8%)
  matrix products  7.6 us (3%)
  other arithmetic  4.99 us (2%)
  local copies, waits for them, and re-layouts  3.35 us (1%)
    all_to_all x1, blocking collectives, on_device(): arrived = send(rows)  79.2 us
    all_to_all x1, blocking collectives, on_device(): back = send(results)  78.4 us
    ppermute x6, waiting for transfers between devices, swap_chips(): return lax.ppermute(v, 'zh', [(i, i ^ r) for i in range(4)])  27.3 us
    ppermute x6, starting transfers between devices, swap_chips(): return lax.ppermute(v, 'zh', [(i, i ^ r) for i in range(4)])  12.1 us
    pallas_call x2, Pallas kernels, run(): pl.pallas_call(kernel, grid_spec=pltpu.PrefetchScalarGridSpec(num_scalar_...  10.6 us
    pallas_call x1, Pallas kernels, on_device(): pl.pallas_call(expert_kernel, grid=(1,), in_specs=[source_block(0), sourc...  8.69 us
    ppermute x10, starting transfers between devices, swap_cores(): return lax.ppermute(v, 'core', CORES)  8.47 us
  transfers between devices with their start and end apart: 16, of which 7 were waited for; matrix products, arithmetic and copies ran while one was open for 5% of the time, Pallas kernels for 2%

profile of v5, /device:TPU:65, one launch (start us, length us, event | category | flops | bytes accessed | tf_op | source)
XLA Modules:
  0.0 244.8 jit_solution(5088883464786721280)
XLA Ops:
  0.6 0.8 collective-permute-start.7
  1.4 0.1 collective-permute-start.8
  1.5 1.0 pad_maximum_fusion.3.refs_0_
  2.5 1.2 collective-permute-start
  3.7 5.2 %collective-permute-start.1 = (bf16[2,128,384]{2,1,0:T(8,128)(2,1)S(1)}, bf16[2,128,384]{2,1,0:T(8,128)(2,1)S(1)}, u32[]{:S(2)}, u32[]{:S(2)}) collective-permute-start(bf16[2,128,384]{2,1,0:T(8,128)(2,1)S(1)} %pad_maximum_fusion.3.refs_0_), channel_id=1, source_target_pairs={{0,4},{2,6},{4,0},{6,2},{1,5},{3,7},{5,1},{7,3},{8,12},{10,14},{12... | collective-permute-start | bytes 589832 | tf_op jit(solution)/shard_map/ppermute | solution.py:32
  8.8 0.0 collective-permute-start.2
  8.8 0.7 fusion.31
  9.5 0.2 fusion.32
  9.7 0.7 select_reduce_fusion
  10.5 0.1 copy.48
  10.6 0.1 copy.49
  10.7 0.7 multiply_add_fusion
  11.4 0.1 copy.50
  11.5 8.2 %collective-permute-done.refs_1_ = bf16[2,128,384]{2,1,0:T(8,128)(2,1)S(1)} collective-permute-done((bf16[2,128,384]{2,1,0:T(8,128)(2,1)S(1)}, bf16[2,128,384]{2,1,0:T(8,128)(2,1)S(1)}, u32[]{:S(2)}, u32[]{:S(2)}) %collective-permute-start) | collective-permute-done | bytes 196640 | tf_op jit(solution)/shard_map/ppermute | solution.py:32
  19.7 0.7 collective-permute-start.3
  20.5 0.1 copy.51.qt_ref
  20.5 0.8 copy.52
  21.3 0.0 collective-permute-done.1.refs_2_
  21.4 1.6 collective-permute-start.4
  22.9 2.6 %collective-permute-done.2.refs_3_ = bf16[2,128,384]{2,1,0:T(8,128)(2,1)S(1)} collective-permute-done((bf16[2,128,384]{2,1,0:T(8,128)(2,1)S(1)}, bf16[2,128,384]{2,1,0:T(8,128)(2,1)S(1)}, u32[]{:S(2)}, u32[]{:S(2)}) %collective-permute-start.2) | collective-permute-done | bytes 196640 | tf_op jit(solution)/shard_map/ppermute | solution.py:32
  25.5 2.6 %collective-permute-start.5 = (bf16[2,128,384]{2,1,0:T(8,128)(2,1)S(1)}, bf16[2,128,384]{2,1,0:T(8,128)(2,1)S(1)}, u32[]{:S(2)}, u32[]{:S(2)}) collective-permute-start(bf16[2,128,384]{2,1,0:T(8,128)(2,1)S(1)} %collective-permute-done.1.refs_2_), channel_id=1, source_target_pairs={{0,1},{1,0},{2,3},{3,2},{4,5},{5,4},{6,7},{7,6},{8,9},{9,8},{10,11... | collective-permute-start | bytes 589832 | tf_op jit(solution)/shard_map/ppermute | solution.py:28
  28.1 0.0 collective-permute-done.3.refs_4_
  28.1 0.0 collective-permute-start.6
  28.1 0.1 pad_add_fusion.order
  28.2 0.0 collective-permute-done.4.refs_5_
  28.2 1.0 collective-permute-done.5.refs_6_
  29.1 0.4 collective-permute-done.6.refs_7_
  29.5 0.7 copy-done
  30.2 5.2 %shard_map.119 = (bf16[32,32,3072]{2,1,0:T(8,128)(2,1)S(1)}, bf16[128,3072]{1,0:T(8,128)(2,1)S(1)}, bf16[128,3072]{1,0:T(8,128)(2,1)S(1)}, f32[128,128]{1,0:T(8,128)S(1)}) custom-call(s32[5]{0:T(128)S(1)} %pad_add_fusion.order, s32[4,128]{1,0:T(4,128)S(1)} %copy.51.qt_ref, f32[4,128]{1,0:T(4,128)S(1)} %bitcast.30, ...), custom_call_target="tpu_custom_call" | custom-call | flops 805306368 | bytes 6291456 | tf_op jit(solution)/shard_map/pallas_call | solution.py:209
  35.4 0.0 collective-permute-done.7.wi_b
  35.4 0.0 collective-permute-done.8.wo_b
  35.4 0.0 copy-start.1
  35.4 0.0 copy-start.2
  35.4 79.2 %all_to_all.10.x_ref.g_ref = bf16[32,32,3072]{2,1,0:T(8,128)(2,1)S(1)} all-to-all(bf16[32,32,3072]{2,1,0:T(8,128)(2,1)S(1)} %get-tuple-element.33), channel_id=1, replica_groups=mesh['y'=4,'zl'=2,'x'=4,'zh'=4,'core'=2] {'y','zl','x'}, dimensions={0} | all-to-all | bytes 12582912 | tf_op jit(solution)/shard_map/all_to_all | solution.py:285
  114.6 8.7 %shard_map.120 = (bf16[32,32,3072]{2,1,0:T(8,128)(2,1)S(1)}, bf16[512,512]{1,0:T(8,128)(2,1)S(1)}, bf16[512,512]{1,0:T(8,128)(2,1)S(1)}) custom-call(bf16[32,32,3072]{2,1,0:T(8,128)(2,1)S(1)} %all_to_all.10.x_ref.g_ref, bf16[32,32,3072]{2,1,0:T(8,128)(2,1)S(1)} %all_to_all.10.x_ref.g_ref, bf16[3072,256]{1,0:T(8,128)(2,1)S(1)} %bitcast.32, ...), custom_call_target="tpu_custom_call" | custom-call | flops 6442450944 | bytes 18874368 | tf_op jit(solution)/shard_map/pallas_call | solution.py:300
  123.3 78.4 %all_to_all.11.out_rows.dx_rows = bf16[32,32,3072]{2,1,0:T(8,128)(2,1)S(1)} all-to-all(bf16[32,32,3072]{2,1,0:T(8,128)(2,1)S(1)} %get-tuple-element.36), channel_id=1, replica_groups=mesh['y'=4,'zl'=2,'x'=4,'zh'=4,'core'=2] {'y','zl','x'}, dimensions={0} | all-to-all | bytes 12582912 | tf_op jit(solution)/shard_map/all_to_all | solution.py:318
  201.7 5.5 %shard_map.121 = (bf16[4,128,768]{2,1,0:T(8,128)(2,1)S(1)}, bf16[4,128,768]{2,1,0:T(8,128)(2,1)S(1)}, bf16[128,128]{1,0:T(8,128)(2,1)S(1)}) custom-call(s32[5]{0:T(128)S(1)} %pad_add_fusion.order, s32[128,4]{1,0:T(8,128)S(1)} %fusion.34.q_ref, f32[128,128]{1,0:T(8,128)S(1)} %pad.8.g_ref, f32[128,128]{1,0:T(8,128)S(1)} %get-tuple-element.32.stats_ref, ...), custom_call_target="tpu_custom_call" | custom-call | flops 1610612736 | bytes 6291456 | tf_op jit(solution)/shard_map/pallas_call | solution.py:209
  207.2 1.8 collective-permute-start.9
  209.0 0.1 collective-permute-start.10
  209.1 1.9 collective-permute-done.10
  210.9 0.1 reduce-precision_convert_fusion.1
  211.1 0.1 fusion.37
  211.2 0.1 fusion.14
  211.3 0.1 pad_maximum_fusion
  211.4 0.6 fusion.40
  212.1 1.0 convolution_convert_fusion.1
  213.1 0.7 collective-permute-start.14
  213.8 1.0 convolution_convert_fusion
  214.8 0.2 collective-permute-start.15
  215.0 0.2 slice_reduce_fusion.1
  215.2 1.1 collective-permute-start.11
  216.3 3.8 %collective-permute-start.12 = (bf16[128,896]{1,0:T(8,128)(2,1)S(1)}, bf16[128,896]{1,0:T(8,128)(2,1)S(1)}, u32[]{:S(2)}, u32[]{:S(2)}) collective-permute-start(bf16[128,896]{1,0:T(8,128)(2,1)S(1)} %get-tuple-element.45), channel_id=1, source_target_pairs={{0,4},{2,6},{4,0},{6,2},{1,5},{3,7},{5,1},{7,3},{8,12},{10,14},{12... | collective-permute-start | bytes 688136 | tf_op jit(solution)/shard_map/ppermute | solution.py:32
  220.1 0.8 collective-permute-start.13
  220.9 2.7 %convert_add_fusion.1 = f32[3072,256]{1,0:T(8,128)} fusion(bf16[3072,256]{1,0:T(8,128)(2,1)S(1)} %collective-permute-done.14, bf16[512,3072]{1,0:T(8,128)(2,1)S(1)} %bitcast.38, bf16[512,512]{1,0:T(8,128)(2,1)S(1)} %get-tuple-element.48), kind=kOutput, calls=%fused_computation.3 | convolution fusion | flops 806879232 | bytes 8126464 | tf_op jit(solution)/shard_map/dot_general | solution.py:349
  223.6 0.0 collective-permute-done.15
  223.6 2.7 %convert_add_fusion = f32[256,3072]{1,0:T(8,128)} fusion(bf16[256,3072]{1,0:T(8,128)(2,1)S(1)} %collective-permute-done.15, bf16[512,3072]{1,0:T(8,128)(2,1)S(1)} %bitcast.36, bf16[512,512]{1,0:T(8,128)(2,1)S(1)} %get-tuple-element.49), kind=kOutput, calls=%fused_computation.2 | convolution fusion | flops 806879232 | bytes 8126464 | tf_op jit(solution)/shard_map/dot_general | solution.py:344
  226.3 9.4 %collective-permute-done.11 = bf16[128,896]{1,0:T(8,128)(2,1)S(1)} collective-permute-done((bf16[128,896]{1,0:T(8,128)(2,1)S(1)}, bf16[128,896]{1,0:T(8,128)(2,1)S(1)}, u32[]{:S(2)}, u32[]{:S(2)}) %collective-permute-start.11) | collective-permute-done | bytes 229408 | tf_op jit(solution)/shard_map/ppermute | solution.py:32
  235.7 0.0 collective-permute-done.12
  235.7 7.1 %collective-permute-done.13 = bf16[128,896]{1,0:T(8,128)(2,1)S(1)} collective-permute-done((bf16[128,896]{1,0:T(8,128)(2,1)S(1)}, bf16[128,896]{1,0:T(8,128)(2,1)S(1)}, u32[]{:S(2)}, u32[]{:S(2)}) %collective-permute-start.13) | collective-permute-done | bytes 229408 | tf_op jit(solution)/shard_map/ppermute | solution.py:32
  242.8 0.2 fusion.25
  243.0 0.2 fusion.23
  243.2 0.7 copy.53
  243.9 0.1 fusion.1
  244.0 0.8 fusion.18
  (21 shorter events, 0.2 us)
Async XLA Ops:
  0.6 34.7 %collective-permute-start.7 = (bf16[3072,256]{1,0:T(8,128)(2,1)}, bf16[3072,256]{1,0:T(8,128)(2,1)S(1)}, u32[]{:S(2)}, u32[]{:S(2)}) collective-permute-start(bf16[3072,256]{1,0:T(8,128)(2,1)} %bitcast.31), channel_id=1, source_target_pairs={{0,1},{1,0},{2,3},{3,2},{4,5},{5,4},{6,7},{7,6},{8,9},{9,8},{10,11... | collective-permute-start | bytes 4718600 | tf_op jit(solution)/shard_map/ppermute | solution.py:28
  1.4 34.0 %collective-permute-start.8 = (bf16[256,3072]{1,0:T(8,128)(2,1)}, bf16[256,3072]{1,0:T(8,128)(2,1)}, u32[]{:S(2)}, u32[]{:S(2)}) collective-permute-start(bf16[256,3072]{1,0:T(8,128)(2,1)} %bitcast.33), channel_id=1, source_target_pairs={{0,1},{1,0},{2,3},{3,2},{4,5},{5,4},{6,7},{7,6},{8,9},{9,8},{10,11... | collective-permute-start | bytes 4718600 | tf_op jit(solution)/shard_map/ppermute | solution.py:28
  2.5 17.2 %collective-permute-start = (bf16[2,128,384]{2,1,0:T(8,128)(2,1)S(1)}, bf16[2,128,384]{2,1,0:T(8,128)(2,1)S(1)}, u32[]{:S(2)}, u32[]{:S(2)}) collective-permute-start(bf16[2,128,384]{2,1,0:T(8,128)(2,1)S(1)} %pad_maximum_fusion.3.refs_0_), channel_id=1, source_target_pairs={{0,2},{2,0},{4,6},{6,4},{1,3},{3,1},{5,7},{7,5},{8,10},{10,8},{12,... | collective-permute-start | bytes 589832 | tf_op jit(solution)/shard_map/ppermute | solution.py:32
  3.7 17.7 %collective-permute-start.1 = (bf16[2,128,384]{2,1,0:T(8,128)(2,1)S(1)}, bf16[2,128,384]{2,1,0:T(8,128)(2,1)S(1)}, u32[]{:S(2)}, u32[]{:S(2)}) collective-permute-start(bf16[2,128,384]{2,1,0:T(8,128)(2,1)S(1)} %pad_maximum_fusion.3.refs_0_), channel_id=1, source_target_pairs={{0,4},{2,6},{4,0},{6,2},{1,5},{3,7},{5,1},{7,3},{8,12},{10,14},{12... | collective-permute-start | bytes 589832 | tf_op jit(solution)/shard_map/ppermute | solution.py:32
  8.8 16.7 %collective-permute-start.2 = (bf16[2,128,384]{2,1,0:T(8,128)(2,1)S(1)}, bf16[2,128,384]{2,1,0:T(8,128)(2,1)S(1)}, u32[]{:S(2)}, u32[]{:S(2)}) collective-permute-start(bf16[2,128,384]{2,1,0:T(8,128)(2,1)S(1)} %pad_maximum_fusion.3.refs_0_), channel_id=1, source_target_pairs={{0,6},{2,4},{4,2},{6,0},{1,7},{3,5},{5,3},{7,1},{8,14},{10,12},{12... | collective-permute-start | bytes 589832 | tf_op jit(solution)/shard_map/ppermute | solution.py:32
  19.7 8.4 %collective-permute-start.3 = (bf16[2,128,384]{2,1,0:T(8,128)(2,1)S(1)}, bf16[2,128,384]{2,1,0:T(8,128)(2,1)S(1)}, u32[]{:S(2)}, u32[]{:S(2)}) collective-permute-start(bf16[2,128,384]{2,1,0:T(8,128)(2,1)S(1)} %pad_maximum_fusion.3.refs_0_), channel_id=1, source_target_pairs={{0,1},{1,0},{2,3},{3,2},{4,5},{5,4},{6,7},{7,6},{8,9},{9,8},{10,11... | collective-permute-start | bytes 589832 | tf_op jit(solution)/shard_map/ppermute | solution.py:28
  21.4 6.8 %collective-permute-start.4 = (bf16[2,128,384]{2,1,0:T(8,128)(2,1)S(1)}, bf16[2,128,384]{2,1,0:T(8,128)(2,1)S(1)}, u32[]{:S(2)}, u32[]{:S(2)}) collective-permute-start(bf16[2,128,384]{2,1,0:T(8,128)(2,1)S(1)} %collective-permute-done.refs_1_), channel_id=1, source_target_pairs={{0,1},{1,0},{2,3},{3,2},{4,5},{5,4},{6,7},{7,6},{8,9},{9,8},{10,11... | collective-permute-start | bytes 589832 | tf_op jit(solution)/shard_map/ppermute | solution.py:28
  25.5 3.6 %collective-permute-start.5 = (bf16[2,128,384]{2,1,0:T(8,128)(2,1)S(1)}, bf16[2,128,384]{2,1,0:T(8,128)(2,1)S(1)}, u32[]{:S(2)}, u32[]{:S(2)}) collective-permute-start(bf16[2,128,384]{2,1,0:T(8,128)(2,1)S(1)} %collective-permute-done.1.refs_2_), channel_id=1, source_target_pairs={{0,1},{1,0},{2,3},{3,2},{4,5},{5,4},{6,7},{7,6},{8,9},{9,8},{10,11... | collective-permute-start | bytes 589832 | tf_op jit(solution)/shard_map/ppermute | solution.py:28
  28.1 1.4 collective-permute-start.6
  29.5 0.7 copy-start
  35.4 79.2 %copy-start.1 = (bf16[1,3072,256]{2,1,0:T(8,128)(2,1)S(1)}, bf16[1,3072,256]{2,1,0:T(8,128)(2,1)}, u32[]{:S(2)}) copy-start(bf16[1,3072,256]{2,1,0:T(8,128)(2,1)} %param.14) | copy-start | bytes 4718596
  35.4 79.2 %copy-start.2 = (bf16[1,256,3072]{2,1,0:T(8,128)(2,1)S(1)}, bf16[1,256,3072]{2,1,0:T(8,128)(2,1)}, u32[]{:S(2)}) copy-start(bf16[1,256,3072]{2,1,0:T(8,128)(2,1)} %param.15) | copy-start | bytes 4718596
  207.2 4.0 %collective-permute-start.9 = (bf16[4,128,768]{2,1,0:T(8,128)(2,1)S(1)}, bf16[4,128,768]{2,1,0:T(8,128)(2,1)S(1)}, u32[]{:S(2)}, u32[]{:S(2)}) collective-permute-start(bf16[4,128,768]{2,1,0:T(8,128)(2,1)S(1)} %get-tuple-element.40), channel_id=1, source_target_pairs={{0,1},{1,0},{2,3},{3,2},{4,5},{5,4},{6,7},{7,6},{8,9},{9,8},{10,11... | collective-permute-start | bytes 2359304 | tf_op jit(solution)/shard_map/ppermute | solution.py:28
  209.0 2.0 collective-permute-start.10
  213.1 7.8 %collective-permute-start.14 = (bf16[3072,256]{1,0:T(8,128)(2,1)S(1)}, bf16[3072,256]{1,0:T(8,128)(2,1)S(1)}, u32[]{:S(2)}, u32[]{:S(2)}) collective-permute-start(bf16[3072,256]{1,0:T(8,128)(2,1)S(1)} %convolution_convert_fusion.1), channel_id=1, source_target_pairs={{0,1},{1,0},{2,3},{3,2},{4,5},{5,4},{6,7},{7,6},{8,9},{9,8},{10,11... | collective-permute-start | bytes 4718600 | tf_op jit(solution)/shard_map/ppermute | solution.py:28
  214.8 8.8 %collective-permute-start.15 = (bf16[256,3072]{1,0:T(8,128)(2,1)S(1)}, bf16[256,3072]{1,0:T(8,128)(2,1)S(1)}, u32[]{:S(2)}, u32[]{:S(2)}) collective-permute-start(bf16[256,3072]{1,0:T(8,128)(2,1)S(1)} %convolution_convert_fusion), channel_id=1, source_target_pairs={{0,1},{1,0},{2,3},{3,2},{4,5},{5,4},{6,7},{7,6},{8,9},{9,8},{10,11... | collective-permute-start | bytes 4718600 | tf_op jit(solution)/shard_map/ppermute | solution.py:28
  215.2 20.5 %collective-permute-start.11 = (bf16[128,896]{1,0:T(8,128)(2,1)S(1)}, bf16[128,896]{1,0:T(8,128)(2,1)S(1)}, u32[]{:S(2)}, u32[]{:S(2)}) collective-permute-start(bf16[128,896]{1,0:T(8,128)(2,1)S(1)} %get-tuple-element.44), channel_id=1, source_target_pairs={{0,2},{2,0},{4,6},{6,4},{1,3},{3,1},{5,7},{7,5},{8,10},{10,8},{12,... | collective-permute-start | bytes 688136 | tf_op jit(solution)/shard_map/ppermute | solution.py:32
  216.3 19.4 %collective-permute-start.12 = (bf16[128,896]{1,0:T(8,128)(2,1)S(1)}, bf16[128,896]{1,0:T(8,128)(2,1)S(1)}, u32[]{:S(2)}, u32[]{:S(2)}) collective-permute-start(bf16[128,896]{1,0:T(8,128)(2,1)S(1)} %get-tuple-element.45), channel_id=1, source_target_pairs={{0,4},{2,6},{4,0},{6,2},{1,5},{3,7},{5,1},{7,3},{8,12},{10,14},{12... | collective-permute-start | bytes 688136 | tf_op jit(solution)/shard_map/ppermute | solution.py:32
  220.1 22.7 %collective-permute-start.13 = (bf16[128,896]{1,0:T(8,128)(2,1)S(1)}, bf16[128,896]{1,0:T(8,128)(2,1)S(1)}, u32[]{:S(2)}, u32[]{:S(2)}) collective-permute-start(bf16[128,896]{1,0:T(8,128)(2,1)S(1)} %get-tuple-element.46), channel_id=1, source_target_pairs={{0,6},{2,4},{4,2},{6,0},{1,7},{3,5},{5,3},{7,1},{8,14},{10,12},{12... | collective-permute-start | bytes 688136 | tf_op jit(solution)/shard_map/ppermute | solution.py:32
  223.6 20.4 %copy-start.3 = (bf16[128,384]{1,0:T(8,128)(2,1)S(1)}, bf16[128,384]{1,0:T(8,128)(2,1)}, u32[]{:S(2)}) copy-start(bf16[128,384]{1,0:T(8,128)(2,1)} %param.8) | copy-start | bytes 294916
  223.6 20.4 %copy-start.4 = (bf16[128,384]{1,0:T(8,128)(2,1)S(1)}, bf16[128,384]{1,0:T(8,128)(2,1)}, u32[]{:S(2)}) copy-start(bf16[128,384]{1,0:T(8,128)(2,1)} %param.10) | copy-start | bytes 294916
  223.6 20.4 %copy-start.5 = (bf16[128,384]{1,0:T(8,128)(2,1)S(1)}, bf16[128,384]{1,0:T(8,128)(2,1)}, u32[]{:S(2)}) copy-start(bf16[128,384]{1,0:T(8,128)(2,1)} %param.9) | copy-start | bytes 294916
